TPU v7x, 32 devices: a whole 2x2x4 slice. The times are simulated.
32 devices in a mesh: dp: 8 (over z, x), tensor: 4 (over y, core).
Axes of the slice: x: 2, y: 2, z: 4, core: 2. Of those that a mesh axis runs over, the one named last changes fastest.
Arguments:
- tokens: bfloat16 [16384, 1024], P('dp', 'tensor'), may hold values from -6 to 6
- out_grad: bfloat16 [16384, 1024], P('dp', 'tensor'), may hold values from -6 to 6
- segments: int32 [8, 2048], P('dp'), may hold values from 0 to 3, never falling along the last dimension, each value on 1 to 1792 neighbouring positions
- padding: int32 [8, 2048], P('dp'), may hold values 0 or 1
- norm1_gain: bfloat16 [1024], P('tensor'), may hold values from 0.5 to 1.5
- norm1_bias: bfloat16 [1024], P('tensor'), may hold values from -3 to 3
- w_query: bfloat16 [1024, 1024], P(None, 'tensor'), may hold values from -1 to 1
- b_query: bfloat16 [1024], P('tensor'), may hold values from -4 to 4
- w_key: bfloat16 [1024, 1024], P(None, 'tensor'), may hold values from -0.1875 to 0.1875
- w_value: bfloat16 [1024, 1024], P(None, 'tensor'), may hold values from -0.1875 to 0.1875
- b_value: bfloat16 [1024], P('tensor'), may hold values from -4 to 4
- w_dense: bfloat16 [1024, 1024], P('tensor'), may hold values from -0.5 to 0.5
- dense_bias: bfloat16 [1024], P('tensor'), may hold values from -4 to 4
- norm2_gain: bfloat16 [1024], P('tensor'), may hold values from 0.5 to 1.5
- norm2_bias: bfloat16 [1024], P('tensor'), may hold values from -3 to 3
- w_up: bfloat16 [1024, 4096], P(None, 'tensor'), may hold values from -0.1875 to 0.1875
- b_up: bfloat16 [4096], P('tensor'), may hold values from -4 to 4
- w_down: bfloat16 [4096, 1024], P('tensor'), may hold values from -0.09375 to 0.09375
- down_bias: bfloat16 [1024], P('tensor'), may hold values from -4 to 4
Outputs:
- output: bfloat16 [16384, 1024], P('dp', 'tensor')
- tokens_grad: float32 [16384, 1024], P('dp', 'tensor')
- norm1_gain_grad: float32 [1024], P('tensor')
- norm1_bias_grad: float32 [1024], P('tensor')
- w_query_grad: float32 [1024, 1024], P('dp', 'tensor')
- b_query_grad: float32 [1024], P('tensor')
- w_key_grad: float32 [1024, 1024], P('dp', 'tensor')
- w_value_grad: float32 [1024, 1024], P('dp', 'tensor')
- b_value_grad: float32 [1024], P('tensor')
- w_dense_grad: float32 [1024, 1024], P('tensor', 'dp')
- dense_bias_grad: float32 [1024], P('tensor')
- norm2_gain_grad: float32 [1024], P('tensor')
- norm2_bias_grad: float32 [1024], P('tensor')
- w_up_grad: float32 [1024, 4096], P('dp', 'tensor')
- b_up_grad: float32 [4096], P('tensor')
- w_down_grad: float32 [4096, 1024], P('tensor', 'dp')
- down_bias_grad: float32 [1024], P('tensor')
- head_max: float32 [16], P('tensor')
- clipped_query: float32 [1024, 1024], P(None, 'tensor')
- clipped_query_bias: float32 [1024], P('tensor')
- clipped_key: float32 [1024, 1024], P(None, 'tensor')
Inputs may be any that keep to these rules, and one draw needn't show every extreme that they name: `segments`: document numbers never fall along a sequence and each of the 4 numbers occurs; a document spans 1 to 1792 tokens, and one spans exactly that many.
All inputs are finite; a program needn't handle non-finite values. No bound on the sum of `padding` on one device may be relied on, other than what follows from the above.
Results may differ from a plain program's by a relative error of at most 0.018.
Values may be sent and summed in bfloat16 or wider, within the bound.
A program may use at most 192 MiB of HBM per device.

v0:
```python
import math

import jax
import jax.numpy as jnp
from jax import lax
from jax.sharding import PartitionSpec as P

HEADS = 16
HD = 64
WIN = 1024
BLOCK = 512


EPS = 1e-05
TAU = 2.0
NEG = -1e30


def rows_inner(left_side, right_side):
    return lax.dot_general(
        left_side, right_side, (((0,), (0,)), ((), ())), preferred_element_type=jnp.float32
    )


def times_transposed(left_side, right_side):
    return lax.dot_general(
        left_side, right_side, (((1,), (1,)), ((), ())), preferred_element_type=jnp.float32
    )


def gelu_tanh(values):
    return jax.nn.gelu(values, approximate=True)


def shards(
    tokens,
    out_grad,
    segments,
    padding,
    norm1_gain,
    norm1_bias,
    w_query,
    b_query,
    w_key,
    w_value,
    b_value,
    w_dense,
    dense_bias,
    norm2_gain,
    norm2_bias,
    w_up,
    b_up,
    w_down,
    down_bias,
):
    tensor_rank = lax.axis_index("tensor")
    share_width = tokens.shape[1]
    row_width = share_width * lax.axis_size("tensor")
    tok_rows = tokens.shape[0]
    local_heads = share_width // HD
    seq_count, seq_len = segments.shape
    blocks = seq_len // BLOCK
    score_scale = 1.0 / math.sqrt(HD)
    vectors = jnp.stack([norm1_gain, norm1_bias, dense_bias, norm2_gain, norm2_bias, down_bias])
    x_rows, dy_rows, vec_rows = (
        lax.all_gather(tokens, "tensor", axis=1, tiled=True),
        lax.all_gather(out_grad, "tensor", axis=1, tiled=True),
        lax.all_gather(vectors, "tensor", axis=1, tiled=True),
    )

    def reduce_part(partial_term):
        return lax.psum(partial_term.astype(jnp.bfloat16), "tensor").astype(jnp.float32)

    def row_totals(first_sum, second):
        return (first_sum, second)

    def own_share(whole_rows):
        return lax.dynamic_slice_in_dim(
            whole_rows, tensor_rank * share_width, share_width, whole_rows.ndim - 1
        )

    def forward_norm(input_rows, gain_row, bias_row):
        total_sum, square_sum = row_totals(
            jnp.sum(input_rows, axis=1, keepdims=True),
            jnp.sum(input_rows * input_rows, axis=1, keepdims=True),
        )
        mean_row = total_sum / row_width
        rstd_row = lax.rsqrt(square_sum / row_width - mean_row * mean_row + EPS)
        normed = (input_rows - mean_row) * rstd_row
        return (normed * gain_row + bias_row, normed, rstd_row)

    def norm_backward(grad_norm, normed, rstd_row, gain_row):
        scaled = grad_norm * gain_row
        first_sum, second = row_totals(
            jnp.sum(scaled, axis=1, keepdims=True), jnp.sum(scaled * normed, axis=1, keepdims=True)
        )
        grad_inputs = rstd_row * (scaled - first_sum / row_width - normed * second / row_width)
        return (grad_inputs, jnp.sum(grad_norm * normed, axis=0), jnp.sum(grad_norm, axis=0))

    vector_single_float = vec_rows.astype(jnp.float32)
    input_rows = x_rows.astype(jnp.float32)
    first_norm_output, first_centered_scaled, first_inverse_deviation = forward_norm(
        input_rows, vector_single_float[0], vector_single_float[1]
    )
    act_first = first_norm_output.astype(jnp.bfloat16)
    queries = (
        jnp.dot(act_first, w_query, preferred_element_type=jnp.float32)
        + b_query.astype(jnp.float32)
    ).astype(jnp.bfloat16)
    keys_all = jnp.dot(act_first, w_key, preferred_element_type=jnp.float32).astype(jnp.bfloat16)
    values_all = (
        jnp.dot(act_first, w_value, preferred_element_type=jnp.float32)
        + b_value.astype(jnp.float32)
    ).astype(jnp.bfloat16)
    head_ids = tensor_rank * local_heads + jnp.arange(local_heads)
    slopes = jnp.exp2(-8.0 * (head_ids.astype(jnp.float32) + 1.0) / HEADS)
    query_four = queries.reshape(seq_count, seq_len, local_heads, HD)
    front = ((0, 0), (WIN, 0), (0, 0), (0, 0))
    key_pad = jnp.pad(keys_all.reshape(seq_count, seq_len, local_heads, HD), front)
    value_pad = jnp.pad(values_all.reshape(seq_count, seq_len, local_heads, HD), front)
    seg_pad = jnp.pad(segments, ((0, 0), (WIN, 0)), constant_values=-1)
    pad_keys = jnp.pad(padding, ((0, 0), (WIN, 0)))
    offsets = jnp.arange(BLOCK)[:, None] + WIN - jnp.arange(BLOCK + WIN)[None, :]
    near_mask = (offsets >= 0) & (offsets < WIN)
    distance = offsets.astype(jnp.float32)

    def block_inputs(block_index):
        seq_id = block_index // blocks
        row_start = block_index % blocks * BLOCK
        q_block = lax.dynamic_slice(
            query_four, (seq_id, row_start, 0, 0), (1, BLOCK, local_heads, HD)
        )[0]
        k_block = lax.dynamic_slice(
            key_pad, (seq_id, row_start, 0, 0), (1, BLOCK + WIN, local_heads, HD)
        )[0]
        v_block = lax.dynamic_slice(
            value_pad, (seq_id, row_start, 0, 0), (1, BLOCK + WIN, local_heads, HD)
        )[0]
        seg_q = lax.dynamic_slice(segments, (seq_id, row_start), (1, BLOCK))[0]
        seg_k = lax.dynamic_slice(seg_pad, (seq_id, row_start), (1, BLOCK + WIN))[0]
        pad_k = lax.dynamic_slice(pad_keys, (seq_id, row_start), (1, BLOCK + WIN))[0]
        allowed = (
            near_mask
            & (seg_q[:, None] == seg_k[None, :])
            & ((pad_k[None, :] == 1) | (offsets == 0))
        )
        raw_scores = (
            jnp.einsum("qhd,khd->hqk", q_block, k_block, preferred_element_type=jnp.float32)
            * score_scale
        )
        masked = jnp.where(allowed[None], raw_scores - slopes[:, None, None] * distance[None], NEG)
        return (seq_id, row_start, q_block, k_block, v_block, allowed, raw_scores, masked)

    def forward_block(block_index):
        seq_id, row_start, q_block, k_block, v_block, allowed, raw_scores, masked = block_inputs(
            block_index
        )
        top_score = jnp.max(masked, axis=2, keepdims=True)
        weights = jnp.where(allowed[None], jnp.exp(masked - top_score), 0.0)
        row_total = jnp.sum(weights, axis=2, keepdims=True)
        probabilities = (weights / row_total).astype(jnp.bfloat16)
        block_context = jnp.einsum(
            "hqk,khd->qhd", probabilities, v_block, preferred_element_type=jnp.float32
        )
        biggest = jnp.max(jnp.where(allowed[None], raw_scores, NEG), axis=(1, 2))
        return (
            block_context.astype(jnp.bfloat16).reshape(BLOCK, share_width),
            top_score + jnp.log(row_total),
            biggest,
        )

    contexts, log_totals, block_max = lax.map(forward_block, jnp.arange(seq_count * blocks))
    context = contexts.reshape(tok_rows, share_width)
    local_max = jnp.max(block_max, axis=0)
    head_max = lax.pmax(local_max, "dp")
    attn_sum = reduce_part(jnp.dot(context, w_dense, preferred_element_type=jnp.float32))
    hidden_single = input_rows + attn_sum + vector_single_float[2]
    second_norm_output, second_centered_scaled, second_inverse_deviation = forward_norm(
        hidden_single, vector_single_float[3], vector_single_float[4]
    )
    act_second = second_norm_output.astype(jnp.bfloat16)
    pre_act = jnp.dot(act_second, w_up, preferred_element_type=jnp.float32) + b_up.astype(
        jnp.float32
    )
    gelu_out, gelu_back = jax.vjp(gelu_tanh, pre_act)
    hidden_act = gelu_out.astype(jnp.bfloat16)
    mlp_sum = reduce_part(jnp.dot(hidden_act, w_down, preferred_element_type=jnp.float32))
    output = own_share(hidden_single + mlp_sum + vector_single_float[5]).astype(jnp.bfloat16)
    grad_output = dy_rows.astype(jnp.float32)
    grad_down_bias = jnp.sum(grad_output, axis=0)
    grad_w_down = rows_inner(hidden_act, dy_rows)
    grad_pre = gelu_back(times_transposed(dy_rows, w_down))[0].astype(jnp.bfloat16)
    grad_b_up = jnp.sum(grad_pre.astype(jnp.float32), axis=0)
    grad_w_up = rows_inner(act_second, grad_pre)
    second_norm_gradient = reduce_part(times_transposed(grad_pre, w_up))
    grad_through, grad_gain_second, grad_bias_second = norm_backward(
        second_norm_gradient,
        second_centered_scaled,
        second_inverse_deviation,
        vector_single_float[3],
    )
    grad_hidden = grad_output + grad_through
    grad_dense_bias = jnp.sum(grad_hidden, axis=0)
    hidden_low = grad_hidden.astype(jnp.bfloat16)
    grad_w_dense = rows_inner(context, hidden_low)
    grad_context = (
        times_transposed(hidden_low, w_dense)
        .astype(jnp.bfloat16)
        .reshape(seq_count, seq_len, local_heads, HD)
    )

    def backward_block(carried, block_index):
        key_acc, value_acc = carried
        seq_id, row_start, q_block, k_block, v_block, allowed, raw_scores, masked = block_inputs(
            block_index
        )
        probabilities = jnp.where(allowed[None], jnp.exp(masked - log_totals[block_index]), 0.0)
        grad_ctx = lax.dynamic_slice(
            grad_context, (seq_id, row_start, 0, 0), (1, BLOCK, local_heads, HD)
        )[0]
        grad_probs = jnp.einsum(
            "qhd,khd->hqk", grad_ctx, v_block, preferred_element_type=jnp.float32
        )
        delta_row = jnp.sum(probabilities * grad_probs, axis=2, keepdims=True)
        grad_scores = (probabilities * (grad_probs - delta_row)).astype(jnp.bfloat16)
        grad_q = (
            jnp.einsum("hqk,khd->qhd", grad_scores, k_block, preferred_element_type=jnp.float32)
            * score_scale
        )
        grad_k = (
            jnp.einsum("hqk,qhd->khd", grad_scores, q_block, preferred_element_type=jnp.float32)
            * score_scale
        )
        grad_v = jnp.einsum(
            "hqk,qhd->khd",
            probabilities.astype(jnp.bfloat16),
            grad_ctx,
            preferred_element_type=jnp.float32,
        )
        corner = (seq_id, row_start, 0, 0)
        extent = (1, BLOCK + WIN, local_heads, HD)
        key_acc = lax.dynamic_update_slice(
            key_acc, lax.dynamic_slice(key_acc, corner, extent) + grad_k[None], corner
        )
        value_acc = lax.dynamic_update_slice(
            value_acc, lax.dynamic_slice(value_acc, corner, extent) + grad_v[None], corner
        )
        return ((key_acc, value_acc), grad_q)

    zero_pad = jnp.zeros((seq_count, seq_len + WIN, local_heads, HD), jnp.float32)
    (key_acc, value_acc), grad_q_blocks = lax.scan(
        backward_block, (zero_pad, zero_pad), jnp.arange(seq_count * blocks)
    )
    grad_query = grad_q_blocks.reshape(tok_rows, share_width).astype(jnp.bfloat16)
    grad_key = key_acc[:, WIN:].reshape(tok_rows, share_width).astype(jnp.bfloat16)
    grad_value = value_acc[:, WIN:].reshape(tok_rows, share_width).astype(jnp.bfloat16)
    grad_b_query = jnp.sum(grad_query.astype(jnp.float32), axis=0)
    grad_b_value = jnp.sum(grad_value.astype(jnp.float32), axis=0)
    grad_w_query = rows_inner(act_first, grad_query)
    grad_w_key = rows_inner(act_first, grad_key)
    grad_w_value = rows_inner(act_first, grad_value)
    first_norm_gradient = reduce_part(
        times_transposed(grad_query, w_query)
        + times_transposed(grad_key, w_key)
        + times_transposed(grad_value, w_value)
    )
    grad_into, grad_gain_first, grad_bias_first = norm_backward(
        first_norm_gradient, first_centered_scaled, first_inverse_deviation, vector_single_float[0]
    )
    tokens_grad = own_share(grad_hidden + grad_into)
    matrix_sums = (
        lax.psum_scatter(grad_w_query, "dp", scatter_dimension=0, tiled=True),
        lax.psum_scatter(grad_w_key, "dp", scatter_dimension=0, tiled=True),
        lax.psum_scatter(grad_w_value, "dp", scatter_dimension=0, tiled=True),
        lax.psum_scatter(grad_w_dense, "dp", scatter_dimension=1, tiled=True),
        lax.psum_scatter(grad_w_up, "dp", scatter_dimension=0, tiled=True),
        lax.psum_scatter(grad_w_down, "dp", scatter_dimension=1, tiled=True),
    )
    vector_sums = lax.psum(
        (
            own_share(grad_gain_first),
            own_share(grad_bias_first),
            grad_b_query,
            grad_b_value,
            own_share(grad_dense_bias),
            own_share(grad_gain_second),
            own_share(grad_bias_second),
            grad_b_up,
            own_share(grad_down_bias),
        ),
        "dp",
    )
    column_scale = jnp.repeat(jnp.sqrt(TAU / jnp.maximum(head_max, TAU)), HD)
    clipped_query = w_query.astype(jnp.float32) * column_scale
    clipped_query_bias = b_query.astype(jnp.float32) * column_scale
    clipped_key = w_key.astype(jnp.float32) * column_scale
    return (
        output,
        tokens_grad,
        vector_sums[0],
        vector_sums[1],
        matrix_sums[0],
        vector_sums[2],
        matrix_sums[1],
        matrix_sums[2],
        vector_sums[3],
        matrix_sums[3],
        vector_sums[4],
        vector_sums[5],
        vector_sums[6],
        matrix_sums[4],
        vector_sums[7],
        matrix_sums[5],
        vector_sums[8],
        head_max,
        clipped_query,
        clipped_query_bias,
        clipped_key,
    )


def solution(mesh):
    in_specs = (
        P("dp", "tensor"),
        P("dp", "tensor"),
        P("dp", None),
        P("dp", None),
        P("tensor"),
        P("tensor"),
        P(None, "tensor"),
        P("tensor"),
        P(None, "tensor"),
        P(None, "tensor"),
        P("tensor"),
        P("tensor", None),
        P("tensor"),
        P("tensor"),
        P("tensor"),
        P(None, "tensor"),
        P("tensor"),
        P("tensor", None),
        P("tensor"),
    )
    out_specs = (
        P("dp", "tensor"),
        P("dp", "tensor"),
        P("tensor"),
        P("tensor"),
        P("dp", "tensor"),
        P("tensor"),
        P("dp", "tensor"),
        P("dp", "tensor"),
        P("tensor"),
        P("tensor", "dp"),
        P("tensor"),
        P("tensor"),
        P("tensor"),
        P("dp", "tensor"),
        P("tensor"),
        P("tensor", "dp"),
        P("tensor"),
        P("tensor"),
        P(None, "tensor"),
        P("tensor"),
        P(None, "tensor"),
    )
    return jax.shard_map(shards, mesh=mesh, in_specs=in_specs, out_specs=out_specs, check_vma=False)
```

profile of v0, /device:TPU:0, one launch (start us, length us, event | category | flops | bytes accessed | tf_op | source)
XLA Modules:
  0.0 1191.8 jit_solution(4768493959316764649)
XLA Ops:
  21.6 25.8 %all-gather.3.cloned.1.call-done = bf16[2048,1024]{1,0:T(8,128)(2,1)} async-done(((bf16[2048,256]{1,0:T(8,128)(2,1)}), bf16[2048,1024]{1,0:T(8,128)(2,1)}) %all-gather.3.cloned.1.call-update) | async-done | bytes 4194320 | tf_op jit(solution)/shard_map/all_gather | solution.py:66
  61.8 99.9 %while.36 = (s32[]{:T(128)}, bf16[4,512,256]{2,1,0:T(8,128)(2,1)S(1)}, f32[4,4,512,1]{2,1,3,0:T(4,128)S(1)}, f32[4,4]{1,0:T(4,128)}, s32[4]{0:T(128)S(1)}, /*ind...) while((s32[]{:T(128)}, ...), condition=%wide.region_6.7_spmd.clone.clone, body=%wide.region_2.6_spmd.clone.clone.sunk | while | flops 883293696 | bytes 63019040 | solution.py:172
  71.6 7.3 select_reduce_fusion.2
  96.5 7.3 select_reduce_fusion.2
  121.5 7.3 select_reduce_fusion.2
  146.4 7.3 select_reduce_fusion.2
  167.2 84.8 %all-reduce.10.cloned.1.call-done = bf16[2048,1024]{1,0:T(8,128)(2,1)} async-done(((bf16[2048,1024]{1,0:T(8,128)(2,1)}), bf16[2048,1024]{1,0:T(8,128)(2,1)}) %all-reduce.10.cloned.1.call-update) | async-done | bytes 4194320 | tf_op jit(solution)/shard_map/psum | solution.py:72
  264.4 6.6 fusion.119
  271.0 17.9 %all-gather.5.cloned.1.call-done = bf16[2048,1024]{1,0:T(8,128)(2,1)} async-done(((bf16[2048,256]{1,0:T(8,128)(2,1)}), bf16[2048,1024]{1,0:T(8,128)(2,1)}) %all-gather.5.cloned.1.call-update) | async-done | bytes 4194320 | tf_op jit(solution)/shard_map/all_gather | solution.py:67
  288.9 13.4 %convert_reduce_fusion.4 = (f32[1024]{0:T(1024)}, bf16[2048,1024]{1,0:T(8,128)(2,1)S(1)}) fusion(f32[2048,1024]{1,0:T(8,128)} %fusion.119, f32[1024]{0:T(1024)S(1)} %convert_element_type.159, bf16[2048,1024]{1,0:T(8,128)(2,1)} %all-gather.5.cloned.1.call-done, bf16[1024,1024]{1,0:T(8,128)(2,1)S(1)} %copy-done), kind=kOutput, calls=%fused_computation.124 | convolution fusion | flops 4343200768 | bytes 18882560 | tf_op jit(solution)/shard_map/dot_general | solution.py:26
  311.1 11.1 convolution_convert_fusion.2
  322.2 74.0 %all-reduce.12.cloned.1.call-done = bf16[2048,1024]{1,0:T(8,128)(2,1)} async-done(((bf16[2048,1024]{1,0:T(8,128)(2,1)}), bf16[2048,1024]{1,0:T(8,128)(2,1)}) %all-reduce.12.cloned.1.call-update) | async-done | bytes 4194320 | tf_op jit(solution)/shard_map/psum | solution.py:72
  396.2 7.1 fusion.97
  403.4 7.2 fusion.116
  417.8 149.9 %while.37 = (s32[]{:T(128)}, f32[1,3072,4,64]{1,3,2,0:T(8,128)}, f32[1,3072,4,64]{1,3,2,0:T(8,128)}, bf16[4,512,4,64]{1,3,2,0:T(8,128)(2,1)S(1)}, s32[4]{0:T(128...) while((s32[]{:T(128)}, f32[1,3072,4,64]{1,3,2,0:T(8,128)}, ...), condition=%wide.region_16.17_spmd.clone.clone, body=%wide.region_14.16_spmd.clone.clone.sunk | while | flops 2060975616 | bytes 169162880 | solution.py:251
  426.8 10.1 multiply_reduce_fusion.4
  436.9 6.3 multiply_convert_fusion.5
  464.2 10.1 multiply_reduce_fusion.4
  501.6 10.1 multiply_reduce_fusion.4
  538.9 10.1 multiply_reduce_fusion.4
  600.0 12.6 %fusion.113 = f32[1024,1024]{1,0:T(8,128)} fusion(bf16[2048,1024]{1,0:T(8,128)(2,1)} %all-gather.5.cloned.1.call-done, f32[2048,1024]{1,0:T(8,128)} %fusion.119, f32[1024]{0:T(1024)S(1)} %copy-done.41), kind=kOutput, calls=%fused_computation.169 | convolution fusion | flops 4315938816 | bytes 16781312 | tf_op jit(solution)/shard_map/dot_general | solution.py:20
  612.8 10.3 fusion.125
  623.9 21.7 %pmax.7 = f32[4]{0:T(128)S(1)} all-reduce(f32[4]{0:T(128)S(1)} %reduce_max.33), channel_id=1, replica_groups=mesh['dp'=8,'tensor'=4] {'dp'}, use_global_device_ids=true, to_apply=%region_45.46 | all-reduce | flops 4 | bytes 32 | tf_op jit(solution)/shard_map/pmax | solution.py:175
  651.2 81.3 %all-reduce.14.cloned.1.call-done = (bf16[2048,1024]{1,0:T(8,128)(2,1)}, bf16[2048,1024]{1,0:T(8,128)(2,1)}) async-done(((bf16[2048,1024]{1,0:T(8,128)(2,1)}, bf16[2048,1024]{1,0:T(8,128)(2,1)}), (bf16[2048,1024]{1,0:T(8,128)(2,1)}, bf16[2048,1024]{1,0:T(8,128)(2,1)})) %all-reduce.14.cloned.1.call-update) | async-done | bytes 8388624 | tf_op jit(solution)/shard_map/psum | solution.py:72
  732.5 10.4 fusion.98
  743.1 37.1 %all-reduce.4 = (f32[256]{0:T(256)}, f32[256]{0:T(256)}, f32[256]{0:T(256)}, f32[256]{0:T(256)}, f32[256]{0:T(256)}, /*index=5*/f32[256]{0:T(256)}, f32[256]{0:T(256)}, f32[1024]{0:T(1024)}, f32[256]{0:T(256)}) all-reduce(f32[256]{0:T(256)S(1)} %dynamic_slice.154, ...), channel_id=1, replica_groups=mesh['dp'=8,'tensor'=4] {'dp'}, use_global_device_ids=true, to_apply=%region_21.22 | all-reduce | flops 3072 | bytes 24576 | tf_op jit(solution)/shard_map/psum | solution.py:279
  787.6 12.8 %reduce-scatter.13.cloned.1.call-done = f32[256,128]{1,0:T(8,128)} async-done(((f32[256,1024]{1,0:T(8,128)}), f32[256,128]{1,0:T(8,128)}) %reduce-scatter.13.cloned.1.call-update) | async-done | bytes 131088 | tf_op jit(solution)/shard_map/reduce_scatter | solution.py:275
  800.3 66.9 %reduce-scatter.7.cloned.1.call-done = f32[128,256]{1,0:T(8,128)} async-done(((f32[1024,256]{1,0:T(8,128)}), f32[128,256]{1,0:T(8,128)}) %reduce-scatter.7.cloned.1.call-update) | async-done | bytes 131088 | tf_op jit(solution)/shard_map/reduce_scatter | solution.py:272
  867.3 66.5 %reduce-scatter.9.cloned.1.call-done = f32[128,256]{1,0:T(8,128)} async-done(((f32[1024,256]{1,0:T(8,128)}), f32[128,256]{1,0:T(8,128)}) %reduce-scatter.9.cloned.1.call-update) | async-done | bytes 131088 | tf_op jit(solution)/shard_map/reduce_scatter | solution.py:273
  933.8 66.9 %reduce-scatter.11.cloned.1.call-done = f32[128,256]{1,0:T(8,128)} async-done(((f32[1024,256]{1,0:T(8,128)}), f32[128,256]{1,0:T(8,128)}) %reduce-scatter.11.cloned.1.call-update) | async-done | bytes 131088 | tf_op jit(solution)/shard_map/reduce_scatter | solution.py:274
  1000.7 91.6 %reduce-scatter.17.cloned.1.call-done = f32[1024,128]{1,0:T(8,128)} async-done(((f32[1024,1024]{1,0:T(8,128)}), f32[1024,128]{1,0:T(8,128)}) %reduce-scatter.17.cloned.1.call-update) | async-done | bytes 524304 | tf_op jit(solution)/shard_map/reduce_scatter | solution.py:277
  1092.3 92.5 %reduce-scatter.15.cloned.1.call-done = f32[128,1024]{1,0:T(8,128)} async-done(((f32[1024,1024]{1,0:T(8,128)}), f32[128,1024]{1,0:T(8,128)}) %reduce-scatter.15.cloned.1.call-update) | async-done | bytes 524304 | tf_op jit(solution)/shard_map/reduce_scatter | solution.py:276
  (327 shorter events, 260.2 us)
Async XLA Ops:
  7.2 281.7 %copy-start = (bf16[1024,1024]{1,0:T(8,128)(2,1)S(1)}, bf16[1024,1024]{1,0:T(8,128)(2,1)}, u32[]{:S(2)}) copy-start(bf16[1024,1024]{1,0:T(8,128)(2,1)} %param.40) | copy-start | bytes 6291460
  7.2 40.1 %all-gather.3.cloned.1.call-start = ((), (), s32[]{:S(2)}) async-start(), calls=%async_computation.6 | async-start | bytes 5242880 | tf_op jit(solution)/shard_map/all_gather | solution.py:66
  7.9 244.1 %all-reduce.10.cloned.1.call-start = ((), (), s32[]{:S(2)}) async-start(), calls=%async_computation.7 | async-start | bytes 8388608 | tf_op jit(solution)/shard_map/psum | solution.py:72
  21.6 34.0 %copy-start.35 = (f32[1,1024]{1,0:T(1,128)}, f32[1,1024]{1,0:T(1,128)S(1)}, u32[]{:S(2)}) copy-start(f32[1,1024]{1,0:T(1,128)S(1)} %get-tuple-element.676) | copy-start | bytes 12292
  161.7 95.1 %copy-start.11 = (bf16[4,512,256]{2,1,0:T(8,128)(2,1)}, bf16[4,512,256]{2,1,0:T(8,128)(2,1)S(1)}, u32[]{:S(2)}) copy-start(bf16[4,512,256]{2,1,0:T(8,128)(2,1)S(1)} %get-tuple-element.421) | copy-start | bytes 3145732
  161.8 90.3 %copy-start.38 = (f32[1,1024]{1,0:T(1,128)S(1)}, f32[1,1024]{1,0:T(1,128)}, u32[]{:S(2)}) copy-start(f32[1,1024]{1,0:T(1,128)} %get-tuple-element.675) | copy-start | bytes 12292
  166.4 122.5 %all-gather.5.cloned.1.call-start = ((), (), s32[]{:S(2)}) async-start(), calls=%async_computation.8 | async-start | bytes 5242880 | tf_op jit(solution)/shard_map/all_gather | solution.py:67
  167.2 229.1 %all-reduce.12.cloned.1.call-start = ((), (), s32[]{:S(2)}) async-start(), calls=%async_computation.9 | async-start | bytes 8388608 | tf_op jit(solution)/shard_map/psum | solution.py:72
  167.2 143.9 %copy-start.40 = (f32[1024]{0:T(1024)}, f32[1024]{0:T(1024)S(1)}, u32[]{:S(2)}) copy-start(f32[1024]{0:T(1024)S(1)} %convert_element_type.159) | copy-start | bytes 12292
  252.1 8.8 copy-start.34
  252.1 8.8 copy-start.37
  288.9 15.4 %copy-start.46 = (bf16[1024,1024]{1,0:T(8,128)(2,1)S(1)}, bf16[1024,1024]{1,0:T(8,128)(2,1)}, u32[]{:S(2)}) copy-start(bf16[1024,1024]{1,0:T(8,128)(2,1)} %param.38) | copy-start | bytes 6291460
  310.6 421.9 %all-reduce.14.cloned.1.call-start = ((), (), s32[]{:S(2)}) async-start(), calls=%async_computation.16 | async-start | bytes 16777216 | tf_op jit(solution)/shard_map/psum | solution.py:72
  579.0 221.4 %reduce-scatter.13.cloned.1.call-start = ((), (), s32[]{:S(2)}) async-start(), calls=%async_computation.13 | async-start | bytes 1179648 | tf_op jit(solution)/shard_map/reduce_scatter | solution.py:275
  585.8 9.3 copy-start.15
  585.8 281.4 %reduce-scatter.7.cloned.1.call-start = ((), (), s32[]{:S(2)}) async-start(), calls=%async_computation.10 | async-start | bytes 1179648 | tf_op jit(solution)/shard_map/reduce_scatter | solution.py:272
  590.5 9.5 copy-start.41
  590.5 343.3 %reduce-scatter.9.cloned.1.call-start = ((), (), s32[]{:S(2)}) async-start(), calls=%async_computation.11 | async-start | bytes 1179648 | tf_op jit(solution)/shard_map/reduce_scatter | solution.py:273
  595.1 405.6 %reduce-scatter.11.cloned.1.call-start = ((), (), s32[]{:S(2)}) async-start(), calls=%async_computation.12 | async-start | bytes 1179648 | tf_op jit(solution)/shard_map/reduce_scatter | solution.py:274
  599.7 492.6 %reduce-scatter.17.cloned.1.call-start = ((), (), s32[]{:S(2)}) async-start(), calls=%async_computation.15 | async-start | bytes 4718592 | tf_op jit(solution)/shard_map/reduce_scatter | solution.py:277
  612.6 10.5 copy-start.43
  612.7 33.1 %copy-start.44 = (bf16[256]{0:T(256)(128)(2,1)S(1)}, bf16[256]{0:T(256)(128)(2,1)}, u32[]{:S(2)}) copy-start(bf16[256]{0:T(256)(128)(2,1)} %param.30) | copy-start | bytes 1540
  612.7 33.7 %copy-start.23 = (bf16[1024,256]{1,0:T(8,128)(2,1)S(1)}, bf16[1024,256]{1,0:T(8,128)(2,1)}, u32[]{:S(2)}) copy-start(bf16[1024,256]{1,0:T(8,128)(2,1)} %param.29) | copy-start | bytes 1572868
  612.7 33.6 %copy-start.26 = (bf16[1024,256]{1,0:T(8,128)(2,1)S(1)}, bf16[1024,256]{1,0:T(8,128)(2,1)}, u32[]{:S(2)}) copy-start(bf16[1024,256]{1,0:T(8,128)(2,1)} %param.31) | copy-start | bytes 1572868
  612.7 38.1 %copy-start.19 = (bf16[4,512,4,64]{1,3,2,0:T(8,128)(2,1)S(1)}, bf16[4,512,4,64]{1,3,2,0:T(8,128)(2,1)}, u32[]{:S(2)}) copy-start(bf16[4,512,4,64]{1,3,2,0:T(8,128)(2,1)} %copy-done.18) | copy-start | bytes 3145732
  612.7 572.1 %reduce-scatter.15.cloned.1.call-start = ((), (), s32[]{:S(2)}) async-start(), calls=%async_computation.14 | async-start | bytes 4718592 | tf_op jit(solution)/shard_map/reduce_scatter | solution.py:276
  623.1 109.4 %copy-start.30 = (f32[2048]{0:T(1024)S(1)}, f32[2048]{0:T(1024)}, u32[]{:S(2)}) copy-start(f32[2048]{0:T(1024)} %copy-done.29) | copy-start | bytes 24580
  623.1 109.4 %copy-start.33 = (f32[2048]{0:T(1024)S(1)}, f32[2048]{0:T(1024)}, u32[]{:S(2)}) copy-start(f32[2048]{0:T(1024)} %copy-done.32) | copy-start | bytes 24580
  623.1 109.4 %copy-start.36 = (f32[1,1024]{1,0:T(1,128)S(1)}, f32[1,1024]{1,0:T(1,128)}, u32[]{:S(2)}) copy-start(f32[1,1024]{1,0:T(1,128)} %copy-done.35) | copy-start | bytes 12292
  645.6 97.3 %copy-start.47 = (f32[4]{0:T(128)}, f32[4]{0:T(128)S(1)}, u32[]{:S(2)}) copy-start(f32[4]{0:T(128)S(1)} %pmax.7) | copy-start | bytes 52
  732.5 10.6 copy-start.39
  732.5 452.3 %copy-start.1 = (bf16[1024,1024]{1,0:T(8,128)(2,1)S(1)}, bf16[1024,1024]{1,0:T(8,128)(2,1)}, u32[]{:S(2)}) copy-start(bf16[1024,1024]{1,0:T(8,128)(2,1)} %param.40) | copy-start | bytes 6291460
  (46 other events, 219.9 us)
Sparse Core Ops, SparseCore 0:
  9.6 37.7 all-gather.2
  166.5 85.4 all-reduce.9
  253.7 35.1 all-gather.4
  310.7 85.4 all-reduce.11
  579.1 153.3 all-reduce.13
  736.3 63.9 reduce-scatter.12
  804.7 62.5 reduce-scatter.6
  871.2 62.4 reduce-scatter.8
  938.1 62.5 reduce-scatter.10
  1004.8 87.4 reduce-scatter.16
  1096.9 87.8 reduce-scatter.14
where the time goes:
time: 1200 us; the launch traced here: 1190 us
  waiting for transfers between devices  682 us (57%)
  matrix products  234 us (20%)
  other arithmetic  120 us (10%)
  blocking collectives  65 us (5%)
  local copies, waits for them, and re-layouts  52.4 us (4%)
  loops' own time  22.3 us (2%)
  between operations  14.9 us (1%)
    psum x3, waiting for transfers between devices, reduce_part(): lax.psum(partial_term.astype(jnp.bfloat16), 'tensor').astype(jnp.float32)  240 us
    reduce_scatter x1, waiting for transfers between devices, shards(): lax.psum_scatter(grad_w_up, 'dp', scatter_dimension=0, tiled=True)  92.5 us
    reduce_scatter x1, waiting for transfers between devices, shards(): lax.psum_scatter(grad_w_down, 'dp', scatter_dimension=1, tiled=True)  91.6 us
    reduce_scatter x1, waiting for transfers between devices, shards(): lax.psum_scatter(grad_w_value, 'dp', scatter_dimension=0, tiled=True)  66.9 us
    reduce_scatter x1, waiting for transfers between devices, shards(): lax.psum_scatter(grad_w_query, 'dp', scatter_dimension=0, tiled=True)  66.9 us
    reduce_scatter x1, waiting for transfers between devices, shards(): lax.psum_scatter(grad_w_key, 'dp', scatter_dimension=0, tiled=True)  66.5 us
    dot_general x8, matrix products, block_inputs(): jnp.einsum('qhd,khd->hqk', q_block, k_block, preferred_element_type=jnp.f...  61 us
    dot_general x6, matrix products, rows_inner(): lax.dot_general(left_side, right_side, (((0,), (0,)), ((), ())), preferre...  42.2 us
  transfers between devices with their start and end apart: 11, of which 11 were waited for; matrix products, arithmetic and copies ran while one was open for 8% of the time, Pallas kernels for 0%

commit v1 on v0

v1 whole, which is shorter than its diff:
```python
import functools
import math

import jax
import jax.numpy as jnp
from jax import lax
from jax.experimental import pallas as pl
from jax.experimental.pallas import tpu as pltpu
from jax.sharding import PartitionSpec as P

HEADS = 16
HD = 64
WIN = 1024
D = 1024
FF = 4096
SEQ = 2048
B = 256
NB = SEQ // B
SLOTS = WIN // B + 1
STRIP = SLOTS * B
LH = 4
SHARE = LH * HD
UNITS = FF // 4
TILE = 512
OWN = SEQ // 2

EPS = 1e-05
TAU = 2.0
NEG = -1e30
F32 = jnp.float32
BF = jnp.bfloat16
VMEM_LIMIT = 56 * 2**20


def dot(a, b):
    return jnp.dot(a, b, preferred_element_type=F32)


def dot_nt(a, b):
    return lax.dot_general(a, b, (((1,), (1,)), ((), ())), preferred_element_type=F32)


def params():
    return pltpu.CompilerParams(
        dimension_semantics=("arbitrary",), vmem_limit_bytes=VMEM_LIMIT
    )


def feature_block(rank):
    return pl.ds(pl.multiple_of(rank * SHARE, SHARE), SHARE)


def head_of_lane(shape):
    return lax.broadcasted_iota(jnp.int32, shape, 1) // HD


def row_stats(rows):
    mean = jnp.sum(rows, axis=1, keepdims=True) / D
    square = jnp.sum(rows * rows, axis=1, keepdims=True) / D
    return mean, lax.rsqrt(square - mean * mean + EPS)


def split_store(keep_ref, send_ref, value_ref, core):
    for half in range(2):
        cols = slice(half * SHARE, (half + 1) * SHARE)
        keep_ref[:, cols] = value_ref[:, feature_block(2 * half + core)].astype(keep_ref.dtype)
        send_ref[:, cols] = value_ref[:, feature_block(2 * half + 1 - core)].astype(
            send_ref.dtype
        )


def fwd_kernel(
    ids, x0, x1, x2, x3, vec, wq, wk, wv, bqv, wd, lo, pad, alibi,
    p_ref, q_ref, k_ref, v_ref, linv_ref, ctx_ref, keep_ref, send_ref, hm_ref,
    xs, qm_s, k_s, va_s, u_s, res_s, lo_s,
):
    b = pl.program_id(0)
    t = ids[0]
    core = lax.rem(t, 2)
    for r, x in enumerate((x0, x1, x2, x3)):
        xs[:, feature_block(t ^ r)] = x[...].astype(F32)
    rows = xs[...]
    mean, rstd = row_stats(rows)
    n1 = ((rows - mean) * rstd * vec[0:1, :] + vec[1:2, :]).astype(BF)
    q = (dot(n1, wq[...]) + bqv[0:1, :]).astype(BF)
    k = dot(n1, wk[...]).astype(BF)
    v = (dot(n1, wv[...]) + bqv[1:2, :]).astype(BF)
    qs = q * jnp.asarray(1.0 / math.sqrt(HD), BF)
    q_ref[...] = qs
    k_ref[...] = k
    v_ref[...] = v
    here = pl.ds(pl.multiple_of(b * B, B), B)
    k_s[here, :] = k
    lanes = head_of_lane((B, SHARE))
    for h in range(LH):
        qm_s[h] = jnp.where(lanes == h, qs, jnp.zeros_like(qs))
        va_s[h, here, :] = jnp.where(lanes == h, v, jnp.ones_like(v))
    lo_s[...] = jnp.broadcast_to(lo[...], (B, B))

    @pl.when(b == 0)
    def _():
        hm_ref[...] = jnp.full(hm_ref.shape, NEG, F32)

    row_i = lax.broadcasted_iota(jnp.int32, (B, B), 0)
    col_i = lax.broadcasted_iota(jnp.int32, (B, B), 1)

    def attend(nb):
        start = pl.multiple_of((b + 1 - nb) * B, B)

        def head(h, carry):
            qm = qm_s[h]
            top = jnp.full((B, 128), NEG, F32)
            biggest = hm_ref[h]
            for r in range(nb):
                slot = SLOTS - nb + r
                base = pl.multiple_of(start + r * B, B)
                s = dot_nt(qm, k_s[pl.ds(base, B), :])
                inside = col_i + base >= lo_s[...]
                shut = pad[0:1, pl.ds(base, B)]
                if r == nb - 1:
                    s = jnp.where(row_i == col_i, s, s + shut)
                    s = jnp.where(inside & (col_i <= row_i), s, NEG)
                else:
                    s = jnp.where(inside, s + shut, NEG)
                biggest = jnp.maximum(biggest, jnp.max(s.reshape(B // 8, 8, B), axis=0))
                s = s + alibi[pl.ds(h, 1), slot * B : (slot + 1) * B]
                u_s[:, slot * B : (slot + 1) * B] = s
                top = jnp.maximum(top, jnp.maximum(s[:, :128], s[:, 128:]))
            hm_ref[h] = biggest
            top = jnp.max(top, axis=1, keepdims=True)
            for r in range(nb):
                slot = SLOTS - nb + r
                cols = slice(slot * B, (slot + 1) * B)
                p_ref[h, :, cols] = jnp.exp(u_s[:, cols] - top).astype(BF)
            res_s[h] = dot(p_ref[h, :, (SLOTS - nb) * B :], va_s[h, pl.ds(start, nb * B), :])
            return carry

        lax.fori_loop(0, LH, head, 0)

    count = b - ids[1 + b] + 1
    for nb in range(1, SLOTS + 1):
        pl.when(count == nb)(functools.partial(attend, nb))

    ctx = res_s[0]
    total = res_s[LH - 1]
    for h in range(1, LH):
        ctx = jnp.where(lanes == h, res_s[h], ctx)
        total = jnp.where(lanes == h, res_s[h - 1], total)
    inv = 1.0 / pltpu.roll(total, SHARE - HD, 1)
    linv_ref[...] = inv
    ctx = (ctx * inv).astype(BF)
    ctx_ref[...] = ctx
    xs[...] = dot(ctx, wd[...])
    split_store(keep_ref, send_ref, xs, core)


def attention_forward(ids, xs, vec, wq, wk, wv, bqv, wd, lo, pad, alibi):
    row = lambda width: pl.BlockSpec((B, width), lambda b, ids: (b, 0))
    whole = lambda shape: pl.BlockSpec(shape, lambda b, ids: (0,) * len(shape))
    return pl.pallas_call(
        fwd_kernel,
        grid_spec=pltpu.PrefetchScalarGridSpec(
            num_scalar_prefetch=1,
            grid=(NB,),
            in_specs=[row(SHARE)] * 4
            + [whole((8, D))]
            + [whole((D, SHARE))] * 3
            + [whole((8, SHARE)), whole((SHARE, D)), row(1), whole((8, SEQ)), whole((8, STRIP))],
            out_specs=[
                pl.BlockSpec((LH, B, STRIP), lambda b, ids: (0, b, 0)),
                row(SHARE), row(SHARE), row(SHARE), row(SHARE), row(SHARE), row(D // 2), row(D // 2),
                whole((LH, 8, B)),
            ],
            scratch_shapes=[
                pltpu.VMEM((B, D), F32),
                pltpu.VMEM((LH, B, SHARE), BF),
                pltpu.VMEM((SEQ, SHARE), BF),
                pltpu.VMEM((LH, SEQ, SHARE), BF),
                pltpu.VMEM((B, STRIP), F32),
                pltpu.VMEM((LH, B, SHARE), F32),
                pltpu.VMEM((B, B), jnp.int32),
            ],
        ),
        out_shape=[
            jax.ShapeDtypeStruct((LH, SEQ, STRIP), BF),
            jax.ShapeDtypeStruct((SEQ, SHARE), BF),
            jax.ShapeDtypeStruct((SEQ, SHARE), BF),
            jax.ShapeDtypeStruct((SEQ, SHARE), BF),
            jax.ShapeDtypeStruct((SEQ, SHARE), F32),
            jax.ShapeDtypeStruct((SEQ, SHARE), BF),
            jax.ShapeDtypeStruct((SEQ, D // 2), BF),
            jax.ShapeDtypeStruct((SEQ, D // 2), BF),
            jax.ShapeDtypeStruct((LH, 8, B), F32),
        ],
        compiler_params=params(),
        cost_estimate=pl.CostEstimate(
            flops=16 * 10**9, bytes_accessed=40 * 2**20, transcendentals=8 * 10**6
        ),
        name="attention_forward",
    )(ids, *xs, vec, wq, wk, wv, bqv, wd, lo, pad, alibi)


def mlp_kernel(
    ids, a_own, a_par, x0, x1, x2, x3, d0, d1, d2, d3, vec, bup, wu0, wu1, wd0, wd1,
    mk_ref, ms_ref, gn_ref, h1_ref, gu_ref, gd_ref, bs_ref,
    n2_s, n2t_s, dy_s, dyt_s, am_s, ag_s, act_s, gp_s,
):
    i = pl.program_id(0)
    t = ids[0]
    core = lax.rem(t, 2)

    @pl.when(i == 0)
    def _():
        def assemble(rb, carry):
            rows = pl.ds(pl.multiple_of(rb * B, B), B)
            for r, (x, d) in enumerate(((x0, d0), (x1, d1), (x2, d2), (x3, d3))):
                h1_ref[rows, feature_block(t ^ r)] = x[rb, 0].astype(F32)
                dy_s[rows, feature_block(t ^ r)] = d[rows, :]
            for part, a in ((core, a_own), (1 - core, a_par)):
                for half in range(2):
                    cols = feature_block(2 * half + part)
                    h1_ref[rows, cols] += a[rows, half * SHARE : (half + 1) * SHARE].astype(F32)
            value = h1_ref[rows, :] + vec[2:3, :]
            h1_ref[rows, :] = value
            mean, rstd = row_stats(value)
            n2 = ((value - mean) * rstd * vec[3:4, :] + vec[4:5, :]).astype(BF)
            n2_s[rows, :] = n2
            n2t_s[:, rows] = n2.T
            dyt_s[:, rows] = dy_s[rows, :].T
            am_s[rows, :] = jnp.zeros((B, D), F32)
            ag_s[rows, :] = jnp.zeros((B, D), F32)
            return carry

        lax.fori_loop(0, OWN // B, assemble, 0)

    def tile(wu, wd, which):
        bias = bup[which : which + 1, pl.ds(pl.multiple_of(lax.rem(i, 2) * TILE, TILE), TILE)]
        scale = math.sqrt(2.0 / math.pi)

        def rows_of(rb, sums):
            rows = pl.ds(pl.multiple_of(rb * B, B), B)
            pre = dot(n2_s[rows, :], wu[...]) + bias
            back = dot_nt(dy_s[rows, :], wd[...])
            square = pre * pre
            th = jnp.tanh(scale * pre * (1.0 + 0.044715 * square))
            half = 0.5 * (1.0 + th)
            act = (pre * half).astype(BF)
            slope = half + 0.5 * pre * (1.0 - th * th) * (scale + (3 * 0.044715 * scale) * square)
            gp = (slope * back).astype(BF)
            act_s[rows, :] = act
            gp_s[rows, :] = gp
            am_s[rows, :] += dot(act, wd[...])
            ag_s[rows, :] += dot_nt(gp, wu[...])
            return sums + jnp.sum(gp.astype(F32), axis=0, keepdims=True)

        sums = lax.fori_loop(0, OWN // B, rows_of, jnp.zeros((1, TILE), F32))
        bs_ref[...] = jnp.broadcast_to(sums, bs_ref.shape)

        def grads(fb, carry):
            rows = pl.ds(pl.multiple_of(fb * B, B), B)
            gu_ref[rows, :] = dot(n2t_s[rows, :], gp_s[...]).astype(gu_ref.dtype)
            gd_ref[rows, :] = dot(dyt_s[rows, :], act_s[...]).astype(gd_ref.dtype)
            return carry

        lax.fori_loop(0, D // B, grads, 0)

    pl.when(i < 2)(lambda: tile(wu0, wd0, 0))
    pl.when(i >= 2)(lambda: tile(wu1, wd1, 1))

    @pl.when(i == 3)
    def _():
        split_store(mk_ref, ms_ref, am_s, core)
        gn_ref[...] = ag_s[...].astype(BF)


def feed_forward(ids, a_own, a_par, xs, ds, vec, bup, wu0, wu1, wd0, wd1):
    whole = lambda shape: pl.BlockSpec(shape, lambda i, ids: (0,) * len(shape))
    low = lambda i: jnp.minimum(i, 1)
    high = lambda i: jnp.maximum(i - 2, 0)
    xs = [x.reshape(NB // 2, 2, B, SHARE) for x in xs]
    return pl.pallas_call(
        mlp_kernel,
        grid_spec=pltpu.PrefetchScalarGridSpec(
            num_scalar_prefetch=1,
            grid=(4,),
            in_specs=[whole((OWN, D // 2))] * 2
            + [pl.BlockSpec((NB // 2, 1, B, SHARE), lambda i, ids: (0, ids[0] // 2, 0, 0))] * 4
            + [whole((OWN, SHARE))] * 4
            + [
                whole((8, D)),
                whole((8, UNITS)),
                pl.BlockSpec((D, TILE), lambda i, ids: (0, low(i))),
                pl.BlockSpec((D, TILE), lambda i, ids: (0, high(i))),
                pl.BlockSpec((TILE, D), lambda i, ids: (low(i), 0)),
                pl.BlockSpec((TILE, D), lambda i, ids: (high(i), 0)),
            ],
            out_specs=[
                whole((OWN, D // 2)),
                whole((OWN, D // 2)),
                whole((OWN, D)),
                whole((OWN, D)),
                pl.BlockSpec((D, TILE), lambda i, ids: (0, i)),
                pl.BlockSpec((D, TILE), lambda i, ids: (0, i)),
                pl.BlockSpec((8, TILE), lambda i, ids: (0, i)),
            ],
            scratch_shapes=[
                pltpu.VMEM((OWN, D), BF),
                pltpu.VMEM((D, OWN), BF),
                pltpu.VMEM((OWN, D), BF),
                pltpu.VMEM((D, OWN), BF),
                pltpu.VMEM((OWN, D), F32),
                pltpu.VMEM((OWN, D), F32),
                pltpu.VMEM((OWN, TILE), BF),
                pltpu.VMEM((OWN, TILE), BF),
            ],
        ),
        out_shape=[
            jax.ShapeDtypeStruct((OWN, D // 2), BF),
            jax.ShapeDtypeStruct((OWN, D // 2), BF),
            jax.ShapeDtypeStruct((OWN, D), BF),
            jax.ShapeDtypeStruct((OWN, D), F32),
            jax.ShapeDtypeStruct((D, 2 * UNITS), BF),
            jax.ShapeDtypeStruct((D, 2 * UNITS), BF),
            jax.ShapeDtypeStruct((8, 2 * UNITS), F32),
        ],
        compiler_params=params(),
        cost_estimate=pl.CostEstimate(
            flops=26 * 10**9, bytes_accessed=40 * 2**20, transcendentals=2 * 10**6
        ),
        name="feed_forward",
    )(ids, a_own, a_par, *xs, *ds, vec, bup, wu0, wu1, wd0, wd1)


def mid_kernel(
    ids, h1, gn, gr, d0, d1, d2, d3, mk, mr, vec,
    gh_ref, gs_ref, oo_ref, os_ref, cs_ref,
    w_s,
):
    i = pl.program_id(0)
    t = ids[0]
    core = lax.rem(t, 2)
    y = t // 2
    for r, d in enumerate((d0, d1, d2, d3)):
        w_s[:, feature_block(t ^ r)] = d[...].astype(F32)
    dy = w_s[...]
    rows = h1[...]
    for half, ref in ((y, oo_ref), (1 - y, os_ref)):
        cols = feature_block(2 * half + core)
        part = pl.ds(pl.multiple_of(half * SHARE, SHARE), SHARE)
        total = mk[:, part].astype(F32) + mr[:, part].astype(F32)
        ref[...] = (h1[:, cols] + total + vec[5:6, cols]).astype(BF)
    mean, rstd = row_stats(rows)
    xhat = (rows - mean) * rstd
    grad = gn[...].astype(F32) + gr[...].astype(F32)
    scaled = grad * vec[3:4, :]
    first = jnp.sum(scaled, axis=1, keepdims=True) / D
    second = jnp.sum(scaled * xhat, axis=1, keepdims=True) / D
    gh = dy + rstd * (scaled - first - xhat * second)
    low = gh.astype(BF)
    gh_ref[...] = low
    w_s[...] = gh
    for half in range(2):
        gs_ref[:, half * SHARE : (half + 1) * SHARE] = w_s[:, feature_block(2 * half + core)].astype(BF)

    @pl.when(i == 0)
    def _():
        cs_ref[...] = jnp.zeros(cs_ref.shape, F32)

    for n, value in enumerate((grad * xhat, grad, gh, dy)):
        cs_ref[n : n + 1, :] += jnp.sum(value, axis=0, keepdims=True)


def middle(ids, h1, gn, gr, ds, mk, mr, vec):
    row = lambda width: pl.BlockSpec((B, width), lambda i, ids: (i, 0))
    whole = lambda shape: pl.BlockSpec(shape, lambda i, ids: (0,) * len(shape))
    return pl.pallas_call(
        mid_kernel,
        grid_spec=pltpu.PrefetchScalarGridSpec(
            num_scalar_prefetch=1,
            grid=(OWN // B,),
            in_specs=[row(D)] * 3 + [row(SHARE)] * 4 + [row(D // 2)] * 2 + [whole((8, D))],
            out_specs=[row(D), row(D // 2), row(SHARE), row(SHARE), whole((8, D))],
            scratch_shapes=[pltpu.VMEM((B, D), F32)],
        ),
        out_shape=[
            jax.ShapeDtypeStruct((OWN, D), BF),
            jax.ShapeDtypeStruct((OWN, D // 2), BF),
            jax.ShapeDtypeStruct((OWN, SHARE), BF),
            jax.ShapeDtypeStruct((OWN, SHARE), BF),
            jax.ShapeDtypeStruct((8, D), F32),
        ],
        compiler_params=params(),
        cost_estimate=pl.CostEstimate(flops=20 * 2**20, bytes_accessed=16 * 2**20, transcendentals=0),
        name="second_norm_backward",
    )(ids, h1, gn, gr, *ds, mk, mr, vec)


def bwd_kernel(
    ids, x0, x1, x2, x3, gh, ga, gb, p_ref, q_ref, linv_ref, ctx_ref, k_ref, v_ref, vec, wq, wk, wv, wd,
    keep_ref, send_ref, st_ref, ghx_ref, gw_ref, bs_ref,
    xs, gh_s, gm_s, gt_s, qt_s, dl_s, ds_s, res_s, dkt_s, dvt_s, acc_s,
):
    i = pl.program_id(0)
    b = NB - 1 - i
    t = ids[0]
    core = lax.rem(t, 2)
    y = t // 2

    @pl.when(i == 0)
    def _():
        dkt_s[...] = jnp.zeros(dkt_s.shape, F32)
        dvt_s[...] = jnp.zeros(dvt_s.shape, F32)
        acc_s[...] = jnp.zeros(acc_s.shape, F32)
        bs_ref[...] = jnp.zeros(bs_ref.shape, F32)

    @pl.when(lax.rem(b, 2) == y)
    def _():
        gh_s[...] = gh[...]

    @pl.when(lax.rem(b, 2) != y)
    def _():
        for part, ref in ((core, ga), (1 - core, gb)):
            for half in range(2):
                gh_s[:, feature_block(2 * half + part)] = ref[:, half * SHARE : (half + 1) * SHARE]

    ghl = gh_s[...]
    ghx_ref[...] = gh_s[:, feature_block(t)]
    gc = dot_nt(ghl, wd[...]).astype(BF).astype(F32)
    ctx = ctx_ref[...]
    scaled = gc * linv_ref[...]
    gcs = scaled.astype(BF)
    product = scaled * ctx.astype(F32)
    lanes = head_of_lane((B, SHARE))
    q = q_ref[...]
    qt_s[...] = q.T.reshape(LH, HD, B)
    gt_s[...] = gcs.T.reshape(LH, HD, B)
    for h in range(LH):
        gm_s[h] = jnp.where(lanes == h, gcs, jnp.zeros_like(gcs))
        delta = jnp.sum(jnp.where(lanes == h, product, 0.0), axis=1, keepdims=True)
        dl_s[h] = jnp.broadcast_to(delta, (B, B))

    def attend(nb):
        start = pl.multiple_of((b + 1 - nb) * B, B)

        def head(h, carry):
            gm = gm_s[h]
            for r in range(nb):
                slot = SLOTS - nb + r
                cols = slice(slot * B, (slot + 1) * B)
                dp = dot_nt(gm, v_ref[pl.ds(pl.multiple_of(start + r * B, B), B), :])
                ds_s[:, cols] = (p_ref[h, :, cols].astype(F32) * (dp - dl_s[h])).astype(BF)
            live = slice((SLOTS - nb) * B, STRIP)
            keys = pl.ds(start, nb * B)
            res_s[h] = dot(ds_s[:, live], k_ref[keys, :])
            dkt_s[h, :, keys] += dot(qt_s[h], ds_s[:, live])
            dvt_s[h, :, keys] += dot(gt_s[h], p_ref[h, :, live])
            return carry

        lax.fori_loop(0, LH, head, 0)

    count = b - ids[1 + b] + 1
    for nb in range(1, SLOTS + 1):
        pl.when(count == nb)(functools.partial(attend, nb))

    dq = res_s[0]
    for h in range(1, LH):
        dq = jnp.where(lanes == h, res_s[h], dq)
    dq = (dq * (1.0 / math.sqrt(HD))).astype(BF)
    here = pl.ds(pl.multiple_of(b * B, B), B)
    dkt = dkt_s[:, :, here].reshape(SHARE, B).astype(BF)
    dvt = dvt_s[:, :, here].reshape(SHARE, B).astype(BF)
    dk = dkt.T
    dv = dvt.T
    bs_ref[0:1, :] += jnp.sum(dq.astype(F32), axis=0, keepdims=True)
    bs_ref[1:2, :] += jnp.sum(dv.astype(F32), axis=0, keepdims=True)

    for r, x in enumerate((x0, x1, x2, x3)):
        xs[:, feature_block(t ^ r)] = x[...].astype(F32)
    rows = xs[...]
    mean, rstd = row_stats(rows)
    xhat = (rows - mean) * rstd
    n1 = (xhat * vec[0:1, :] + vec[1:2, :]).astype(BF)
    acc_s[0:SHARE, :] += dot(dq.T, n1)
    acc_s[SHARE : 2 * SHARE, :] += dot(dkt, n1)
    acc_s[2 * SHARE : 3 * SHARE, :] += dot(dvt, n1)
    acc_s[3 * SHARE :, :] += dot(ctx.T, ghl)

    grad = dot_nt(dq, wq[...]) + dot_nt(dk, wk[...]) + dot_nt(dv, wv[...])
    xs[...] = grad
    split_store(keep_ref, send_ref, xs, core)
    scaled = grad * vec[0:1, :]
    first = jnp.sum(scaled, axis=1, keepdims=True)
    second = jnp.sum(scaled * xhat, axis=1, keepdims=True)
    column = lax.broadcasted_iota(jnp.int32, (B, 128), 1)
    packed = jnp.where(
        column == 0, first, jnp.where(column == 1, second, jnp.where(column == 2, mean, rstd))
    )
    st_ref[...] = packed.T[0:8, :]

    @pl.when(i == NB - 1)
    def _():
        gw_ref[...] = acc_s[...].astype(BF)


def attention_backward(ids, xs, gh, ga, gb, p, q, linv, ctx, k, v, vec, wq, wk, wv, wd):
    row = lambda width: pl.BlockSpec((B, width), lambda i, ids: (NB - 1 - i, 0))
    own = lambda width: pl.BlockSpec((B, width), lambda i, ids: ((NB - 1 - i) // 2, 0))
    whole = lambda shape: pl.BlockSpec(shape, lambda i, ids: (0,) * len(shape))
    return pl.pallas_call(
        bwd_kernel,
        grid_spec=pltpu.PrefetchScalarGridSpec(
            num_scalar_prefetch=1,
            grid=(NB,),
            in_specs=[row(SHARE)] * 4
            + [own(D), own(D // 2), own(D // 2)]
            + [pl.BlockSpec((LH, B, STRIP), lambda i, ids: (0, NB - 1 - i, 0))]
            + [row(SHARE)] * 3
            + [whole((SEQ, SHARE))] * 2
            + [whole((8, D))]
            + [whole((D, SHARE))] * 3
            + [whole((SHARE, D))],
            out_specs=[
                row(D // 2),
                row(D // 2),
                pl.BlockSpec((8, B), lambda i, ids: (0, NB - 1 - i)),
                row(SHARE),
                whole((D, D)),
                whole((8, SHARE)),
            ],
            scratch_shapes=[
                pltpu.VMEM((B, D), F32),
                pltpu.VMEM((B, D), BF),
                pltpu.VMEM((LH, B, SHARE), BF),
                pltpu.VMEM((LH, HD, B), BF),
                pltpu.VMEM((LH, HD, B), BF),
                pltpu.VMEM((LH, B, B), F32),
                pltpu.VMEM((B, STRIP), BF),
                pltpu.VMEM((LH, B, SHARE), F32),
                pltpu.VMEM((LH, HD, SEQ), F32),
                pltpu.VMEM((LH, HD, SEQ), F32),
                pltpu.VMEM((4 * SHARE, D), F32),
            ],
        ),
        out_shape=[
            jax.ShapeDtypeStruct((SEQ, D // 2), BF),
            jax.ShapeDtypeStruct((SEQ, D // 2), BF),
            jax.ShapeDtypeStruct((8, SEQ), F32),
            jax.ShapeDtypeStruct((SEQ, SHARE), BF),
            jax.ShapeDtypeStruct((4 * SHARE, D), BF),
            jax.ShapeDtypeStruct((8, SHARE), F32),
        ],
        compiler_params=params(),
        cost_estimate=pl.CostEstimate(
            flops=30 * 10**9, bytes_accessed=50 * 2**20, transcendentals=0
        ),
        name="attention_backward",
    )(ids, *xs, gh, ga, gb, p, q, linv, ctx, k, v, vec, wq, wk, wv, wd)


def swap(value, axis, bit):
    size = lax.axis_size(axis)
    return lax.ppermute(value, axis, [(i, i ^ bit) for i in range(size)])


def dp_bits():
    bits, bit = [], 1
    while bit < lax.axis_size("dp"):
        bits.append(bit)
        bit *= 2
    return bits


def dp_total(value):
    for bit in dp_bits():
        value = value + swap(value, "dp", bit)
    return value


def pick(value, axis, index):
    return lax.dynamic_index_in_dim(value, index, axis, keepdims=False)


def dp_scatter(value, order):
    rank = lax.axis_index("dp")
    size = lax.axis_size("dp")
    levels = len(dp_bits())
    rest = value.shape[1:]
    value = value.reshape((2,) * levels + rest)
    left = list(reversed(dp_bits()))
    for bit in order:
        axis = left.index(bit)
        left.pop(axis)
        mine = (rank // bit) % 2
        other = swap(pick(value, axis, 1 - mine), "dp", bit)
        value = (pick(value, axis, mine).astype(F32) + other.astype(F32)).astype(BF)
    return value.reshape(rest)


def shards(
    tokens,
    out_grad,
    segments,
    padding,
    norm1_gain,
    norm1_bias,
    w_query,
    b_query,
    w_key,
    w_value,
    b_value,
    w_dense,
    dense_bias,
    norm2_gain,
    norm2_bias,
    w_up,
    b_up,
    w_down,
    down_bias,
):
    t = lax.axis_index("tensor")
    rank = lax.axis_index("dp")
    size = lax.axis_size("dp")
    core, y = t % 2, t // 2
    core_swap = lambda value: swap(value, "tensor", 1)
    y_swap = lambda value: swap(value, "tensor", 2)
    rows8 = lambda value: jnp.pad(value, ((0, 8 - value.shape[0]), (0, 0)))

    x_own = tokens
    x_y = y_swap(x_own)
    x_core = core_swap(x_own)
    x_far = core_swap(x_y)
    xs = [x_own, x_core, x_y, x_far]
    vectors = jnp.stack([norm1_gain, norm1_bias, dense_bias, norm2_gain, norm2_bias, down_bias])
    vec = lax.dynamic_update_slice(jnp.zeros((6, D), BF), vectors, (0, t * SHARE))
    vec = vec + core_swap(vec)
    vec = rows8((vec + y_swap(vec)).astype(F32))

    part = D // size
    cut = lambda w: lax.dynamic_slice_in_dim(w, rank * part, part, 0)
    w_part = y_swap(jnp.concatenate([cut(w_up), cut(w_down)], axis=1))
    w_other = lax.all_gather(w_part, "dp", axis=0, tiled=True)
    up_other, down_other = w_other[:, :UNITS], w_other[:, UNITS:]
    b_up_pair = jnp.stack([b_up, y_swap(b_up)]).astype(F32)

    seg = segments.reshape(SEQ)
    index = jnp.arange(SEQ, dtype=jnp.int32)
    first = jnp.zeros((SEQ,), jnp.int32)
    for value in range(1, 4):
        first = jnp.where(seg == value, jnp.sum((seg < value).astype(jnp.int32)), first)
    lowest = jnp.maximum(first, index - (WIN - 1))
    ids = jnp.concatenate([t[None].astype(jnp.int32), lowest[::B] // B])
    pad_row = rows8(jnp.where(padding.reshape(1, SEQ) == 1, 0.0, NEG).astype(F32))
    heads = t * LH + jnp.arange(LH)
    slopes = jnp.exp2(-8.0 * (heads.astype(F32) + 1.0) / HEADS)
    alibi = rows8(slopes[:, None] * (jnp.arange(STRIP) - (STRIP - 1)).astype(F32)[None, :])

    p, q, k, v, linv, ctx, keep, send, hm = attention_forward(
        ids, xs, vec, w_query, w_key, w_value,
        rows8(jnp.stack([b_query, b_value]).astype(F32)), w_dense,
        lowest.reshape(SEQ, 1), pad_row, alibi,
    )

    by_y = lambda value, which: pick(value.reshape(NB // 2, 2, B, value.shape[-1]), 1, which).reshape(
        OWN, value.shape[-1]
    )
    d_own = by_y(out_grad, y)
    d_y = y_swap(by_y(out_grad, 1 - y))
    ds = [d_own, core_swap(d_own), d_y, core_swap(d_y)]

    both = (keep.astype(F32) + core_swap(send).astype(F32)).astype(BF)
    mine = by_y(both, y).astype(F32) + y_swap(by_y(both, 1 - y)).astype(F32)
    a_own = mine.astype(BF)
    a_par = core_swap(a_own)

    mk, ms, gn, h1, gu, gd, bs = feed_forward(
        ids, a_own, a_par, xs, ds, vec, rows8(b_up_pair), w_up, up_other, w_down, down_other
    )
    gr = core_swap(gn)
    mr = core_swap(ms)
    gh, gs, out_own, out_send, cs = middle(ids, h1, gn, gr, ds, mk, mr, vec)
    ga = y_swap(gs)
    gb = core_swap(ga)

    out_y = y_swap(out_send)
    pair = jnp.stack([out_own, out_y]).reshape(2, NB // 2, B, SHARE)
    output = jnp.where(y == 0, pair, pair[::-1]).transpose(1, 0, 2, 3).reshape(SEQ, SHARE)

    grads = jnp.concatenate([gu, gd], axis=1).reshape(size, D // size, 4 * UNITS)
    bits = dp_bits()
    grads = dp_scatter(grads, bits).reshape(D // size, 2, 2, UNITS)
    grads = grads[:, :, 0].astype(F32) + y_swap(grads[:, :, 1]).astype(F32)
    w_up_grad = grads[:, 0]
    w_down_grad = grads[:, 1].T

    keep, send, stats, ghx, gw, qv = attention_backward(
        ids, xs, gh, ga, gb, p, q, linv, ctx, k, v, vec, w_query, w_key, w_value, w_dense
    )
    both = (keep.astype(F32) + core_swap(send).astype(F32)).astype(BF).reshape(SEQ, 2, SHARE)
    g_first = pick(both, 1, y).astype(F32) + y_swap(pick(both, 1, 1 - y)).astype(F32)
    sums = stats[0:2]
    sums = sums + core_swap(sums)
    sums = sums + y_swap(sums)
    first, second = sums[0][:, None] / D, sums[1][:, None] / D
    mean, rstd = stats[2][:, None], stats[3][:, None]
    xhat = (tokens.astype(F32) - mean) * rstd
    scaled = g_first * norm1_gain.astype(F32)[None, :]
    tokens_grad = ghx.astype(F32) + rstd * (scaled - first - xhat * second)

    gw = gw.reshape(4 * SHARE, size, D // size).transpose(1, 0, 2)
    gw = dp_scatter(gw, bits).astype(F32).reshape(4, SHARE, D // size)

    local = jnp.max(hm, axis=(1, 2))
    for bit in bits:
        local = jnp.maximum(local, swap(local, "dp", bit))
    head_max = local
    cs4 = cs[0:4].reshape(4, 2, 2, SHARE)
    cs4 = pick(cs4, 2, core)
    early = jnp.concatenate([pick(cs4, 1, y).reshape(-1), bs[0, :UNITS]])
    away = jnp.concatenate([pick(cs4, 1, 1 - y).reshape(-1), bs[0, UNITS:]])
    early = dp_total(early + y_swap(away))
    late = dp_total(
        jnp.concatenate([jnp.sum(g_first * xhat, axis=0), jnp.sum(g_first, axis=0), qv[0], qv[1]])
    )
    of = lambda value, n: value[n * SHARE : (n + 1) * SHARE]

    column_scale = jnp.repeat(jnp.sqrt(TAU / jnp.maximum(head_max, TAU)), HD)
    return (
        output,
        tokens_grad,
        of(late, 0),
        of(late, 1),
        gw[0].T,
        of(late, 2),
        gw[1].T,
        gw[2].T,
        of(late, 3),
        gw[3],
        of(early, 2),
        of(early, 0),
        of(early, 1),
        w_up_grad,
        early[4 * SHARE :],
        w_down_grad,
        of(early, 3),
        head_max,
        w_query.astype(F32) * column_scale,
        b_query.astype(F32) * column_scale,
        w_key.astype(F32) * column_scale,
    )


def solution(mesh):
    in_specs = (
        P("dp", "tensor"),
        P("dp", "tensor"),
        P("dp", None),
        P("dp", None),
        P("tensor"),
        P("tensor"),
        P(None, "tensor"),
        P("tensor"),
        P(None, "tensor"),
        P(None, "tensor"),
        P("tensor"),
        P("tensor", None),
        P("tensor"),
        P("tensor"),
        P("tensor"),
        P(None, "tensor"),
        P("tensor"),
        P("tensor", None),
        P("tensor"),
    )
    out_specs = (
        P("dp", "tensor"),
        P("dp", "tensor"),
        P("tensor"),
        P("tensor"),
        P("dp", "tensor"),
        P("tensor"),
        P("dp", "tensor"),
        P("dp", "tensor"),
        P("tensor"),
        P("tensor", "dp"),
        P("tensor"),
        P("tensor"),
        P("tensor"),
        P("dp", "tensor"),
        P("tensor"),
        P("tensor", "dp"),
        P("tensor"),
        P("tensor"),
        P(None, "tensor"),
        P("tensor"),
        P(None, "tensor"),
    )
    return jax.shard_map(shards, mesh=mesh, in_specs=in_specs, out_specs=out_specs, check_vma=False)
```

time: 1200 us -> 473 us (0.39)
  waiting for transfers between devices: 682 us -> 176 us
  matrix products: 234 us -> 0 us
  Pallas kernels: 0 us -> 151 us
  other arithmetic: 120 us -> 37.8 us
  blocking collectives: 65 us -> 0 us
  starting transfers between devices: 1.17 us -> 30.9 us
  loops' own time: 22.3 us -> 0 us
    reduce_scatter x6 -> x0, waiting for transfers between devices: 397 us -> none  [the longest x1 92.5 us: shards(): lax.psum_scatter(grad_w_up, 'dp', scatter_dimension=0, tiled=True)]
    psum x3 -> x0, waiting for transfers between devices: 240 us -> none  [reduce_part(): lax.psum(partial_term.astype(jnp.bfloat16), 'tensor').astype(jnp.float32)]
    dot_general x46 -> x0, matrix products: 234 us -> none  [the longest x8 61 us: block_inputs(): jnp.einsum('qhd,khd->hqk', q_block, k_block, preferred_element_type=jnp.f...]
    ppermute x0 -> x39, waiting for transfers between devices: none -> 176 us  [swap(): return lax.ppermute(value, axis, [(i, i ^ bit) for i in range(size)])]
    pallas_call x0 -> x4, Pallas kernels: none -> 151 us  [the longest x1 48.7 us: feed_forward(): pl.pallas_call(mlp_kernel, grid_spec=pltpu.PrefetchScalarGridSpec(num_sca...]
    all_gather x2 -> x1, waiting for transfers between devices: 43.6 us -> 0.01 us  [shards(): w_other = lax.all_gather(w_part, 'dp', axis=0, tiled=True)]
    psum x1 -> x0, blocking collectives: 37.1 us -> none  [shards(): lax.psum((own_share(grad_gain_first), own_share(grad_bias_first), grad_b_...]
    ppermute x0 -> x39, starting transfers between devices: none -> 30.9 us  [swap(): return lax.ppermute(value, axis, [(i, i ^ bit) for i in range(size)])]
  transfers between devices with their start and end apart: 11 -> 40, of which waited for: 11 -> 20; matrix products, arithmetic and copies ran while one was open for 8% -> 19% of each run, Pallas kernels for 0% -> 20%
where the time goes in v1:
time: 473 us
  waiting for transfers between devices  176 us (37%)
  Pallas kernels  151 us (32%)
  local copies, waits for them, and re-layouts  61.7 us (13%)
  other arithmetic  37.8 us (8%)
  starting transfers between devices  30.9 us (7%)
  between operations  14.7 us (3%)
    ppermute x39, waiting for transfers between devices, swap(): return lax.ppermute(value, axis, [(i, i ^ bit) for i in range(size)])  176 us
    pallas_call x1, Pallas kernels, feed_forward(): pl.pallas_call(mlp_kernel, grid_spec=pltpu.PrefetchScalarGridSpec(num_sca...  48.7 us
    pallas_call x1, Pallas kernels, attention_backward(): pl.pallas_call(bwd_kernel, grid_spec=pltpu.PrefetchScalarGridSpec(num_sca...  48.1 us
    pallas_call x1, Pallas kernels, attention_forward(): pl.pallas_call(fwd_kernel, grid_spec=pltpu.PrefetchScalarGridSpec(num_sca...  44.6 us
    ppermute x39, starting transfers between devices, swap(): return lax.ppermute(value, axis, [(i, i ^ bit) for i in range(size)])  30.9 us
    dynamic_slice x7, local copies, waits for them, and re-layouts, pick(): return lax.dynamic_index_in_dim(value, index, axis, keepdims=False)  17.7 us
    unnamed x61, local copies, waits for them, and re-layouts  15.4 us
    pallas_call x1, Pallas kernels, middle(): pl.pallas_call(mid_kernel, grid_spec=pltpu.PrefetchScalarGridSpec(num_sca...  9.77 us
  transfers between devices with their start and end apart: 40, of which 20 were waited for; matrix products, arithmetic and copies ran while one was open for 19% of the time, Pallas kernels for 20%

profile of v1, /device:TPU:0, one launch (start us, length us, event | category | flops | bytes accessed | tf_op | source)
XLA Modules:
  0.0 472.6 jit_solution(12730907985115107839)
XLA Ops:
  7.8 2.6 collective-permute-start.1
  22.4 12.3 %collective-permute-done.1.x2 = bf16[2048,256]{1,0:T(8,128)(2,1)} collective-permute-done((bf16[2048,256]{1,0:T(8,128)(2,1)}, bf16[2048,256]{1,0:T(8,128)(2,1)}, u32[]{:S(2)}, u32[]{:S(2)}) %collective-permute-start.1) | collective-permute-done | bytes 1048608 | tf_op jit(solution)/shard_map/ppermute | solution.py:562
  34.7 10.8 %collective-permute-done.12 = bf16[128,2048]{1,0:T(8,128)(2,1)S(1)} collective-permute-done((bf16[128,2048]{1,0:T(8,128)(2,1)S(1)}, bf16[128,2048]{1,0:T(8,128)(2,1)S(1)}, u32[]{:S(2)}, u32[]{:S(2)}) %collective-permute-start.12) | collective-permute-done | bytes 524320 | tf_op jit(solution)/shard_map/ppermute | solution.py:562
  51.5 44.6 %attention_forward.1 = (bf16[4,2048,1280]{2,1,0:T(8,128)(2,1)}, bf16[2048,256]{1,0:T(8,128)(2,1)}, bf16[2048,256]{1,0:T(8,128)(2,1)}, bf16[2048,256]{1,0:T(8,128...) custom-call(s32[9]{0:T(128)} %pad_add_fusion.ids, ...), custom_call_target="tpu_custom_call" | custom-call | flops 16000000000 | bytes 41943040 | tf_op jit(solution)/shard_map/attention_forward/pallas_call | solution.py:160
  96.1 4.3 collective-permute-done.5
  100.5 2.2 add_convert_fusion.1
  105.8 23.2 %collective-permute-done.6 = bf16[1024,512]{1,0:T(8,128)(2,1)S(1)} collective-permute-done((bf16[1024,512]{1,0:T(8,128)(2,1)S(1)}, bf16[1024,512]{1,0:T(8,128)(2,1)S(1)}, u32[]{:S(2)}, u32[]{:S(2)}) %collective-permute-start.6) | collective-permute-done | bytes 1048608 | tf_op jit(solution)/shard_map/ppermute | solution.py:562
  129.9 9.6 %collective-permute-done.9.d2 = bf16[1024,256]{1,0:T(8,128)(2,1)S(1)} collective-permute-done((bf16[1024,256]{1,0:T(8,128)(2,1)S(1)}, bf16[1024,256]{1,0:T(8,128)(2,1)S(1)}, u32[]{:S(2)}, u32[]{:S(2)}) %collective-permute-start.9) | collective-permute-done | bytes 524320 | tf_op jit(solution)/shard_map/ppermute | solution.py:562
  143.8 4.8 %fusion.23 = (bf16[1024,1024]{1,0:T(8,128)(2,1)}, bf16[1024,1024]{1,0:T(8,128)(2,1)}) fusion(bf16[1024,2048]{1,0:T(8,128)(2,1)} %all-gather.2.cloned.1.call-done), kind=kLoop, calls=%fused_computation.98 | loop fusion | bytes 8388608 | tf_op jit(solution)/shard_map/slice | solution.py:642
  149.6 48.7 %feed_forward.1 = (bf16[1024,512]{1,0:T(8,128)(2,1)}, bf16[1024,512]{1,0:T(8,128)(2,1)}, bf16[1024,1024]{1,0:T(8,128)(2,1)}, f32[1024,1024]{1,0:T(8,128)}, bf16[...) custom-call(s32[9]{0:T(128)} %pad_add_fusion.ids, bf16[1024,512]{1,0:T(8,128)(2,1)} %copy-done.10, ...), custom_call_target="tpu_custom_call" | custom-call | flops 25999998976 | bytes 41943040 | tf_op jit(solution)/shard_map/feed_forward/pallas_call | solution.py:281
  199.0 3.5 collective-permute-done.36
  202.6 3.5 collective-permute-done.37
  206.1 2.2 collective-permute-start.38
  208.3 2.2 collective-permute-done.38
  213.8 9.8 %second_norm_backward.1 = (bf16[1024,1024]{1,0:T(8,128)(2,1)}, bf16[1024,512]{1,0:T(8,128)(2,1)}, bf16[1024,256]{1,0:T(8,128)(2,1)}, bf16[1024,256]{1,0:T(8,128)(2,1)}, f32[8,1024]{1,0:T(8,128)}) custom-call(s32[9]{0:T(128)} %pad_add_fusion.ids, f32[1024,1024]{1,0:T(8,128)} %get-tuple-element.50.h1, bf16[1024,1024]{1,0:T(8,128)(2,1)} %get-tuple-element.51.gn, ...), custom_call_target="tpu_custom_call" | custom-call | flops 20971520 | bytes 16777216 | tf_op jit(solution)/shard_map/second_norm_backward/pallas_call | solution.py:376
  226.5 7.9 %pad_maximum_fusion = bf16[1024,4096]{1,0:T(8,128)(2,1)} fusion(bf16[1024,2048]{1,0:T(8,128)(2,1)} %get-tuple-element.73, bf16[1024,2048]{1,0:T(8,128)(2,1)} %get-tuple-element.72), kind=kLoop, calls=%fused_computation | loop fusion | flops 16777216 | bytes 16777216 | tf_op jit(solution)/shard_map/concatenate | solution.py:688
  234.4 11.4 %collective-permute-done.28 = f32[2048]{0:T(1024)S(1)} collective-permute-done((f32[2048]{0:T(1024)S(1)}, f32[2048]{0:T(1024)S(1)}, u32[]{:S(2)}, u32[]{:S(2)}) %collective-permute-start.28) | collective-permute-done | bytes 8224 | tf_op jit(solution)/shard_map/ppermute | solution.py:562
  247.5 7.9 %constant_dynamic-slice_fusion.1 = (bf16[2,2,1,128,4096]{4,3,2,1,0:T(8,128)(2,1)}, bf16[2,2,1,128,4096]{4,3,2,1,0:T(8,128)(2,1)}) fusion(bf16[2,2,2,128,4096]{4,3,2,1,0:T(8,128)(2,1)} %bitcast.105, s32[]{:T(128)S(6)} %select_n.175, s32[]{:T(128)S(6)} %select_n.176), kind=kLoop, calls=%fused_computation.70 | loop fusion | bytes 16777224 | tf_op jit(solution)/shard_map/jit(dynamic_index_in_dim)/dynamic_slice | solution.py:580
  255.4 6.5 %copy.77 = bf16[2,2,1,128,4096]{3,4,0,1,2:T(8,128)(2,1)} copy(bf16[2,2,1,128,4096]{4,3,2,1,0:T(8,128)(2,1)} %get-tuple-element.146) | data formatting | bytes 8388608 | tf_op jit(solution)/shard_map/jit(dynamic_index_in_dim)/dynamic_slice | solution.py:580
  267.7 2.3 collective-permute-start.31
  270.6 6.4 %copy.88 = bf16[2,2,1,128,4096]{3,4,0,1,2:T(8,128)(2,1)} copy(bf16[2,2,1,128,4096]{4,3,2,1,0:T(8,128)(2,1)} %get-tuple-element.145) | data formatting | bytes 8388608
  279.6 48.1 %attention_backward.1 = (bf16[2048,512]{1,0:T(8,128)(2,1)}, bf16[2048,512]{1,0:T(8,128)(2,1)}, f32[8,2048]{1,0:T(8,128)}, bf16[2048,256]{1,0:T(8,128)(2,1)}, bf1...) custom-call(s32[9]{0:T(128)} %pad_add_fusion.ids, bf16[2048,256]{1,0:T(8,128)(2,1)} %x0.3, ...), custom_call_target="tpu_custom_call" | custom-call | flops 30000001024 | bytes 52428800 | tf_op jit(solution)/shard_map/attention_backward/pallas_call | solution.py:509
  331.8 23.9 %collective-permute-done.32 = bf16[2,2,128,4096]{2,3,0,1:T(8,128)(2,1)} collective-permute-done((bf16[2,2,128,4096]{2,3,0,1:T(8,128)(2,1)}, bf16[2,2,128,4096]{2,3,0,1:T(8,128)(2,1)}, u32[]{:S(2)}, u32[]{:S(2)}) %collective-permute-start.32) | collective-permute-done | bytes 4194336 | tf_op jit(solution)/shard_map/ppermute | solution.py:562
  355.7 3.3 fusion
  366.0 6.9 %collective-permute-done.25 = bf16[2,2,1024,128]{3,2,1,0:T(8,128)(2,1)S(1)} collective-permute-done((bf16[2,2,1024,128]{3,2,1,0:T(8,128)(2,1)S(1)}, bf16[2,2,1024,128]{3,2,1,0:T(8,128)(2,1)S(1)}, u32[]{:S(2)}, u32[]{:S(2)}) %collective-permute-start.25) | collective-permute-done | bytes 1048608 | tf_op jit(solution)/shard_map/ppermute | solution.py:562
  375.3 2.4 copy.72
  382.3 36.2 %collective-permute-done.33 = bf16[2,128,4096]{1,2,0:T(8,128)(2,1)} collective-permute-done((bf16[2,128,4096]{1,2,0:T(8,128)(2,1)}, bf16[2,128,4096]{1,2,0:T(8,128)(2,1)}, u32[]{:S(2)}, u32[]{:S(2)}) %collective-permute-start.33) | collective-permute-done | bytes 2097184 | tf_op jit(solution)/shard_map/ppermute | solution.py:562
  418.5 2.8 fusion.1
  422.5 2.2 collective-permute-done.26
  428.7 5.0 %multiply_reduce_fusion = (f32[256]{0:T(256)S(1)}, f32[256]{0:T(256)S(1)}, f32[2048,256]{1,0:T(8,128)}) fusion(bf16[2048,256]{1,0:T(8,128)(2,1)} %x0.3, bf16[2048,256]{1,0:T(8,128)(2,1)} %collective-permute-done.19, bf16[2048,1,256]{2,0,1:T(8,128)(2,1)} %copy.87, f32[2048]{0:T(1024)S(1)} %bitcast.125, f32[2048]{0:T(1024)S(1)} %bitcast.124, ...), kind=kLoop, calls=%fused_computation.16 | loop fusion | flops 8388096 | bytes 6327296 | tf_op jit(solution)/shard_map/reduce_sum | solution.py:722
  434.5 17.3 %collective-permute-done.34 = bf16[128,4096]{0,1:T(8,128)(2,1)} collective-permute-done((bf16[128,4096]{0,1:T(8,128)(2,1)}, bf16[128,4096]{0,1:T(8,128)(2,1)}, u32[]{:S(2)}, u32[]{:S(2)}) %collective-permute-start.34) | collective-permute-done | bytes 1048608 | tf_op jit(solution)/shard_map/ppermute | solution.py:562
  456.1 2.5 collective-permute-done.23
  (213 shorter events, 80.5 us)
Async XLA Ops:
  7.2 136.6 %all-gather.2.cloned.1.call-start = ((), (), s32[]{:S(2)}) async-start(), calls=%async_computation | async-start | bytes 4718592 | tf_op jit(solution)/shard_map/all_gather | solution.py:641
  7.2 44.2 %collective-permute-start = (bf16[2048,256]{1,0:T(8,128)(2,1)}, bf16[2048,256]{1,0:T(8,128)(2,1)}, u32[]{:S(2)}, u32[]{:S(2)}) collective-permute-start(bf16[2048,256]{1,0:T(8,128)(2,1)} %x0.3), channel_id=1, source_target_pairs={{0,1},{1,0},{2,3},{3,2},{4,5},{5,4},{6,7},{7,6},{8,9},{9,8},{10,11... | collective-permute-start | bytes 3145736 | tf_op jit(solution)/shard_map/ppermute | solution.py:562
  7.8 26.9 %collective-permute-start.1 = (bf16[2048,256]{1,0:T(8,128)(2,1)}, bf16[2048,256]{1,0:T(8,128)(2,1)}, u32[]{:S(2)}, u32[]{:S(2)}) collective-permute-start(bf16[2048,256]{1,0:T(8,128)(2,1)} %x0.3), channel_id=1, source_target_pairs={{0,2},{1,3},{2,0},{3,1},{4,6},{5,7},{6,4},{7,5},{8,10},{9,11},{10,... | collective-permute-start | bytes 3145736 | tf_op jit(solution)/shard_map/ppermute | solution.py:562
  14.4 32.6 %collective-permute-start.3 = (bf16[6,1024]{1,0:T(8,128)(2,1)S(1)}, bf16[6,1024]{1,0:T(8,128)(2,1)S(1)}, u32[]{:S(2)}, u32[]{:S(2)}) collective-permute-start(bf16[6,1024]{1,0:T(8,128)(2,1)S(1)} %constant_dynamic-update-slice_fusion.1), channel_id=1, source_target_pairs={{0,1},{1,0},{2,3},{3,2},{4,5},{5,4},{6,7},{7,6},{8,9},{9,8},{10,11... | collective-permute-start | bytes 36872 | tf_op jit(solution)/shard_map/ppermute | solution.py:562
  15.7 29.8 %collective-permute-start.12 = (bf16[128,2048]{1,0:T(8,128)(2,1)S(1)}, bf16[128,2048]{1,0:T(8,128)(2,1)S(1)}, u32[]{:S(2)}, u32[]{:S(2)}) collective-permute-start(bf16[128,2048]{1,0:T(8,128)(2,1)S(1)} %pad_maximum_fusion.2), channel_id=1, source_target_pairs={{0,2},{1,3},{2,0},{3,1},{4,6},{5,7},{6,4},{7,5},{8,10},{9,11},{10,... | collective-permute-start | bytes 1572872 | tf_op jit(solution)/shard_map/ppermute | solution.py:562
  34.7 16.8 %collective-permute-start.2 = (bf16[2048,256]{1,0:T(8,128)(2,1)}, bf16[2048,256]{1,0:T(8,128)(2,1)}, u32[]{:S(2)}, u32[]{:S(2)}) collective-permute-start(bf16[2048,256]{1,0:T(8,128)(2,1)} %collective-permute-done.1.x2), channel_id=1, source_target_pairs={{0,1},{1,0},{2,3},{3,2},{4,5},{5,4},{6,7},{7,6},{8,9},{9,8},{10,11... | collective-permute-start | bytes 3145736 | tf_op jit(solution)/shard_map/ppermute | solution.py:562
  102.9 26.1 %collective-permute-start.6 = (bf16[1024,512]{1,0:T(8,128)(2,1)S(1)}, bf16[1024,512]{1,0:T(8,128)(2,1)S(1)}, u32[]{:S(2)}, u32[]{:S(2)}) collective-permute-start(bf16[1024,512]{1,0:T(8,128)(2,1)S(1)} %bitcast.117), channel_id=1, source_target_pairs={{0,2},{1,3},{2,0},{3,1},{4,6},{5,7},{6,4},{7,5},{8,10},{9,11},{10,... | collective-permute-start | bytes 3145736 | tf_op jit(solution)/shard_map/ppermute | solution.py:562
  104.8 34.6 %collective-permute-start.9 = (bf16[1024,256]{1,0:T(8,128)(2,1)S(1)}, bf16[1024,256]{1,0:T(8,128)(2,1)S(1)}, u32[]{:S(2)}, u32[]{:S(2)}) collective-permute-start(bf16[1024,256]{1,0:T(8,128)(2,1)S(1)} %bitcast.123), channel_id=1, source_target_pairs={{0,2},{1,3},{2,0},{3,1},{4,6},{5,7},{6,4},{7,5},{8,10},{9,11},{10,... | collective-permute-start | bytes 1572872 | tf_op jit(solution)/shard_map/ppermute | solution.py:562
  129.3 19.3 %collective-permute-start.7 = (bf16[1024,512]{1,0:T(8,128)(2,1)S(1)}, bf16[1024,512]{1,0:T(8,128)(2,1)}, u32[]{:S(2)}, u32[]{:S(2)}) collective-permute-start(bf16[1024,512]{1,0:T(8,128)(2,1)S(1)} %fusion.4.a_own), channel_id=1, source_target_pairs={{0,1},{1,0},{2,3},{3,2},{4,5},{5,4},{6,7},{7,6},{8,9},{9,8},{10,11... | collective-permute-start | bytes 3145736 | tf_op jit(solution)/shard_map/ppermute | solution.py:562
  129.4 19.2 %collective-permute-start.8 = (bf16[1024,256]{1,0:T(8,128)(2,1)S(1)}, bf16[1024,256]{1,0:T(8,128)(2,1)S(1)}, u32[]{:S(2)}, u32[]{:S(2)}) collective-permute-start(bf16[1024,256]{1,0:T(8,128)(2,1)S(1)} %bitcast.113), channel_id=1, source_target_pairs={{0,1},{1,0},{2,3},{3,2},{4,5},{5,4},{6,7},{7,6},{8,9},{9,8},{10,11... | collective-permute-start | bytes 1572872 | tf_op jit(solution)/shard_map/ppermute | solution.py:562
  139.5 9.1 %collective-permute-start.10 = (bf16[1024,256]{1,0:T(8,128)(2,1)S(1)}, bf16[1024,256]{1,0:T(8,128)(2,1)S(1)}, u32[]{:S(2)}, u32[]{:S(2)}) collective-permute-start(bf16[1024,256]{1,0:T(8,128)(2,1)S(1)} %collective-permute-done.9.d2), channel_id=1, source_target_pairs={{0,1},{1,0},{2,3},{3,2},{4,5},{5,4},{6,7},{7,6},{8,9},{9,8},{10,11... | collective-permute-start | bytes 1572872 | tf_op jit(solution)/shard_map/ppermute | solution.py:562
  198.3 13.7 %collective-permute-start.13 = (bf16[1024,1024]{1,0:T(8,128)(2,1)}, bf16[1024,1024]{1,0:T(8,128)(2,1)S(1)}, u32[]{:S(2)}, u32[]{:S(2)}) collective-permute-start(bf16[1024,1024]{1,0:T(8,128)(2,1)} %get-tuple-element.51.gn), channel_id=1, source_target_pairs={{0,1},{1,0},{2,3},{3,2},{4,5},{5,4},{6,7},{7,6},{8,9},{9,8},{10,11... | collective-permute-start | bytes 6291464 | tf_op jit(solution)/shard_map/ppermute | solution.py:562
  198.3 13.7 %collective-permute-start.14 = (bf16[1024,512]{1,0:T(8,128)(2,1)}, bf16[1024,512]{1,0:T(8,128)(2,1)S(1)}, u32[]{:S(2)}, u32[]{:S(2)}) collective-permute-start(bf16[1024,512]{1,0:T(8,128)(2,1)} %get-tuple-element.53), channel_id=1, source_target_pairs={{0,1},{1,0},{2,3},{3,2},{4,5},{5,4},{6,7},{7,6},{8,9},{9,8},{10,11... | collective-permute-start | bytes 3145736 | tf_op jit(solution)/shard_map/ppermute | solution.py:562
  206.1 4.4 collective-permute-start.38
  223.5 40.8 %collective-permute-start.16 = (bf16[1024,512]{1,0:T(8,128)(2,1)}, bf16[1024,512]{1,0:T(8,128)(2,1)S(1)}, u32[]{:S(2)}, u32[]{:S(2)}) collective-permute-start(bf16[1024,512]{1,0:T(8,128)(2,1)} %get-tuple-element.57), channel_id=1, source_target_pairs={{0,2},{1,3},{2,0},{3,1},{4,6},{5,7},{6,4},{7,5},{8,10},{9,11},{10,... | collective-permute-start | bytes 3145736 | tf_op jit(solution)/shard_map/ppermute | solution.py:562
  226.2 19.7 %collective-permute-start.28 = (f32[2048]{0:T(1024)S(1)}, f32[2048]{0:T(1024)S(1)}, u32[]{:S(2)}, u32[]{:S(2)}) collective-permute-start(f32[2048]{0:T(1024)S(1)} %pad_maximum_fusion.3), channel_id=1, source_target_pairs={{0,2},{1,3},{2,0},{3,1},{4,6},{5,7},{6,4},{7,5},{8,10},{9,11},{10,... | collective-permute-start | bytes 24584 | tf_op jit(solution)/shard_map/ppermute | solution.py:562
  245.9 18.2 %collective-permute-start.29 = (f32[2048]{0:T(1024)S(1)}, f32[2048]{0:T(1024)S(1)}, u32[]{:S(2)}, u32[]{:S(2)}) collective-permute-start(f32[2048]{0:T(1024)S(1)} %maximum_add_fusion), channel_id=1, source_target_pairs={{0,4},{4,0},{8,12},{12,8},{16,20},{20,16},{24,28},{28,24},{1,5},{5... | collective-permute-start | bytes 24584 | tf_op jit(solution)/shard_map/ppermute | solution.py:562
  261.9 93.8 %collective-permute-start.32 = (bf16[2,2,128,4096]{2,3,0,1:T(8,128)(2,1)}, bf16[2,2,128,4096]{2,3,0,1:T(8,128)(2,1)}, u32[]{:S(2)}, u32[]{:S(2)}) collective-permute-start(bf16[2,2,128,4096]{2,3,0,1:T(8,128)(2,1)} %bitcast.110), channel_id=1, source_target_pairs={{0,4},{4,0},{8,12},{12,8},{16,20},{20,16},{24,28},{28,24},{1,5},{5... | collective-permute-start | bytes 12582920 | tf_op jit(solution)/shard_map/ppermute | solution.py:562
  262.3 15.9 %collective-permute-start.15 = (bf16[1024,256]{1,0:T(8,128)(2,1)}, bf16[1024,256]{1,0:T(8,128)(2,1)S(1)}, u32[]{:S(2)}, u32[]{:S(2)}) collective-permute-start(bf16[1024,256]{1,0:T(8,128)(2,1)} %get-tuple-element.55), channel_id=1, source_target_pairs={{0,2},{1,3},{2,0},{3,1},{4,6},{5,7},{6,4},{7,5},{8,10},{9,11},{10,... | collective-permute-start | bytes 1572872 | tf_op jit(solution)/shard_map/ppermute | solution.py:562
  264.4 15.2 %collective-permute-start.17 = (bf16[1024,512]{1,0:T(8,128)(2,1)S(1)}, bf16[1024,512]{1,0:T(8,128)(2,1)}, u32[]{:S(2)}, u32[]{:S(2)}) collective-permute-start(bf16[1024,512]{1,0:T(8,128)(2,1)S(1)} %collective-permute-done.16.ga), channel_id=1, source_target_pairs={{0,1},{1,0},{2,3},{3,2},{4,5},{5,4},{6,7},{7,6},{8,9},{9,8},{10,11... | collective-permute-start | bytes 3145736 | tf_op jit(solution)/shard_map/ppermute | solution.py:562
  267.7 9.3 %collective-permute-start.31 = (f32[2048]{0:T(1024)S(1)}, f32[2048]{0:T(1024)S(1)}, u32[]{:S(2)}, u32[]{:S(2)}) collective-permute-start(f32[2048]{0:T(1024)S(1)} %add.235), channel_id=1, source_target_pairs={{0,16},{4,20},{8,24},{12,28},{16,0},{20,4},{24,8},{28,12},{1,17},{... | collective-permute-start | bytes 24584 | tf_op jit(solution)/shard_map/ppermute | solution.py:562
  327.6 47.0 %collective-permute-start.18 = (bf16[2048,512]{1,0:T(8,128)(2,1)}, bf16[2048,512]{1,0:T(8,128)(2,1)S(1)}, u32[]{:S(2)}, u32[]{:S(2)}) collective-permute-start(bf16[2048,512]{1,0:T(8,128)(2,1)} %get-tuple-element.67), channel_id=1, source_target_pairs={{0,1},{1,0},{2,3},{3,2},{4,5},{5,4},{6,7},{7,6},{8,9},{9,8},{10,11... | collective-permute-start | bytes 6291464 | tf_op jit(solution)/shard_map/ppermute | solution.py:562
  328.6 33.5 %collective-permute-start.20 = (f32[2,2048]{1,0:T(2,128)S(1)}, f32[2,2048]{1,0:T(2,128)S(1)}, u32[]{:S(2)}, u32[]{:S(2)}) collective-permute-start(f32[2,2048]{1,0:T(2,128)S(1)} %slice.98), channel_id=1, source_target_pairs={{0,1},{1,0},{2,3},{3,2},{4,5},{5,4},{6,7},{7,6},{8,9},{9,8},{10,11... | collective-permute-start | bytes 49160 | tf_op jit(solution)/shard_map/ppermute | solution.py:562
  331.3 41.6 %collective-permute-start.25 = (bf16[2,2,1024,128]{3,2,1,0:T(8,128)(2,1)S(1)}, bf16[2,2,1024,128]{3,2,1,0:T(8,128)(2,1)S(1)}, u32[]{:S(2)}, u32[]{:S(2)}) collective-permute-start(bf16[2,2,1024,128]{3,2,1,0:T(8,128)(2,1)S(1)} %dynamic-slice_bitcast_fusion.2), channel_id=1, source_target_pairs={{0,4},{4,0},{8,12},{12,8},{16,20},{20,16},{24,28},{28,24},{1,5},{5... | collective-permute-start | bytes 3145736 | tf_op jit(solution)/shard_map/ppermute | solution.py:562
  361.8 56.7 %collective-permute-start.33 = (bf16[2,128,4096]{1,2,0:T(8,128)(2,1)}, bf16[2,128,4096]{1,2,0:T(8,128)(2,1)}, u32[]{:S(2)}, u32[]{:S(2)}) collective-permute-start(bf16[2,128,4096]{1,2,0:T(8,128)(2,1)} %dynamic-slice_bitcast_fusion), channel_id=1, source_target_pairs={{0,8},{4,12},{8,0},{12,4},{16,24},{20,28},{24,16},{28,20},{1,9},{5... | collective-permute-start | bytes 6291464 | tf_op jit(solution)/shard_map/ppermute | solution.py:562
  374.1 50.6 %collective-permute-start.26 = (bf16[2,1024,128]{2,1,0:T(8,128)(2,1)}, bf16[2,1024,128]{2,1,0:T(8,128)(2,1)}, u32[]{:S(2)}, u32[]{:S(2)}) collective-permute-start(bf16[2,1024,128]{2,1,0:T(8,128)(2,1)} %dynamic-slice_bitcast_fusion.3), channel_id=1, source_target_pairs={{0,8},{4,12},{8,0},{12,4},{16,24},{20,28},{24,16},{28,20},{1,9},{5... | collective-permute-start | bytes 1572872 | tf_op jit(solution)/shard_map/ppermute | solution.py:562
  380.7 48.0 %collective-permute-start.19 = (bf16[2048,256]{1,0:T(8,128)(2,1)}, bf16[2048,256]{1,0:T(8,128)(2,1)}, u32[]{:S(2)}, u32[]{:S(2)}) collective-permute-start(bf16[2048,256]{1,0:T(8,128)(2,1)} %bitcast.20), channel_id=1, source_target_pairs={{0,2},{1,3},{2,0},{3,1},{4,6},{5,7},{6,4},{7,5},{8,10},{9,11},{10,... | collective-permute-start | bytes 3145736 | tf_op jit(solution)/shard_map/ppermute | solution.py:562
  422.3 29.5 %collective-permute-start.34 = (bf16[128,4096]{0,1:T(8,128)(2,1)}, bf16[128,4096]{0,1:T(8,128)(2,1)}, u32[]{:S(2)}, u32[]{:S(2)}) collective-permute-start(bf16[128,4096]{0,1:T(8,128)(2,1)} %dynamic-slice_bitcast_fusion.1), channel_id=1, source_target_pairs={{0,16},{4,20},{8,24},{12,28},{16,0},{20,4},{24,8},{28,12},{1,17},{... | collective-permute-start | bytes 3145736 | tf_op jit(solution)/shard_map/ppermute | solution.py:562
  426.7 28.4 %collective-permute-start.27 = (bf16[1024,128]{1,0:T(8,128)(2,1)S(1)}, bf16[1024,128]{1,0:T(8,128)(2,1)}, u32[]{:S(2)}, u32[]{:S(2)}) collective-permute-start(bf16[1024,128]{1,0:T(8,128)(2,1)S(1)} %dynamic-slice_bitcast_fusion.4), channel_id=1, source_target_pairs={{0,16},{4,20},{8,24},{12,28},{16,0},{20,4},{24,8},{28,12},{1,17},{... | collective-permute-start | bytes 786440 | tf_op jit(solution)/shard_map/ppermute | solution.py:562
  433.7 21.3 %collective-permute-start.22 = (f32[1024]{0:T(1024)S(1)}, f32[1024]{0:T(1024)S(1)}, u32[]{:S(2)}, u32[]{:S(2)}) collective-permute-start(f32[1024]{0:T(1024)S(1)} %pad_maximum_fusion.4), channel_id=1, source_target_pairs={{0,4},{4,0},{8,12},{12,8},{16,20},{20,16},{24,28},{28,24},{1,5},{5... | collective-permute-start | bytes 12296 | tf_op jit(solution)/shard_map/ppermute | solution.py:562
  453.3 10.4 %collective-permute-start.35 = (bf16[128,2,1024]{0,2,1:T(8,128)(2,1)S(1)}, bf16[128,2,1024]{0,2,1:T(8,128)(2,1)S(1)}, u32[]{:S(2)}, u32[]{:S(2)}) collective-permute-start(bf16[128,2,1024]{0,2,1:T(8,128)(2,1)S(1)} %slice_bitcast_fusion.1), channel_id=1, source_target_pairs={{0,2},{1,3},{2,0},{3,1},{4,6},{5,7},{6,4},{7,5},{8,10},{9,11},{10,... | collective-permute-start | bytes 1572872 | tf_op jit(solution)/shard_map/ppermute | solution.py:562
  458.7 4.5 collective-permute-start.24
  (36 other events, 427.1 us)
Sparse Core Ops, SparseCore 0:
  46.5 74.8 all-gather.1

commit v2 on v1

--- a/solution.py
+++ b/solution.py
@@ -54,10 +54,27 @@
     return lax.broadcasted_iota(jnp.int32, shape, 1) // HD
 
 
+def ordered(kernel, count):
+    return lambda ids, *refs: kernel(ids, *refs[count:])
+
+
+def waits(after):
+    return [pl.BlockSpec(memory_space=pl.ANY)] * len(after)
+
+
 def row_stats(rows):
     mean = jnp.sum(rows, axis=1, keepdims=True) / D
     square = jnp.sum(rows * rows, axis=1, keepdims=True) / D
     return mean, lax.rsqrt(square - mean * mean + EPS)
+
+
+def piece(ids, j, bit, chunk):
+    inner = bit * chunk
+    mine = lax.rem(ids[1 + NB] // bit, 2)
+    base = (j * 128) // inner * (2 * inner) + (j * 128) % inner
+    return [
+        pl.ds(pl.multiple_of(base + side * inner, 128), 128) for side in (mine, 1 - mine)
+    ]
 
 
 def split_store(keep_ref, send_ref, value_ref, core):
@@ -69,43 +86,111 @@
         )
 
 
+TAIL = 3
+
+
+def place():
+    t = lax.axis_index("tensor")
+    core, y = lax.rem(t, 2), lax.div(t, 2)
+    return core, y, (t, 2 * y + 1 - core, 2 * (1 - y) + core, 2 * (1 - y) + 1 - core)
+
+
 def fwd_kernel(
-    ids, x0, x1, x2, x3, vec, wq, wk, wv, bqv, wd, lo, pad, alibi,
-    p_ref, q_ref, k_ref, v_ref, linv_ref, ctx_ref, keep_ref, send_ref, hm_ref,
+    x_any, x_own, vec, wq, wk, wv, bqv, wd, lo, pad, alibi,
+    p_ref, q_ref, k_ref, v_ref, linv_ref, ctx_ref, a_ref, b_ref, x1_ref, x2_ref, x3_ref, hm_ref,
     xs, qm_s, k_s, va_s, u_s, res_s, lo_s,
+    xc, xy, xf, part_keep, part_send, part_got, sum_keep, sum_send, sum_got, whole_own, whole_got,
+    s_xc, r_xc, s_xy, r_xy, s_xf, r_xf, s_pc, r_pc, s_sy, r_sy, s_wc, r_wc,
 ):
-    b = pl.program_id(0)
-    t = ids[0]
-    core = lax.rem(t, 2)
-    for r, x in enumerate((x0, x1, x2, x3)):
-        xs[:, feature_block(t ^ r)] = x[...].astype(F32)
-    rows = xs[...]
-    mean, rstd = row_stats(rows)
-    n1 = ((rows - mean) * rstd * vec[0:1, :] + vec[1:2, :]).astype(BF)
-    q = (dot(n1, wq[...]) + bqv[0:1, :]).astype(BF)
-    k = dot(n1, wk[...]).astype(BF)
-    v = (dot(n1, wv[...]) + bqv[1:2, :]).astype(BF)
-    qs = q * jnp.asarray(1.0 / math.sqrt(HD), BF)
-    q_ref[...] = qs
-    k_ref[...] = k
-    v_ref[...] = v
-    here = pl.ds(pl.multiple_of(b * B, B), B)
-    k_s[here, :] = k
-    lanes = head_of_lane((B, SHARE))
-    for h in range(LH):
-        qm_s[h] = jnp.where(lanes == h, qs, jnp.zeros_like(qs))
-        va_s[h, here, :] = jnp.where(lanes == h, v, jnp.ones_like(v))
-    lo_s[...] = jnp.broadcast_to(lo[...], (B, B))
-
-    @pl.when(b == 0)
-    def _():
+    step = pl.program_id(0)
+    core, y, ranks = place()
+
+    def rows(b):
+        return pl.ds(pl.multiple_of(b * B, B), B)
+
+    def remote(src, dst, send, got, rank):
+        return pltpu.make_async_remote_copy(
+            src_ref=src, dst_ref=dst, send_sem=send, recv_sem=got,
+            device_id={"tensor": rank}, device_id_type=pl.DeviceIdType.MESH,
+        )
+
+    def to_core(b):
+        return remote(x_any.at[rows(b)], xc.at[b], s_xc.at[b], r_xc.at[b], ranks[1])
+
+    def to_y(b):
+        return remote(x_any.at[rows(b)], xy.at[b], s_xy.at[b], r_xy.at[b], ranks[2])
+
+    def forward(b):
+        return remote(xy.at[b], xf.at[b], s_xf.at[b], r_xf.at[b], ranks[1])
+
+    def part_to_core(b):
+        return remote(part_send.at[b], part_got.at[b], s_pc.at[b], r_pc.at[b], ranks[1])
+
+    def sum_to_y(j):
+        return remote(sum_send.at[j], sum_got.at[j], s_sy.at[j], r_sy.at[j], ranks[2])
+
+    def whole_to_core(j):
+        return remote(whole_own.at[j], whole_got.at[j], s_wc.at[j], r_wc.at[j], ranks[1])
+
+    @pl.when(step == 0)
+    def _():
+        barrier = pltpu.get_barrier_semaphore()
+        for rank in (ranks[1], ranks[2]):
+            pl.semaphore_signal(
+                barrier, inc=1, device_id={"tensor": rank}, device_id_type=pl.DeviceIdType.MESH
+            )
+        pl.semaphore_wait(barrier, 2)
+        for b in range(3):
+            to_y(b).start()
+            to_core(b).start()
+        to_y(0).wait_recv()
+        forward(0).start()
         hm_ref[...] = jnp.full(hm_ref.shape, NEG, F32)
+
+    for b in range(3, NB):
+
+        @pl.when(step == b - 2)
+        def _():
+            to_y(b).start()
+            to_core(b).start()
 
     row_i = lax.broadcasted_iota(jnp.int32, (B, B), 0)
     col_i = lax.broadcasted_iota(jnp.int32, (B, B), 1)
+    lanes = head_of_lane((B, SHARE))
+
+    @pl.when(step < NB - 1)
+    def _():
+        to_y(step + 1).wait_recv()
+        forward(step + 1).start()
+
+    @pl.when(step < NB)
+    def _():
+        to_core(step).wait_recv()
+        forward(step).wait_recv()
+        blocks = (x_own[...], xc[step], xy[step], xf[step])
+        for rank, block, ref in zip(ranks, blocks, (None, x1_ref, x2_ref, x3_ref)):
+            xs[:, feature_block(rank)] = block.astype(F32)
+            if ref is not None:
+                ref[...] = block
+        value = xs[...]
+        mean, rstd = row_stats(value)
+        n1 = ((value - mean) * rstd * vec[0:1, :] + vec[1:2, :]).astype(BF)
+        q = (dot(n1, wq[...]) + bqv[0:1, :]).astype(BF)
+        k = dot(n1, wk[...]).astype(BF)
+        v = (dot(n1, wv[...]) + bqv[1:2, :]).astype(BF)
+        qs = q * jnp.asarray(1.0 / math.sqrt(HD), BF)
+        q_ref[...] = qs
+        k_ref[...] = k
+        v_ref[...] = v
+        here = rows(step)
+        k_s[here, :] = k
+        for h in range(LH):
+            qm_s[h] = jnp.where(lanes == h, qs, jnp.zeros_like(qs))
+            va_s[h, here, :] = jnp.where(lanes == h, v, jnp.ones_like(v))
+        lo_s[...] = jnp.broadcast_to(lo[...], (B, B))
 
     def attend(nb):
-        start = pl.multiple_of((b + 1 - nb) * B, B)
+        start = pl.multiple_of((step + 1 - nb) * B, B)
 
         def head(h, carry):
             qm = qm_s[h]
@@ -137,73 +222,122 @@
 
         lax.fori_loop(0, LH, head, 0)
 
-    count = b - ids[1 + b] + 1
-    for nb in range(1, SLOTS + 1):
-        pl.when(count == nb)(functools.partial(attend, nb))
-
-    ctx = res_s[0]
-    total = res_s[LH - 1]
-    for h in range(1, LH):
-        ctx = jnp.where(lanes == h, res_s[h], ctx)
-        total = jnp.where(lanes == h, res_s[h - 1], total)
-    inv = 1.0 / pltpu.roll(total, SHARE - HD, 1)
-    linv_ref[...] = inv
-    ctx = (ctx * inv).astype(BF)
-    ctx_ref[...] = ctx
-    xs[...] = dot(ctx, wd[...])
-    split_store(keep_ref, send_ref, xs, core)
-
-
-def attention_forward(ids, xs, vec, wq, wk, wv, bqv, wd, lo, pad, alibi):
-    row = lambda width: pl.BlockSpec((B, width), lambda b, ids: (b, 0))
-    whole = lambda shape: pl.BlockSpec(shape, lambda b, ids: (0,) * len(shape))
+    for nb in range(1, SLOTS):
+        pl.when(step == nb - 1)(functools.partial(attend, nb))
+    pl.when((step >= SLOTS - 1) & (step < NB))(functools.partial(attend, SLOTS))
+
+    @pl.when(step < NB)
+    def _():
+        ctx = res_s[0]
+        total = res_s[LH - 1]
+        for h in range(1, LH):
+            ctx = jnp.where(lanes == h, res_s[h], ctx)
+            total = jnp.where(lanes == h, res_s[h - 1], total)
+        inv = 1.0 / pltpu.roll(total, SHARE - HD, 1)
+        linv_ref[...] = inv
+        ctx = (ctx * inv).astype(BF)
+        ctx_ref[...] = ctx
+        xs[...] = dot(ctx, wd[...])
+        split_store(part_keep.at[step], part_send.at[step], xs, core)
+        part_to_core(step).start()
+
+    @pl.when((step >= 1) & (step <= NB))
+    def _():
+        b = step - 1
+        j = b // 2
+        part_to_core(b).wait_recv()
+        total = part_keep[b].astype(F32) + part_got[b].astype(F32)
+
+        @pl.when(lax.rem(b, 2) == y)
+        def _():
+            sum_keep[j] = total
+
+        @pl.when(lax.rem(b, 2) != y)
+        def _():
+            sum_send[j] = total.astype(BF)
+            sum_to_y(j).start()
+
+    @pl.when((step >= TAIL) & (lax.rem(step + NB - TAIL, 2) == y))
+    def _():
+        j = (step - TAIL) // 2
+        sum_to_y(j).wait_recv()
+        total = (sum_keep[j] + sum_got[j].astype(F32)).astype(BF)
+        whole_own[j] = total
+        a_ref[rows(j), :] = total
+        whole_to_core(j).start()
+
+    @pl.when(step == NB + TAIL - 1)
+    def _():
+        for j in range(NB // 2):
+            whole_to_core(j).wait_recv()
+            b_ref[rows(j), :] = whole_got[j]
+        for b in range(NB):
+            to_core(b).wait_send()
+            to_y(b).wait_send()
+            forward(b).wait_send()
+            part_to_core(b).wait_send()
+        for j in range(NB // 2):
+            sum_to_y(j).wait_send()
+            whole_to_core(j).wait_send()
+
+
+def attention_forward(x, vec, wq, wk, wv, bqv, wd, lo, pad, alibi):
+    last = lambda s: jnp.minimum(s, NB - 1)
+    row = lambda width: pl.BlockSpec((B, width), lambda s: (last(s), 0))
+    whole = lambda shape: pl.BlockSpec(shape, lambda s: (0,) * len(shape))
+    like = jax.ShapeDtypeStruct
+    dma = lambda n: pltpu.SemaphoreType.DMA((n,))
+    half = NB // 2
     return pl.pallas_call(
         fwd_kernel,
-        grid_spec=pltpu.PrefetchScalarGridSpec(
-            num_scalar_prefetch=1,
-            grid=(NB,),
-            in_specs=[row(SHARE)] * 4
-            + [whole((8, D))]
-            + [whole((D, SHARE))] * 3
-            + [whole((8, SHARE)), whole((SHARE, D)), row(1), whole((8, SEQ)), whole((8, STRIP))],
-            out_specs=[
-                pl.BlockSpec((LH, B, STRIP), lambda b, ids: (0, b, 0)),
-                row(SHARE), row(SHARE), row(SHARE), row(SHARE), row(SHARE), row(D // 2), row(D // 2),
-                whole((LH, 8, B)),
-            ],
-            scratch_shapes=[
-                pltpu.VMEM((B, D), F32),
-                pltpu.VMEM((LH, B, SHARE), BF),
-                pltpu.VMEM((SEQ, SHARE), BF),
-                pltpu.VMEM((LH, SEQ, SHARE), BF),
-                pltpu.VMEM((B, STRIP), F32),
-                pltpu.VMEM((LH, B, SHARE), F32),
-                pltpu.VMEM((B, B), jnp.int32),
-            ],
+        grid=(NB + TAIL,),
+        in_specs=[pl.BlockSpec(memory_space=pl.ANY), row(SHARE), whole((8, D))]
+        + [whole((D, SHARE))] * 3
+        + [whole((8, SHARE)), whole((SHARE, D)), row(1), whole((8, SEQ)), whole((8, STRIP))],
+        out_specs=[pl.BlockSpec((LH, B, STRIP), lambda s: (0, last(s), 0))]
+        + [row(SHARE)] * 5
+        + [whole((OWN, D // 2))] * 2
+        + [row(SHARE)] * 3
+        + [whole((LH, 8, B))],
+        scratch_shapes=[
+            pltpu.VMEM((B, D), F32),
+            pltpu.VMEM((LH, B, SHARE), BF),
+            pltpu.VMEM((SEQ, SHARE), BF),
+            pltpu.VMEM((LH, SEQ, SHARE), BF),
+            pltpu.VMEM((B, STRIP), F32),
+            pltpu.VMEM((LH, B, SHARE), F32),
+            pltpu.VMEM((B, B), jnp.int32),
+        ]
+        + [pltpu.VMEM((NB, B, SHARE), BF)] * 3
+        + [pltpu.VMEM((NB, B, D // 2), BF)] * 3
+        + [pltpu.VMEM((half, B, D // 2), F32)]
+        + [pltpu.VMEM((half, B, D // 2), BF)] * 4
+        + [dma(NB)] * 8
+        + [dma(half)] * 4,
+        out_shape=[like((LH, SEQ, STRIP), BF)]
+        + [like((SEQ, SHARE), BF)] * 3
+        + [like((SEQ, SHARE), F32), like((SEQ, SHARE), BF)]
+        + [like((OWN, D // 2), BF)] * 2
+        + [like((SEQ, SHARE), BF)] * 3
+        + [like((LH, 8, B), F32)],
+        compiler_params=pltpu.CompilerParams(
+            dimension_semantics=("arbitrary",),
+            vmem_limit_bytes=VMEM_LIMIT,
+            collective_id=0,
+            has_side_effects=True,
         ),
-        out_shape=[
-            jax.ShapeDtypeStruct((LH, SEQ, STRIP), BF),
-            jax.ShapeDtypeStruct((SEQ, SHARE), BF),
-            jax.ShapeDtypeStruct((SEQ, SHARE), BF),
-            jax.ShapeDtypeStruct((SEQ, SHARE), BF),
-            jax.ShapeDtypeStruct((SEQ, SHARE), F32),
-            jax.ShapeDtypeStruct((SEQ, SHARE), BF),
-            jax.ShapeDtypeStruct((SEQ, D // 2), BF),
-            jax.ShapeDtypeStruct((SEQ, D // 2), BF),
-            jax.ShapeDtypeStruct((LH, 8, B), F32),
-        ],
-        compiler_params=params(),
         cost_estimate=pl.CostEstimate(
             flops=16 * 10**9, bytes_accessed=40 * 2**20, transcendentals=8 * 10**6
         ),
         name="attention_forward",
-    )(ids, *xs, vec, wq, wk, wv, bqv, wd, lo, pad, alibi)
+    )(x, x, vec, wq, wk, wv, bqv, wd, lo, pad, alibi)
 
 
 def mlp_kernel(
     ids, a_own, a_par, x0, x1, x2, x3, d0, d1, d2, d3, vec, bup, wu0, wu1, wd0, wd1,
-    mk_ref, ms_ref, gn_ref, h1_ref, gu_ref, gd_ref, bs_ref,
+    mk_ref, ms_ref, gn_ref, h1_ref, gu_ref, su_ref, gd_ref, sd_ref, bs_ref,
     n2_s, n2t_s, dy_s, dyt_s, am_s, ag_s, act_s, gp_s,
+    *, bits, chunk,
 ):
     i = pl.program_id(0)
     t = ids[0]
@@ -256,13 +390,17 @@
         sums = lax.fori_loop(0, OWN // B, rows_of, jnp.zeros((1, TILE), F32))
         bs_ref[...] = jnp.broadcast_to(sums, bs_ref.shape)
 
-        def grads(fb, carry):
-            rows = pl.ds(pl.multiple_of(fb * B, B), B)
-            gu_ref[rows, :] = dot(n2t_s[rows, :], gp_s[...]).astype(gu_ref.dtype)
-            gd_ref[rows, :] = dot(dyt_s[rows, :], act_s[...]).astype(gd_ref.dtype)
+        def grads(j, carry):
+            to = pl.ds(pl.multiple_of(j * 128, 128), 128)
+            for bit, left, right, keep, send in (
+                (bits[0], n2t_s, gp_s, gu_ref, su_ref),
+                (bits[1], dyt_s, act_s, gd_ref, sd_ref),
+            ):
+                for ref, rows in zip((keep, send), piece(ids, j, bit, chunk)):
+                    ref[to, :] = dot(left[rows, :], right[...]).astype(ref.dtype)
             return carry
 
-        lax.fori_loop(0, D // B, grads, 0)
+        lax.fori_loop(0, D // 256, grads, 0)
 
     pl.when(i < 2)(lambda: tile(wu0, wd0, 0))
     pl.when(i >= 2)(lambda: tile(wu1, wd1, 1))
@@ -273,13 +411,13 @@
         gn_ref[...] = ag_s[...].astype(BF)
 
 
-def feed_forward(ids, a_own, a_par, xs, ds, vec, bup, wu0, wu1, wd0, wd1):
+def feed_forward(ids, a_own, a_par, xs, ds, vec, bup, wu0, wd0, w_other, bits, chunk):
     whole = lambda shape: pl.BlockSpec(shape, lambda i, ids: (0,) * len(shape))
     low = lambda i: jnp.minimum(i, 1)
     high = lambda i: jnp.maximum(i - 2, 0)
     xs = [x.reshape(NB // 2, 2, B, SHARE) for x in xs]
     return pl.pallas_call(
-        mlp_kernel,
+        functools.partial(mlp_kernel, bits=bits, chunk=chunk),
         grid_spec=pltpu.PrefetchScalarGridSpec(
             num_scalar_prefetch=1,
             grid=(4,),
@@ -292,15 +430,17 @@
                 pl.BlockSpec((D, TILE), lambda i, ids: (0, low(i))),
                 pl.BlockSpec((D, TILE), lambda i, ids: (0, high(i))),
                 pl.BlockSpec((TILE, D), lambda i, ids: (low(i), 0)),
-                pl.BlockSpec((TILE, D), lambda i, ids: (high(i), 0)),
+                pl.BlockSpec((TILE, D), lambda i, ids: (high(i), 1)),
             ],
             out_specs=[
                 whole((OWN, D // 2)),
                 whole((OWN, D // 2)),
                 whole((OWN, D)),
                 whole((OWN, D)),
-                pl.BlockSpec((D, TILE), lambda i, ids: (0, i)),
-                pl.BlockSpec((D, TILE), lambda i, ids: (0, i)),
+                pl.BlockSpec((D // 2, TILE), lambda i, ids: (0, i)),
+                pl.BlockSpec((D // 2, TILE), lambda i, ids: (0, i)),
+                pl.BlockSpec((D // 2, TILE), lambda i, ids: (0, i)),
+                pl.BlockSpec((D // 2, TILE), lambda i, ids: (0, i)),
                 pl.BlockSpec((8, TILE), lambda i, ids: (0, i)),
             ],
             scratch_shapes=[
@@ -319,8 +459,10 @@
             jax.ShapeDtypeStruct((OWN, D // 2), BF),
             jax.ShapeDtypeStruct((OWN, D), BF),
             jax.ShapeDtypeStruct((OWN, D), F32),
-            jax.ShapeDtypeStruct((D, 2 * UNITS), BF),
-            jax.ShapeDtypeStruct((D, 2 * UNITS), BF),
+            jax.ShapeDtypeStruct((D // 2, 2 * UNITS), BF),
+            jax.ShapeDtypeStruct((D // 2, 2 * UNITS), BF),
+            jax.ShapeDtypeStruct((D // 2, 2 * UNITS), BF),
+            jax.ShapeDtypeStruct((D // 2, 2 * UNITS), BF),
             jax.ShapeDtypeStruct((8, 2 * UNITS), F32),
         ],
         compiler_params=params(),
@@ -328,7 +470,7 @@
             flops=26 * 10**9, bytes_accessed=40 * 2**20, transcendentals=2 * 10**6
         ),
         name="feed_forward",
-    )(ids, a_own, a_par, *xs, *ds, vec, bup, wu0, wu1, wd0, wd1)
+    )(ids, a_own, a_par, *xs, *ds, vec, bup, wu0, w_other, wd0, w_other)
 
 
 def mid_kernel(
@@ -397,8 +539,9 @@
 
 def bwd_kernel(
     ids, x0, x1, x2, x3, gh, ga, gb, p_ref, q_ref, linv_ref, ctx_ref, k_ref, v_ref, vec, wq, wk, wv, wd,
-    keep_ref, send_ref, st_ref, ghx_ref, gw_ref, bs_ref,
+    f0, f1, f2, f3, st_ref, ghx_ref, ka_ref, sa_ref, kb_ref, sb_ref, bs_ref,
     xs, gh_s, gm_s, gt_s, qt_s, dl_s, ds_s, res_s, dkt_s, dvt_s, acc_s,
+    *, bits, chunk,
 ):
     i = pl.program_id(0)
     b = NB - 1 - i
@@ -480,14 +623,16 @@
     mean, rstd = row_stats(rows)
     xhat = (rows - mean) * rstd
     n1 = (xhat * vec[0:1, :] + vec[1:2, :]).astype(BF)
-    acc_s[0:SHARE, :] += dot(dq.T, n1)
-    acc_s[SHARE : 2 * SHARE, :] += dot(dkt, n1)
-    acc_s[2 * SHARE : 3 * SHARE, :] += dot(dvt, n1)
-    acc_s[3 * SHARE :, :] += dot(ctx.T, ghl)
+    n1t = n1.T
+    acc_s[:, 0:SHARE] += dot(n1t, dq)
+    acc_s[:, SHARE : 2 * SHARE] += dot(n1t, dk)
+    acc_s[:, 2 * SHARE : 3 * SHARE] += dot(n1t, dv)
+    acc_s[:, 3 * SHARE :] += dot(ghl.T, ctx)
 
     grad = dot_nt(dq, wq[...]) + dot_nt(dk, wk[...]) + dot_nt(dv, wv[...])
     xs[...] = grad
-    split_store(keep_ref, send_ref, xs, core)
+    for r, ref in enumerate((f0, f1, f2, f3)):
+        ref[...] = xs[:, feature_block(t ^ r)].astype(BF)
     scaled = grad * vec[0:1, :]
     first = jnp.sum(scaled, axis=1, keepdims=True)
     second = jnp.sum(scaled * xhat, axis=1, keepdims=True)
@@ -499,19 +644,29 @@
 
     @pl.when(i == NB - 1)
     def _():
-        gw_ref[...] = acc_s[...].astype(BF)
-
-
-def attention_backward(ids, xs, gh, ga, gb, p, q, linv, ctx, k, v, vec, wq, wk, wv, wd):
+        for j in range(D // 256):
+            to = slice(j * 128, (j + 1) * 128)
+            for bit, keep, send, cols in (
+                (bits[0], ka_ref, sa_ref, slice(0, 2 * SHARE)),
+                (bits[1], kb_ref, sb_ref, slice(2 * SHARE, 4 * SHARE)),
+            ):
+                for ref, rows in zip((keep, send), piece(ids, j, bit, chunk)):
+                    ref[to, :] = acc_s[rows, cols].astype(BF)
+
+
+def attention_backward(
+    ids, xs, gh, ga, gb, p, q, linv, ctx, k, v, vec, wq, wk, wv, wd, bits, chunk, after
+):
     row = lambda width: pl.BlockSpec((B, width), lambda i, ids: (NB - 1 - i, 0))
     own = lambda width: pl.BlockSpec((B, width), lambda i, ids: ((NB - 1 - i) // 2, 0))
     whole = lambda shape: pl.BlockSpec(shape, lambda i, ids: (0,) * len(shape))
     return pl.pallas_call(
-        bwd_kernel,
+        ordered(functools.partial(bwd_kernel, bits=bits, chunk=chunk), len(after)),
         grid_spec=pltpu.PrefetchScalarGridSpec(
             num_scalar_prefetch=1,
             grid=(NB,),
-            in_specs=[row(SHARE)] * 4
+            in_specs=waits(after)
+            + [row(SHARE)] * 4
             + [own(D), own(D // 2), own(D // 2)]
             + [pl.BlockSpec((LH, B, STRIP), lambda i, ids: (0, NB - 1 - i, 0))]
             + [row(SHARE)] * 3
@@ -520,11 +675,16 @@
             + [whole((D, SHARE))] * 3
             + [whole((SHARE, D))],
             out_specs=[
-                row(D // 2),
-                row(D // 2),
+                row(SHARE),
+                row(SHARE),
+                row(SHARE),
+                row(SHARE),
                 pl.BlockSpec((8, B), lambda i, ids: (0, NB - 1 - i)),
                 row(SHARE),
-                whole((D, D)),
+                whole((D // 2, 2 * SHARE)),
+                whole((D // 2, 2 * SHARE)),
+                whole((D // 2, 2 * SHARE)),
+                whole((D // 2, 2 * SHARE)),
                 whole((8, SHARE)),
             ],
             scratch_shapes=[
@@ -538,15 +698,20 @@
                 pltpu.VMEM((LH, B, SHARE), F32),
                 pltpu.VMEM((LH, HD, SEQ), F32),
                 pltpu.VMEM((LH, HD, SEQ), F32),
-                pltpu.VMEM((4 * SHARE, D), F32),
+                pltpu.VMEM((D, 4 * SHARE), F32),
             ],
         ),
         out_shape=[
-            jax.ShapeDtypeStruct((SEQ, D // 2), BF),
-            jax.ShapeDtypeStruct((SEQ, D // 2), BF),
+            jax.ShapeDtypeStruct((SEQ, SHARE), BF),
+            jax.ShapeDtypeStruct((SEQ, SHARE), BF),
+            jax.ShapeDtypeStruct((SEQ, SHARE), BF),
+            jax.ShapeDtypeStruct((SEQ, SHARE), BF),
             jax.ShapeDtypeStruct((8, SEQ), F32),
             jax.ShapeDtypeStruct((SEQ, SHARE), BF),
-            jax.ShapeDtypeStruct((4 * SHARE, D), BF),
+            jax.ShapeDtypeStruct((D // 2, 2 * SHARE), BF),
+            jax.ShapeDtypeStruct((D // 2, 2 * SHARE), BF),
+            jax.ShapeDtypeStruct((D // 2, 2 * SHARE), BF),
+            jax.ShapeDtypeStruct((D // 2, 2 * SHARE), BF),
             jax.ShapeDtypeStruct((8, SHARE), F32),
         ],
         compiler_params=params(),
@@ -554,7 +719,7 @@
             flops=30 * 10**9, bytes_accessed=50 * 2**20, transcendentals=0
         ),
         name="attention_backward",
-    )(ids, *xs, gh, ga, gb, p, q, linv, ctx, k, v, vec, wq, wk, wv, wd)
+    )(ids, *after, *xs, gh, ga, gb, p, q, linv, ctx, k, v, vec, wq, wk, wv, wd)
 
 
 def swap(value, axis, bit):
@@ -580,20 +745,58 @@
     return lax.dynamic_index_in_dim(value, index, axis, keepdims=False)
 
 
-def dp_scatter(value, order):
+def sum_kernel(bit, km, rm, ko, ro, keep_ref, send_ref):
+    for a, b, ref in ((km, rm, keep_ref), (ko, ro, send_ref)):
+        ref[...] = (a[...].astype(F32) + b[...].astype(F32)).astype(ref.dtype)
+
+
+def sum_and_split(bit, keep, other, inner, after=()):
+    rows, cols = keep.shape
+    step = min(inner, 128)
+    per = inner // step
+    block = lambda side: pl.BlockSpec(
+        (step, cols),
+        lambda i, bit: (i // per * 2 * per + (bit[0] if side else 1 - bit[0]) * per + i % per, 0),
+    )
+    out = pl.BlockSpec((step, cols), lambda i, bit: (i, 0))
+    return pl.pallas_call(
+        ordered(sum_kernel, len(after)),
+        grid_spec=pltpu.PrefetchScalarGridSpec(
+            num_scalar_prefetch=1,
+            grid=(rows // 2 // step,),
+            in_specs=waits(after) + [block(True), block(True), block(False), block(False)],
+            out_specs=[out, out],
+        ),
+        out_shape=[jax.ShapeDtypeStruct((rows // 2, cols), BF)] * 2,
+        compiler_params=params(),
+        cost_estimate=pl.CostEstimate(flops=rows * cols, bytes_accessed=6 * rows * cols, transcendentals=0),
+        name="sum_and_split",
+    )(bit, *after, keep, other, keep, other)
+
+
+def dp_scatter(keep, send, order, after=()):
     rank = lax.axis_index("dp")
-    size = lax.axis_size("dp")
-    levels = len(dp_bits())
-    rest = value.shape[1:]
-    value = value.reshape((2,) * levels + rest)
-    left = list(reversed(dp_bits()))
-    for bit in order:
-        axis = left.index(bit)
-        left.pop(axis)
-        mine = (rank // bit) % 2
-        other = swap(pick(value, axis, 1 - mine), "dp", bit)
-        value = (pick(value, axis, mine).astype(F32) + other.astype(F32)).astype(BF)
-    return value.reshape(rest)
+    chunk = D // lax.axis_size("dp")
+    for n, bit in enumerate(order):
+        other = swap(send, "dp", bit)
+        if n == len(order) - 1:
+            yield keep.astype(F32) + other.astype(F32)
+            return
+        following = order[n + 1]
+        inner = chunk
+        for b in order[n + 2 :]:
+            inner *= 2 if b < following else 1
+        wait = yield send
+        mine = ((rank // following) % 2)[None]
+        keep, send = sum_and_split(mine, keep, other, inner, wait or ())
+
+
+def finish(steps, after=()):
+    try:
+        while True:
+            value = steps.send(after)
+    except StopIteration:
+        return value
 
 
 def shards(
@@ -625,11 +828,6 @@
     y_swap = lambda value: swap(value, "tensor", 2)
     rows8 = lambda value: jnp.pad(value, ((0, 8 - value.shape[0]), (0, 0)))
 
-    x_own = tokens
-    x_y = y_swap(x_own)
-    x_core = core_swap(x_own)
-    x_far = core_swap(x_y)
-    xs = [x_own, x_core, x_y, x_far]
     vectors = jnp.stack([norm1_gain, norm1_bias, dense_bias, norm2_gain, norm2_bias, down_bias])
     vec = lax.dynamic_update_slice(jnp.zeros((6, D), BF), vectors, (0, t * SHARE))
     vec = vec + core_swap(vec)
@@ -639,7 +837,6 @@
     cut = lambda w: lax.dynamic_slice_in_dim(w, rank * part, part, 0)
     w_part = y_swap(jnp.concatenate([cut(w_up), cut(w_down)], axis=1))
     w_other = lax.all_gather(w_part, "dp", axis=0, tiled=True)
-    up_other, down_other = w_other[:, :UNITS], w_other[:, UNITS:]
     b_up_pair = jnp.stack([b_up, y_swap(b_up)]).astype(F32)
 
     seg = segments.reshape(SEQ)
@@ -648,32 +845,36 @@
     for value in range(1, 4):
         first = jnp.where(seg == value, jnp.sum((seg < value).astype(jnp.int32)), first)
     lowest = jnp.maximum(first, index - (WIN - 1))
-    ids = jnp.concatenate([t[None].astype(jnp.int32), lowest[::B] // B])
+    ids = jnp.concatenate(
+        [t[None].astype(jnp.int32), lowest[::B] // B, rank[None].astype(jnp.int32)]
+    )
     pad_row = rows8(jnp.where(padding.reshape(1, SEQ) == 1, 0.0, NEG).astype(F32))
     heads = t * LH + jnp.arange(LH)
     slopes = jnp.exp2(-8.0 * (heads.astype(F32) + 1.0) / HEADS)
     alibi = rows8(slopes[:, None] * (jnp.arange(STRIP) - (STRIP - 1)).astype(F32)[None, :])
 
-    p, q, k, v, linv, ctx, keep, send, hm = attention_forward(
-        ids, xs, vec, w_query, w_key, w_value,
-        rows8(jnp.stack([b_query, b_value]).astype(F32)), w_dense,
-        lowest.reshape(SEQ, 1), pad_row, alibi,
-    )
-
     by_y = lambda value, which: pick(value.reshape(NB // 2, 2, B, value.shape[-1]), 1, which).reshape(
         OWN, value.shape[-1]
     )
     d_own = by_y(out_grad, y)
-    d_y = y_swap(by_y(out_grad, 1 - y))
+    d_send = by_y(out_grad, 1 - y)
+
+    p, q, k, v, linv, ctx, a_own, a_par, x1, x2, x3, hm = attention_forward(
+        tokens, vec, w_query, w_key, w_value,
+        rows8(jnp.stack([b_query, b_value]).astype(F32)), w_dense,
+        lowest.reshape(SEQ, 1), pad_row, alibi,
+    )
+    xs = [tokens, x1, x2, x3]
+
+    d_y = y_swap(d_send)
     ds = [d_own, core_swap(d_own), d_y, core_swap(d_y)]
 
-    both = (keep.astype(F32) + core_swap(send).astype(F32)).astype(BF)
-    mine = by_y(both, y).astype(F32) + y_swap(by_y(both, 1 - y)).astype(F32)
-    a_own = mine.astype(BF)
-    a_par = core_swap(a_own)
-
-    mk, ms, gn, h1, gu, gd, bs = feed_forward(
-        ids, a_own, a_par, xs, ds, vec, rows8(b_up_pair), w_up, up_other, w_down, down_other
+    bits = dp_bits()
+    order_a = bits if size == 8 else bits[::-1]
+    order_b = [2, 4, 1] if size == 8 else [bits[-2], bits[-1], *bits[:-2][::-1]]
+    mk, ms, gn, h1, gu, su, gd, sd, bs = feed_forward(
+        ids, a_own, a_par, xs, ds, vec, rows8(b_up_pair), w_up, w_down, w_other,
+        (order_a[0], order_b[0]), part,
     )
     gr = core_swap(gn)
     mr = core_swap(ms)
@@ -685,18 +886,18 @@
     pair = jnp.stack([out_own, out_y]).reshape(2, NB // 2, B, SHARE)
     output = jnp.where(y == 0, pair, pair[::-1]).transpose(1, 0, 2, 3).reshape(SEQ, SHARE)
 
-    grads = jnp.concatenate([gu, gd], axis=1).reshape(size, D // size, 4 * UNITS)
-    bits = dp_bits()
-    grads = dp_scatter(grads, bits).reshape(D // size, 2, 2, UNITS)
-    grads = grads[:, :, 0].astype(F32) + y_swap(grads[:, :, 1]).astype(F32)
-    w_up_grad = grads[:, 0]
-    w_down_grad = grads[:, 1].T
-
-    keep, send, stats, ghx, gw, qv = attention_backward(
-        ids, xs, gh, ga, gb, p, q, linv, ctx, k, v, vec, w_query, w_key, w_value, w_dense
+    steps_u = dp_scatter(gu, su, order_a)
+    steps_d = dp_scatter(gd, sd, order_b)
+    next(steps_u), next(steps_d)
+    sent = (steps_u.send(()), steps_d.send(()))
+
+    f0, f1, f2, f3, stats, ghx, ka, sa, kb, sb, qv = attention_backward(
+        ids, xs, gh, ga, gb, p, q, linv, ctx, k, v, vec, w_query, w_key, w_value, w_dense,
+        (order_a[0], order_b[0]), part, sent,
     )
-    both = (keep.astype(F32) + core_swap(send).astype(F32)).astype(BF).reshape(SEQ, 2, SHARE)
-    g_first = pick(both, 1, y).astype(F32) + y_swap(pick(both, 1, 1 - y)).astype(F32)
+    add = lambda a, b: (a.astype(F32) + b.astype(F32)).astype(BF)
+    away = add(f2, core_swap(f3))
+    g_first = add(f0, core_swap(f1)).astype(F32) + y_swap(away).astype(F32)
     sums = stats[0:2]
     sums = sums + core_swap(sums)
     sums = sums + y_swap(sums)
@@ -706,21 +907,28 @@
     scaled = g_first * norm1_gain.astype(F32)[None, :]
     tokens_grad = ghx.astype(F32) + rstd * (scaled - first - xhat * second)
 
-    gw = gw.reshape(4 * SHARE, size, D // size).transpose(1, 0, 2)
-    gw = dp_scatter(gw, bits).astype(F32).reshape(4, SHARE, D // size)
-
-    local = jnp.max(hm, axis=(1, 2))
+    gu = finish(steps_u, (qv,))
+    gd = finish(steps_d, (qv,))
+    w_up_grad = gu[:, :UNITS] + y_swap(gu[:, UNITS:].astype(BF)).astype(F32)
+    w_down_grad = (gd[:, :UNITS] + y_swap(gd[:, UNITS:].astype(BF)).astype(F32)).T
+    steps_a = dp_scatter(ka, sa, order_a)
+    steps_b = dp_scatter(kb, sb, order_b)
+    next(steps_a), next(steps_b)
+    g_qk = finish(steps_a, ())
+    g_vd = finish(steps_b, ())
+
+    cs4 = pick(cs[0:4].reshape(4, 2, 2, SHARE), 2, core)
+    early = jnp.concatenate([pick(cs4, 1, y).reshape(-1), bs[0, :UNITS]])
+    apart = jnp.concatenate([pick(cs4, 1, 1 - y).reshape(-1), bs[0, UNITS:]])
+    early = early + y_swap(apart)
+    late = jnp.concatenate([jnp.sum(g_first * xhat, axis=0), jnp.sum(g_first, axis=0), qv[0], qv[1]])
+    packed = jnp.concatenate([early, late, jnp.pad(jnp.max(hm, axis=(1, 2)), (0, 124))])
+    summed = lax.broadcasted_iota(jnp.int32, packed.shape, 0) < packed.shape[0] - 128
     for bit in bits:
-        local = jnp.maximum(local, swap(local, "dp", bit))
-    head_max = local
-    cs4 = cs[0:4].reshape(4, 2, 2, SHARE)
-    cs4 = pick(cs4, 2, core)
-    early = jnp.concatenate([pick(cs4, 1, y).reshape(-1), bs[0, :UNITS]])
-    away = jnp.concatenate([pick(cs4, 1, 1 - y).reshape(-1), bs[0, UNITS:]])
-    early = dp_total(early + y_swap(away))
-    late = dp_total(
-        jnp.concatenate([jnp.sum(g_first * xhat, axis=0), jnp.sum(g_first, axis=0), qv[0], qv[1]])
-    )
+        other = swap(packed, "dp", bit)
+        packed = jnp.where(summed, packed + other, jnp.maximum(packed, other))
+    early, late, head_max = jnp.split(packed, (8 * SHARE, 12 * SHARE))
+    head_max = head_max[:LH]
     of = lambda value, n: value[n * SHARE : (n + 1) * SHARE]
 
     column_scale = jnp.repeat(jnp.sqrt(TAU / jnp.maximum(head_max, TAU)), HD)
@@ -729,12 +937,12 @@
         tokens_grad,
         of(late, 0),
         of(late, 1),
-        gw[0].T,
+        g_qk[:, :SHARE],
         of(late, 2),
-        gw[1].T,
-        gw[2].T,
+        g_qk[:, SHARE:],
+        g_vd[:, :SHARE],
         of(late, 3),
-        gw[3],
+        g_vd[:, SHARE:].T,
         of(early, 2),
         of(early, 0),
         of(early, 1),

time: 473 us -> 369 us (0.78)
  waiting for transfers between devices: 176 us -> 81.4 us
  Pallas kernels: 151 us -> 194 us
  local copies, waits for them, and re-layouts: 61.7 us -> 21.5 us
  other arithmetic: 37.8 us -> 19.7 us
  starting transfers between devices: 30.9 us -> 36.6 us
    ppermute x39 -> x35, waiting for transfers between devices: 176 us -> 81.3 us  [swap(): return lax.ppermute(value, axis, [(i, i ^ bit) for i in range(size)])]
    pallas_call x3 -> x11, Pallas kernels: 141 us -> 184 us  [the longest x1 69.5 us: attention_forward(): pl.pallas_call(fwd_kernel, grid=(NB + TAIL,), in_specs=[pl.BlockSpec(memo...]
    dynamic_slice x7 -> x2, local copies, waits for them, and re-layouts: 17.7 us -> 0.1 us  [pick(): return lax.dynamic_index_in_dim(value, index, axis, keepdims=False)]
    convert_element_type x9 -> x1, other arithmetic: 13.3 us -> 0.3 us  [shards(): add = lambda a, b: (a.astype(F32) + b.astype(F32)).astype(BF)]
    concatenate x4 -> x2, other arithmetic: 8.51 us -> 0.59 us  [the longest x1 0.59 us: shards(): jnp.concatenate([t[None].astype(jnp.int32), lowest[::B] // B, rank[None]....]
    ppermute x39 -> x35, starting transfers between devices: 30.9 us -> 36.5 us  [swap(): return lax.ppermute(value, axis, [(i, i ^ bit) for i in range(size)])]
    unnamed x61 -> x94, local copies, waits for them, and re-layouts: 15.4 us -> 10.3 us
    slice x6, local copies, waits for them, and re-layouts: 8.11 us -> 2.97 us  [the longest x1 1.34 us: shards(): qv[1]]
  transfers between devices with their start and end apart: 40 -> 36, of which waited for: 20 -> 13; matrix products, arithmetic and copies ran while one was open for 19% -> 7% of each run, Pallas kernels for 20% -> 39%
where the time goes in v2:
time: 369 us; the launch traced here: 368 us
  Pallas kernels  194 us (53%)
  waiting for transfers between devices  81.4 us (22%)
  starting transfers between devices  36.6 us (10%)
  local copies, waits for them, and re-layouts  21.5 us (6%)
  other arithmetic  19.7 us (5%)
  between operations  14.8 us (4%)
    ppermute x35, waiting for transfers between devices, swap(): return lax.ppermute(value, axis, [(i, i ^ bit) for i in range(size)])  81.3 us
    pallas_call x1, Pallas kernels, attention_forward(): pl.pallas_call(fwd_kernel, grid=(NB + TAIL,), in_specs=[pl.BlockSpec(memo...  69.5 us
    pallas_call x1, Pallas kernels, feed_forward(): pl.pallas_call(functools.partial(mlp_kernel, bits=bits, chunk=chunk), gri...  48.7 us
    pallas_call x1, Pallas kernels, attention_backward(): pl.pallas_call(ordered(functools.partial(bwd_kernel, bits=bits, chunk=chu...  46.3 us
    ppermute x35, starting transfers between devices, swap(): return lax.ppermute(value, axis, [(i, i ^ bit) for i in range(size)])  36.5 us
    pallas_call x8, Pallas kernels, sum_and_split(): pl.pallas_call(ordered(sum_kernel, len(after)), grid_spec=pltpu.PrefetchS...  19.9 us
    unnamed x94, local copies, waits for them, and re-layouts  10.3 us
    pallas_call x1, Pallas kernels, middle(): pl.pallas_call(mid_kernel, grid_spec=pltpu.PrefetchScalarGridSpec(num_sca...  9.66 us
  transfers between devices with their start and end apart: 36, of which 13 were waited for; matrix products, arithmetic and copies ran while one was open for 7% of the time, Pallas kernels for 39%

profile of v2, /device:TPU:0, one launch (start us, length us, event | category | flops | bytes accessed | tf_op | source)
XLA Modules:
  0.0 368.0 jit_solution(14438780843597306148)
XLA Ops:
  8.6 3.0 collective-permute-start.6
  11.6 11.9 %collective-permute-done.6 = bf16[128,2048]{1,0:T(8,128)(2,1)S(1)} collective-permute-done((bf16[128,2048]{1,0:T(8,128)(2,1)S(1)}, bf16[128,2048]{1,0:T(8,128)(2,1)S(1)}, u32[]{:S(2)}, u32[]{:S(2)}) %collective-permute-start.6) | collective-permute-done | bytes 524320 | tf_op jit(solution)/shard_map/ppermute | solution.py:727
  27.9 2.0 compare_select_fusion.3
  29.9 2.0 fusion.20
  38.4 2.9 collective-permute-done.1
  41.9 69.5 %attention_forward.1 = (bf16[4,2048,1280]{2,1,0:T(8,128)(2,1)}, bf16[2048,256]{1,0:T(8,128)(2,1)}, bf16[2048,256]{1,0:T(8,128)(2,1)}, bf16[2048,256]{1,0:T(8,128...) custom-call(bf16[2048,256]{1,0:T(8,128)(2,1)} %refs_2_.1, ...), custom_call_target="tpu_custom_call" | custom-call | flops 16000000000 | bytes 41943040 | tf_op jit(solution)/shard_map/attention_forward/pallas_call | solution.py:291
  112.4 48.7 %feed_forward.1 = (bf16[1024,512]{1,0:T(8,128)(2,1)}, bf16[1024,512]{1,0:T(8,128)(2,1)}, bf16[1024,1024]{1,0:T(8,128)(2,1)}, f32[1024,1024]{1,0:T(8,128)}, bf16[...) custom-call(s32[10]{0:T(128)} %pad_add_fusion.ids, ...), custom_call_target="tpu_custom_call" | custom-call | flops 25999998976 | bytes 41943040 | tf_op jit(solution)/shard_map/feed_forward/pallas_call | solution.py:419
  164.7 2.5 collective-permute-done.8.mr
  168.8 9.7 %second_norm_backward.1 = (bf16[1024,1024]{1,0:T(8,128)(2,1)}, bf16[1024,512]{1,0:T(8,128)(2,1)}, bf16[1024,256]{1,0:T(8,128)(2,1)}, bf16[1024,256]{1,0:T(8,128)(2,1)}, f32[8,1024]{1,0:T(8,128)}) custom-call(s32[10]{0:T(128)} %pad_add_fusion.ids, f32[1024,1024]{1,0:T(8,128)} %get-tuple-element.79.h1, bf16[1024,1024]{1,0:T(8,128)(2,1)} %get-tuple-element.80.gn, ...), custom_call_target="tpu_custom_call" | custom-call | flops 20971520 | bytes 16777216 | tf_op jit(solution)/shard_map/second_norm_backward/pallas_call | solution.py:518
  178.5 2.9 collective-permute-start.12
  181.4 24.1 %collective-permute-done.12.refs_7_ = bf16[1024,512]{1,0:T(8,128)(2,1)} collective-permute-done((bf16[1024,512]{1,0:T(8,128)(2,1)}, bf16[1024,512]{1,0:T(8,128)(2,1)}, u32[]{:S(2)}, u32[]{:S(2)}) %collective-permute-start.12) | collective-permute-done | bytes 1048608 | tf_op jit(solution)/shard_map/ppermute | solution.py:727
  210.4 3.3 sum_and_split.8
  216.7 3.4 sum_and_split.9
  220.0 2.5 collective-permute-start.32
  222.7 46.3 %attention_backward.1 = (bf16[2048,256]{1,0:T(8,128)(2,1)}, bf16[2048,256]{1,0:T(8,128)(2,1)}, bf16[2048,256]{1,0:T(8,128)(2,1)}, bf16[2048,256]{1,0:T(8,128)(2,...) custom-call(s32[10]{0:T(128)} %pad_add_fusion.ids, ...), custom_call_target="tpu_custom_call" | custom-call | flops 30000001024 | bytes 52428800 | tf_op jit(solution)/shard_map/attention_backward/pallas_call | solution.py:663
  274.1 2.7 sum_and_split.14
  276.9 2.5 collective-permute-start.18
  281.1 2.7 sum_and_split.15
  287.1 2.1 sum_and_split.10
  289.2 2.4 collective-permute-done.26.refs_1_.refs_3_
  292.3 2.1 sum_and_split.12
  294.4 8.7 %collective-permute-done.30 = bf16[128,2048]{1,0:T(8,128)(2,1)S(1)} collective-permute-done((bf16[128,2048]{1,0:T(8,128)(2,1)}, bf16[128,2048]{1,0:T(8,128)(2,1)S(1)}, u32[]{:S(2)}, u32[]{:S(2)}) %collective-permute-start.30) | collective-permute-done | bytes 524320 | tf_op jit(solution)/shard_map/ppermute | solution.py:727
  303.3 2.6 collective-permute-start.31
  306.5 2.1 collective-permute-start.16
  309.2 1.8 sum_and_split.11
  311.0 5.0 %collective-permute-done.27.refs_1_.refs_3_ = bf16[256,512]{1,0:T(8,128)(2,1)S(1)} collective-permute-done((bf16[256,512]{1,0:T(8,128)(2,1)}, bf16[256,512]{1,0:T(8,128)(2,1)S(1)}, u32[]{:S(2)}, u32[]{:S(2)}) %collective-permute-start.27) | collective-permute-done | bytes 262176 | tf_op jit(solution)/shard_map/ppermute | solution.py:727
  321.2 3.8 %collective-permute-done.25 = bf16[128,512]{1,0:T(8,128)(2,1)S(1)} collective-permute-done((bf16[128,512]{1,0:T(8,128)(2,1)}, bf16[128,512]{1,0:T(8,128)(2,1)S(1)}, u32[]{:S(2)}, u32[]{:S(2)}) %collective-permute-start.25) | collective-permute-done | bytes 131104 | tf_op jit(solution)/shard_map/ppermute | solution.py:727
  325.0 14.6 %collective-permute-done.16 = bf16[2048,256]{1,0:T(8,128)(2,1)} collective-permute-done((bf16[2048,256]{1,0:T(8,128)(2,1)S(1)}, bf16[2048,256]{1,0:T(8,128)(2,1)}, u32[]{:S(2)}, u32[]{:S(2)}) %collective-permute-start.16) | collective-permute-done | bytes 1048608 | tf_op jit(solution)/shard_map/ppermute | solution.py:727
  339.6 5.1 %fusion = (f32[256]{0:T(256)S(1)}, f32[256]{0:T(256)S(1)}, f32[2048,256]{1,0:T(8,128)}) fusion(bf16[2048,256]{1,0:T(8,128)(2,1)} %collective-permute-done.16, bf16[2048,256]{1,0:T(8,128)(2,1)} %collective-permute-done.14, bf16[2048,256]{1,0:T(8,128)(2,1)} %get-tuple-element.101, f32[2048]{0:T(1024)} %bitcast.48, f32[2048]{0:T(1024)} %bitcast.49, ...), kind=kLoop, calls=%fused_computation.6 | loop fusion | flops 10485248 | bytes 7375872 | tf_op jit(solution)/shard_map/reduce_sum | solution.py:924
  345.5 3.2 collective-permute-done.20
  348.7 1.9 collective-permute-start.21
  352.6 2.5 collective-permute-start.22
  (223 shorter events, 52.9 us)
Async XLA Ops:
  7.3 104.2 %all-gather.2.cloned.1.call-start = ((), (), s32[]{:S(2)}) async-start(), calls=%async_computation | async-start | bytes 4718592 | tf_op jit(solution)/shard_map/all_gather | solution.py:839
  8.6 15.0 %collective-permute-start.6 = (bf16[128,2048]{1,0:T(8,128)(2,1)S(1)}, bf16[128,2048]{1,0:T(8,128)(2,1)S(1)}, u32[]{:S(2)}, u32[]{:S(2)}) collective-permute-start(bf16[128,2048]{1,0:T(8,128)(2,1)S(1)} %pad_maximum_fusion.1), channel_id=1, source_target_pairs={{0,2},{1,3},{2,0},{3,1},{4,6},{5,7},{6,4},{7,5},{8,10},{9,11},{10,... | collective-permute-start | bytes 1572872 | tf_op jit(solution)/shard_map/ppermute | solution.py:727
  24.4 11.6 %collective-permute-start.5 = (bf16[1024]{0:T(1024)(128)(2,1)S(1)}, bf16[1024]{0:T(1024)(128)(2,1)S(1)}, u32[]{:S(2)}, u32[]{:S(2)}) collective-permute-start(bf16[1024]{0:T(1024)(128)(2,1)S(1)} %copy-done.30), channel_id=1, source_target_pairs={{0,2},{1,3},{2,0},{3,1},{4,6},{5,7},{6,4},{7,5},{8,10},{9,11},{10,... | collective-permute-start | bytes 6152 | tf_op jit(solution)/shard_map/ppermute | solution.py:727
  26.3 9.6 %collective-permute-start = (bf16[6,1024]{1,0:T(8,128)(2,1)S(1)}, bf16[6,1024]{1,0:T(8,128)(2,1)S(1)}, u32[]{:S(2)}, u32[]{:S(2)}) collective-permute-start(bf16[6,1024]{1,0:T(8,128)(2,1)S(1)} %constant_dynamic-update-slice_fusion.5), channel_id=1, source_target_pairs={{0,1},{1,0},{2,3},{3,2},{4,5},{5,4},{6,7},{7,6},{8,9},{9,8},{10,11... | collective-permute-start | bytes 36872 | tf_op jit(solution)/shard_map/ppermute | solution.py:727
  26.5 15.3 %collective-permute-start.3 = (bf16[1024,256]{1,0:T(8,128)(2,1)S(1)}, bf16[1024,256]{1,0:T(8,128)(2,1)S(1)}, u32[]{:S(2)}, u32[]{:S(2)}) collective-permute-start(bf16[1024,256]{1,0:T(8,128)(2,1)S(1)} %bitcast.46), channel_id=1, source_target_pairs={{0,2},{1,3},{2,0},{3,1},{4,6},{5,7},{6,4},{7,5},{8,10},{9,11},{10,... | collective-permute-start | bytes 1572872 | tf_op jit(solution)/shard_map/ppermute | solution.py:727
  26.9 84.5 %collective-permute-start.2 = (bf16[1024,256]{1,0:T(8,128)(2,1)S(1)}, bf16[1024,256]{1,0:T(8,128)(2,1)S(1)}, u32[]{:S(2)}, u32[]{:S(2)}) collective-permute-start(bf16[1024,256]{1,0:T(8,128)(2,1)S(1)} %bitcast.38), channel_id=1, source_target_pairs={{0,1},{1,0},{2,3},{3,2},{4,5},{5,4},{6,7},{7,6},{8,9},{9,8},{10,11... | collective-permute-start | bytes 1572872 | tf_op jit(solution)/shard_map/ppermute | solution.py:727
  41.9 69.6 %collective-permute-start.4 = (bf16[1024,256]{1,0:T(8,128)(2,1)S(1)}, bf16[1024,256]{1,0:T(8,128)(2,1)S(1)}, u32[]{:S(2)}, u32[]{:S(2)}) collective-permute-start(bf16[1024,256]{1,0:T(8,128)(2,1)S(1)} %collective-permute-done.3.d2), channel_id=1, source_target_pairs={{0,1},{1,0},{2,3},{3,2},{4,5},{5,4},{6,7},{7,6},{8,9},{9,8},{10,11... | collective-permute-start | bytes 1572872 | tf_op jit(solution)/shard_map/ppermute | solution.py:727
  161.2 6.0 %collective-permute-start.7 = (bf16[1024,1024]{1,0:T(8,128)(2,1)}, bf16[1024,1024]{1,0:T(8,128)(2,1)S(1)}, u32[]{:S(2)}, u32[]{:S(2)}) collective-permute-start(bf16[1024,1024]{1,0:T(8,128)(2,1)} %get-tuple-element.80.gn), channel_id=1, source_target_pairs={{0,1},{1,0},{2,3},{3,2},{4,5},{5,4},{6,7},{7,6},{8,9},{9,8},{10,11... | collective-permute-start | bytes 6291464 | tf_op jit(solution)/shard_map/ppermute | solution.py:727
  161.7 5.5 %collective-permute-start.8 = (bf16[1024,512]{1,0:T(8,128)(2,1)}, bf16[1024,512]{1,0:T(8,128)(2,1)S(1)}, u32[]{:S(2)}, u32[]{:S(2)}) collective-permute-start(bf16[1024,512]{1,0:T(8,128)(2,1)} %get-tuple-element.82), channel_id=1, source_target_pairs={{0,1},{1,0},{2,3},{3,2},{4,5},{5,4},{6,7},{7,6},{8,9},{9,8},{10,11... | collective-permute-start | bytes 3145736 | tf_op jit(solution)/shard_map/ppermute | solution.py:727
  161.8 48.7 %collective-permute-start.10 = (bf16[512,2048]{1,0:T(8,128)(2,1)}, bf16[512,2048]{1,0:T(8,128)(2,1)}, u32[]{:S(2)}, u32[]{:S(2)}) collective-permute-start(bf16[512,2048]{1,0:T(8,128)(2,1)} %get-tuple-element.86), channel_id=1, source_target_pairs={{0,4},{4,0},{8,12},{12,8},{16,20},{20,16},{24,28},{28,24},{1,5},{5... | collective-permute-start | bytes 6291464 | tf_op jit(solution)/shard_map/ppermute | solution.py:727
  163.1 52.3 %collective-permute-start.11 = (bf16[512,2048]{1,0:T(8,128)(2,1)}, bf16[512,2048]{1,0:T(8,128)(2,1)S(1)}, u32[]{:S(2)}, u32[]{:S(2)}) collective-permute-start(bf16[512,2048]{1,0:T(8,128)(2,1)} %get-tuple-element.89), channel_id=1, source_target_pairs={{0,8},{4,12},{8,0},{12,4},{16,24},{20,28},{24,16},{28,20},{1,9},{5... | collective-permute-start | bytes 6291464 | tf_op jit(solution)/shard_map/ppermute | solution.py:727
  178.5 27.0 %collective-permute-start.12 = (bf16[1024,512]{1,0:T(8,128)(2,1)}, bf16[1024,512]{1,0:T(8,128)(2,1)}, u32[]{:S(2)}, u32[]{:S(2)}) collective-permute-start(bf16[1024,512]{1,0:T(8,128)(2,1)} %get-tuple-element.92), channel_id=1, source_target_pairs={{0,2},{1,3},{2,0},{3,1},{4,6},{5,7},{6,4},{7,5},{8,10},{9,11},{10,... | collective-permute-start | bytes 3145736 | tf_op jit(solution)/shard_map/ppermute | solution.py:727
  205.5 17.2 %collective-permute-start.13 = (bf16[1024,512]{1,0:T(8,128)(2,1)}, bf16[1024,512]{1,0:T(8,128)(2,1)}, u32[]{:S(2)}, u32[]{:S(2)}) collective-permute-start(bf16[1024,512]{1,0:T(8,128)(2,1)} %collective-permute-done.12.refs_7_), channel_id=1, source_target_pairs={{0,1},{1,0},{2,3},{3,2},{4,5},{5,4},{6,7},{7,6},{8,9},{9,8},{10,11... | collective-permute-start | bytes 3145736 | tf_op jit(solution)/shard_map/ppermute | solution.py:727
  205.6 17.0 %collective-permute-start.9 = (bf16[1024,256]{1,0:T(8,128)(2,1)}, bf16[1024,256]{1,0:T(8,128)(2,1)S(1)}, u32[]{:S(2)}, u32[]{:S(2)}) collective-permute-start(bf16[1024,256]{1,0:T(8,128)(2,1)} %get-tuple-element.84), channel_id=1, source_target_pairs={{0,2},{1,3},{2,0},{3,1},{4,6},{5,7},{6,4},{7,5},{8,10},{9,11},{10,... | collective-permute-start | bytes 1572872 | tf_op jit(solution)/shard_map/ppermute | solution.py:727
  208.9 13.7 %collective-permute-start.19 = (f32[2048]{0:T(1024)S(1)}, f32[2048]{0:T(1024)S(1)}, u32[]{:S(2)}, u32[]{:S(2)}) collective-permute-start(f32[2048]{0:T(1024)S(1)} %pad_maximum_fusion.2), channel_id=1, source_target_pairs={{0,2},{1,3},{2,0},{3,1},{4,6},{5,7},{6,4},{7,5},{8,10},{9,11},{10,... | collective-permute-start | bytes 24584 | tf_op jit(solution)/shard_map/ppermute | solution.py:727
  213.8 59.4 %collective-permute-start.29 = (bf16[256,2048]{1,0:T(8,128)(2,1)}, bf16[256,2048]{1,0:T(8,128)(2,1)S(1)}, u32[]{:S(2)}, u32[]{:S(2)}) collective-permute-start(bf16[256,2048]{1,0:T(8,128)(2,1)} %get-tuple-element.87.refs_0_), channel_id=1, source_target_pairs={{0,8},{4,12},{8,0},{12,4},{16,24},{20,28},{24,16},{28,20},{1,9},{5... | collective-permute-start | bytes 3145736 | tf_op jit(solution)/shard_map/ppermute | solution.py:727
  220.0 60.0 %collective-permute-start.32 = (bf16[256,2048]{1,0:T(8,128)(2,1)}, bf16[256,2048]{1,0:T(8,128)(2,1)S(1)}, u32[]{:S(2)}, u32[]{:S(2)}) collective-permute-start(bf16[256,2048]{1,0:T(8,128)(2,1)} %get-tuple-element.90.refs_1_), channel_id=1, source_target_pairs={{0,16},{4,20},{8,24},{12,28},{16,0},{20,4},{24,8},{28,12},{1,17},{... | collective-permute-start | bytes 3145736 | tf_op jit(solution)/shard_map/ppermute | solution.py:727
  269.9 7.0 %collective-permute-start.17 = (f32[2,2048]{1,0:T(2,128)S(1)}, f32[2,2048]{1,0:T(2,128)S(1)}, u32[]{:S(2)}, u32[]{:S(2)}) collective-permute-start(f32[2,2048]{1,0:T(2,128)S(1)} %slice.101), channel_id=1, source_target_pairs={{0,1},{1,0},{2,3},{3,2},{4,5},{5,4},{6,7},{7,6},{8,9},{9,8},{10,11... | collective-permute-start | bytes 49160 | tf_op jit(solution)/shard_map/ppermute | solution.py:727
  271.2 15.1 %collective-permute-start.23 = (bf16[512,512]{1,0:T(8,128)(2,1)S(1)}, bf16[512,512]{1,0:T(8,128)(2,1)S(1)}, u32[]{:S(2)}, u32[]{:S(2)}) collective-permute-start(bf16[512,512]{1,0:T(8,128)(2,1)S(1)} %copy-done.36), channel_id=1, source_target_pairs={{0,4},{4,0},{8,12},{12,8},{16,20},{20,16},{24,28},{28,24},{1,5},{5... | collective-permute-start | bytes 1572872 | tf_op jit(solution)/shard_map/ppermute | solution.py:727
  272.7 18.8 %collective-permute-start.26 = (bf16[512,512]{1,0:T(8,128)(2,1)S(1)}, bf16[512,512]{1,0:T(8,128)(2,1)S(1)}, u32[]{:S(2)}, u32[]{:S(2)}) collective-permute-start(bf16[512,512]{1,0:T(8,128)(2,1)S(1)} %copy-done.35), channel_id=1, source_target_pairs={{0,8},{4,12},{8,0},{12,4},{16,24},{20,28},{24,16},{28,20},{1,9},{5... | collective-permute-start | bytes 1572872 | tf_op jit(solution)/shard_map/ppermute | solution.py:727
  276.8 26.3 %collective-permute-start.30 = (bf16[128,2048]{1,0:T(8,128)(2,1)}, bf16[128,2048]{1,0:T(8,128)(2,1)S(1)}, u32[]{:S(2)}, u32[]{:S(2)}) collective-permute-start(bf16[128,2048]{1,0:T(8,128)(2,1)} %get-tuple-element.123), channel_id=1, source_target_pairs={{0,16},{4,20},{8,24},{12,28},{16,0},{20,4},{24,8},{28,12},{1,17},{... | collective-permute-start | bytes 1572872 | tf_op jit(solution)/shard_map/ppermute | solution.py:727
  276.9 8.0 %collective-permute-start.18 = (f32[2,2048]{1,0:T(2,128)S(1)}, f32[2,2048]{1,0:T(2,128)S(1)}, u32[]{:S(2)}, u32[]{:S(2)}) collective-permute-start(f32[2,2048]{1,0:T(2,128)S(1)} %slice_add_fusion.2), channel_id=1, source_target_pairs={{0,2},{1,3},{2,0},{3,1},{4,6},{5,7},{6,4},{7,5},{8,10},{9,11},{10,... | collective-permute-start | bytes 49160 | tf_op jit(solution)/shard_map/ppermute | solution.py:727
  283.7 19.6 %collective-permute-start.33 = (bf16[128,2048]{1,0:T(8,128)(2,1)}, bf16[128,2048]{1,0:T(8,128)(2,1)S(1)}, u32[]{:S(2)}, u32[]{:S(2)}) collective-permute-start(bf16[128,2048]{1,0:T(8,128)(2,1)} %get-tuple-element.126), channel_id=1, source_target_pairs={{0,4},{4,0},{8,12},{12,8},{16,20},{20,16},{24,28},{28,24},{1,5},{5... | collective-permute-start | bytes 1572872 | tf_op jit(solution)/shard_map/ppermute | solution.py:727
  284.9 21.1 %collective-permute-start.15 = (bf16[2048,256]{1,0:T(8,128)(2,1)S(1)}, bf16[2048,256]{1,0:T(8,128)(2,1)S(1)}, u32[]{:S(2)}, u32[]{:S(2)}) collective-permute-start(bf16[2048,256]{1,0:T(8,128)(2,1)S(1)} %copy-done.34), channel_id=1, source_target_pairs={{0,1},{1,0},{2,3},{3,2},{4,5},{5,4},{6,7},{7,6},{8,9},{9,8},{10,11... | collective-permute-start | bytes 3145736 | tf_op jit(solution)/shard_map/ppermute | solution.py:727
  286.3 38.7 %collective-permute-start.14 = (bf16[2048,256]{1,0:T(8,128)(2,1)}, bf16[2048,256]{1,0:T(8,128)(2,1)}, u32[]{:S(2)}, u32[]{:S(2)}) collective-permute-start(bf16[2048,256]{1,0:T(8,128)(2,1)} %get-tuple-element.102), channel_id=1, source_target_pairs={{0,1},{1,0},{2,3},{3,2},{4,5},{5,4},{6,7},{7,6},{8,9},{9,8},{10,11... | collective-permute-start | bytes 3145736 | tf_op jit(solution)/shard_map/ppermute | solution.py:727
  291.5 14.9 %collective-permute-start.24 = (bf16[256,512]{1,0:T(8,128)(2,1)}, bf16[256,512]{1,0:T(8,128)(2,1)S(1)}, u32[]{:S(2)}, u32[]{:S(2)}) collective-permute-start(bf16[256,512]{1,0:T(8,128)(2,1)} %get-tuple-element.112), channel_id=1, source_target_pairs={{0,8},{4,12},{8,0},{12,4},{16,24},{20,28},{24,16},{28,20},{1,9},{5... | collective-permute-start | bytes 786440 | tf_op jit(solution)/shard_map/ppermute | solution.py:727
  303.1 12.9 %collective-permute-start.27 = (bf16[256,512]{1,0:T(8,128)(2,1)}, bf16[256,512]{1,0:T(8,128)(2,1)S(1)}, u32[]{:S(2)}, u32[]{:S(2)}) collective-permute-start(bf16[256,512]{1,0:T(8,128)(2,1)} %get-tuple-element.118), channel_id=1, source_target_pairs={{0,16},{4,20},{8,24},{12,28},{16,0},{20,4},{24,8},{28,12},{1,17},{... | collective-permute-start | bytes 786440 | tf_op jit(solution)/shard_map/ppermute | solution.py:727
  303.3 17.0 %collective-permute-start.31 = (bf16[128,1024]{1,0:T(8,128)(2,1)S(1)}, bf16[128,1024]{1,0:T(8,128)(2,1)S(1)}, u32[]{:S(2)}, u32[]{:S(2)}) collective-permute-start(bf16[128,1024]{1,0:T(8,128)(2,1)S(1)} %slice.159), channel_id=1, source_target_pairs={{0,2},{1,3},{2,0},{3,1},{4,6},{5,7},{6,4},{7,5},{8,10},{9,11},{10,... | collective-permute-start | bytes 786440 | tf_op jit(solution)/shard_map/ppermute | solution.py:727
  306.1 12.7 %collective-permute-start.34 = (bf16[128,1024]{1,0:T(8,128)(2,1)S(1)}, bf16[128,1024]{1,0:T(8,128)(2,1)S(1)}, u32[]{:S(2)}, u32[]{:S(2)}) collective-permute-start(bf16[128,1024]{1,0:T(8,128)(2,1)S(1)} %slice.158), channel_id=1, source_target_pairs={{0,2},{1,3},{2,0},{3,1},{4,6},{5,7},{6,4},{7,5},{8,10},{9,11},{10,... | collective-permute-start | bytes 786440 | tf_op jit(solution)/shard_map/ppermute | solution.py:727
  306.5 33.1 %collective-permute-start.16 = (bf16[2048,256]{1,0:T(8,128)(2,1)S(1)}, bf16[2048,256]{1,0:T(8,128)(2,1)}, u32[]{:S(2)}, u32[]{:S(2)}) collective-permute-start(bf16[2048,256]{1,0:T(8,128)(2,1)S(1)} %add_convert_fusion), channel_id=1, source_target_pairs={{0,2},{1,3},{2,0},{3,1},{4,6},{5,7},{6,4},{7,5},{8,10},{9,11},{10,... | collective-permute-start | bytes 3145736 | tf_op jit(solution)/shard_map/ppermute | solution.py:727
  316.0 8.9 %collective-permute-start.25 = (bf16[128,512]{1,0:T(8,128)(2,1)}, bf16[128,512]{1,0:T(8,128)(2,1)S(1)}, u32[]{:S(2)}, u32[]{:S(2)}) collective-permute-start(bf16[128,512]{1,0:T(8,128)(2,1)} %get-tuple-element.114), channel_id=1, source_target_pairs={{0,16},{4,20},{8,24},{12,28},{16,0},{20,4},{24,8},{28,12},{1,17},{... | collective-permute-start | bytes 393224 | tf_op jit(solution)/shard_map/ppermute | solution.py:727
  318.7 26.8 %collective-permute-start.28 = (bf16[128,512]{1,0:T(8,128)(2,1)}, bf16[128,512]{1,0:T(8,128)(2,1)S(1)}, u32[]{:S(2)}, u32[]{:S(2)}) collective-permute-start(bf16[128,512]{1,0:T(8,128)(2,1)} %get-tuple-element.120), channel_id=1, source_target_pairs={{0,4},{4,0},{8,12},{12,8},{16,20},{20,16},{24,28},{28,24},{1,5},{5... | collective-permute-start | bytes 393224 | tf_op jit(solution)/shard_map/ppermute | solution.py:727
  (48 other events, 602.8 us)
Sparse Core Ops, SparseCore 0:
  24.5 74.8 all-gather.1

commit v3 on v2

v3 whole, which is shorter than its diff:
```python
import functools
import math

import jax
import jax.numpy as jnp
from jax import lax
from jax.experimental import pallas as pl
from jax.experimental.pallas import tpu as pltpu
from jax.sharding import PartitionSpec as P

HEADS = 16
HD = 64
WIN = 1024
D = 1024
FF = 4096
SEQ = 2048
B = 256
NB = SEQ // B
SLOTS = WIN // B + 1
STRIP = SLOTS * B
LH = 4
SHARE = LH * HD
UNITS = FF // 4
TILE = 512
OWN = SEQ // 2

EPS = 1e-05
TAU = 2.0
NEG = -1e30
F32 = jnp.float32
BF = jnp.bfloat16
VMEM_LIMIT = 62 * 2**20


def dot(a, b):
    return jnp.dot(a, b, preferred_element_type=F32)


def dot_nt(a, b):
    return lax.dot_general(a, b, (((1,), (1,)), ((), ())), preferred_element_type=F32)


def params():
    return pltpu.CompilerParams(
        dimension_semantics=("arbitrary",), vmem_limit_bytes=VMEM_LIMIT
    )


def feature_block(rank):
    return pl.ds(pl.multiple_of(rank * SHARE, SHARE), SHARE)


def head_of_lane(shape):
    return lax.broadcasted_iota(jnp.int32, shape, 1) // HD


def ordered(kernel, count):
    return lambda ids, *refs: kernel(ids, *refs[count:])


def waits(after):
    return [pl.BlockSpec(memory_space=pl.ANY)] * len(after)


def row_stats(rows):
    mean = jnp.sum(rows, axis=1, keepdims=True) / D
    square = jnp.sum(rows * rows, axis=1, keepdims=True) / D
    return mean, lax.rsqrt(square - mean * mean + EPS)


def piece(j, bit, chunk):
    inner = bit * chunk
    mine = dp_bit(bit)
    base = (j * 128) // inner * (2 * inner) + (j * 128) % inner
    return [
        pl.ds(pl.multiple_of(base + side * inner, 128), 128) for side in (mine, 1 - mine)
    ]


def dp_bit(bit):
    return lax.rem(lax.div(lax.axis_index("dp"), bit), 2)


def dp_partner(bit):
    return lax.axis_index("dp") + bit - 2 * bit * dp_bit(bit)


def place():
    t = lax.axis_index("tensor")
    core, y = lax.rem(t, 2), lax.div(t, 2)
    return core, y, (t, 2 * y + 1 - core, 2 * (1 - y) + core, 2 * (1 - y) + 1 - core)


def remote(src, dst, send, got, where):
    return pltpu.make_async_remote_copy(
        src_ref=src, dst_ref=dst, send_sem=send, recv_sem=got,
        device_id=where, device_id_type=pl.DeviceIdType.MESH,
    )


def greet(places):
    barrier = pltpu.get_barrier_semaphore()
    for where in places:
        pl.semaphore_signal(
            barrier, inc=1, device_id=where, device_id_type=pl.DeviceIdType.MESH
        )
    pl.semaphore_wait(barrier, len(places))


def block_rows(b):
    return pl.ds(pl.multiple_of(b * B, B), B)


def remote_params(collective_id):
    return pltpu.CompilerParams(
        dimension_semantics=("arbitrary",),
        vmem_limit_bytes=VMEM_LIMIT,
        collective_id=collective_id,
        has_side_effects=True,
    )


def split_store(keep_ref, send_ref, value_ref, core):
    for half in range(2):
        cols = slice(half * SHARE, (half + 1) * SHARE)
        keep_ref[:, cols] = value_ref[:, feature_block(2 * half + core)].astype(keep_ref.dtype)
        send_ref[:, cols] = value_ref[:, feature_block(2 * half + 1 - core)].astype(
            send_ref.dtype
        )


TAIL = 3


def fwd_kernel(
    x_any, x_own, vec, wq, wk, wv, bqv, wd, lo, pad, alibi,
    p_ref, q_ref, k_ref, v_ref, linv_ref, ctx_ref, a_ref, b_ref, x1_ref, x2_ref, x3_ref, xm_ref, hm_ref,
    xs, qm_s, k_s, va_s, u_s, res_s, lo_s,
    xc, xy, xf, part_keep, part_send, part_got, sum_keep, sum_send, sum_got, whole_own, whole_got,
    s_xc, r_xc, s_xy, r_xy, s_xf, r_xf, s_pc, r_pc, s_sy, r_sy, s_wc, r_wc,
):
    step = pl.program_id(0)
    core, y, ranks = place()

    rows = block_rows
    beside, across = {"tensor": ranks[1]}, {"tensor": ranks[2]}

    def to_core(b):
        return remote(x_any.at[rows(b)], xc.at[b], s_xc.at[b], r_xc.at[b], beside)

    def to_y(b):
        return remote(x_any.at[rows(b)], xy.at[b], s_xy.at[b], r_xy.at[b], across)

    def forward(b):
        return remote(xy.at[b], xf.at[b], s_xf.at[b], r_xf.at[b], beside)

    def part_to_core(b):
        return remote(part_send.at[b], part_got.at[b], s_pc.at[b], r_pc.at[b], beside)

    def sum_to_y(j):
        return remote(sum_send.at[j], sum_got.at[j], s_sy.at[j], r_sy.at[j], across)

    def whole_to_core(j):
        return remote(whole_own.at[j], whole_got.at[j], s_wc.at[j], r_wc.at[j], beside)

    @pl.when(step == 0)
    def _():
        greet((beside, across))
        for b in range(3):
            to_y(b).start()
            to_core(b).start()
        to_y(0).wait_recv()
        forward(0).start()
        hm_ref[...] = jnp.full(hm_ref.shape, NEG, F32)

    for b in range(3, NB):

        @pl.when(step == b - 2)
        def _():
            to_y(b).start()
            to_core(b).start()

    row_i = lax.broadcasted_iota(jnp.int32, (B, B), 0)
    col_i = lax.broadcasted_iota(jnp.int32, (B, B), 1)
    lanes = head_of_lane((B, SHARE))

    @pl.when(step < NB - 1)
    def _():
        to_y(step + 1).wait_recv()
        forward(step + 1).start()

    @pl.when(step < NB)
    def _():
        to_core(step).wait_recv()
        forward(step).wait_recv()
        blocks = (x_own[...], xc[step], xy[step], xf[step])
        for rank, block, ref in zip(ranks, blocks, (None, x1_ref, x2_ref, x3_ref)):
            xs[:, feature_block(rank)] = block.astype(F32)
            if ref is not None:
                ref[...] = block
        value = xs[...]

        @pl.when(lax.rem(step, 2) == y)
        def _():
            xm_ref[rows(step // 2), :] = value.astype(BF)

        mean, rstd = row_stats(value)
        n1 = ((value - mean) * rstd * vec[0:1, :] + vec[1:2, :]).astype(BF)
        q = (dot(n1, wq[...]) + bqv[0:1, :]).astype(BF)
        k = dot(n1, wk[...]).astype(BF)
        v = (dot(n1, wv[...]) + bqv[1:2, :]).astype(BF)
        qs = q * jnp.asarray(1.0 / math.sqrt(HD), BF)
        q_ref[...] = qs
        k_ref[...] = k
        v_ref[...] = v
        here = rows(step)
        k_s[here, :] = k
        for h in range(LH):
            qm_s[h] = jnp.where(lanes == h, qs, jnp.zeros_like(qs))
            va_s[h, here, :] = jnp.where(lanes == h, v, jnp.ones_like(v))
        lo_s[...] = jnp.broadcast_to(lo[...], (B, B))

    def attend(nb):
        start = pl.multiple_of((step + 1 - nb) * B, B)

        def head(h, carry):
            qm = qm_s[h]
            top = jnp.full((B, 128), NEG, F32)
            biggest = hm_ref[h]
            for r in range(nb):
                slot = SLOTS - nb + r
                base = pl.multiple_of(start + r * B, B)
                s = dot_nt(qm, k_s[pl.ds(base, B), :])
                inside = col_i + base >= lo_s[...]
                shut = pad[0:1, pl.ds(base, B)]
                if r == nb - 1:
                    s = jnp.where(row_i == col_i, s, s + shut)
                    s = jnp.where(inside & (col_i <= row_i), s, NEG)
                else:
                    s = jnp.where(inside, s + shut, NEG)
                biggest = jnp.maximum(biggest, jnp.max(s.reshape(B // 8, 8, B), axis=0))
                s = s + alibi[pl.ds(h, 1), slot * B : (slot + 1) * B]
                u_s[:, slot * B : (slot + 1) * B] = s
                top = jnp.maximum(top, jnp.maximum(s[:, :128], s[:, 128:]))
            hm_ref[h] = biggest
            top = jnp.max(top, axis=1, keepdims=True)
            for r in range(nb):
                slot = SLOTS - nb + r
                cols = slice(slot * B, (slot + 1) * B)
                p_ref[h, :, cols] = jnp.exp(u_s[:, cols] - top).astype(BF)
            res_s[h] = dot(p_ref[h, :, (SLOTS - nb) * B :], va_s[h, pl.ds(start, nb * B), :])
            return carry

        lax.fori_loop(0, LH, head, 0)

    for nb in range(1, SLOTS):
        pl.when(step == nb - 1)(functools.partial(attend, nb))
    pl.when((step >= SLOTS - 1) & (step < NB))(functools.partial(attend, SLOTS))

    @pl.when(step < NB)
    def _():
        ctx = res_s[0]
        total = res_s[LH - 1]
        for h in range(1, LH):
            ctx = jnp.where(lanes == h, res_s[h], ctx)
            total = jnp.where(lanes == h, res_s[h - 1], total)
        inv = 1.0 / pltpu.roll(total, SHARE - HD, 1)
        linv_ref[...] = inv
        ctx = (ctx * inv).astype(BF)
        ctx_ref[...] = ctx
        xs[...] = dot(ctx, wd[...])
        split_store(part_keep.at[step], part_send.at[step], xs, core)
        part_to_core(step).start()

    @pl.when((step >= 1) & (step <= NB))
    def _():
        b = step - 1
        j = b // 2
        part_to_core(b).wait_recv()
        total = part_keep[b].astype(F32) + part_got[b].astype(F32)

        @pl.when(lax.rem(b, 2) == y)
        def _():
            sum_keep[j] = total

        @pl.when(lax.rem(b, 2) != y)
        def _():
            sum_send[j] = total.astype(BF)
            sum_to_y(j).start()

    @pl.when((step >= TAIL) & (lax.rem(step + NB - TAIL, 2) == y))
    def _():
        j = (step - TAIL) // 2
        sum_to_y(j).wait_recv()
        total = (sum_keep[j] + sum_got[j].astype(F32)).astype(BF)
        whole_own[j] = total
        a_ref[rows(j), :] = total
        whole_to_core(j).start()

    @pl.when(step == NB + TAIL - 1)
    def _():
        for j in range(NB // 2):
            whole_to_core(j).wait_recv()
            b_ref[rows(j), :] = whole_got[j]
        for b in range(NB):
            to_core(b).wait_send()
            to_y(b).wait_send()
            forward(b).wait_send()
            part_to_core(b).wait_send()
        for j in range(NB // 2):
            sum_to_y(j).wait_send()
            whole_to_core(j).wait_send()


def attention_forward(x, vec, wq, wk, wv, bqv, wd, lo, pad, alibi):
    last = lambda s: jnp.minimum(s, NB - 1)
    row = lambda width: pl.BlockSpec((B, width), lambda s: (last(s), 0))
    whole = lambda shape: pl.BlockSpec(shape, lambda s: (0,) * len(shape))
    like = jax.ShapeDtypeStruct
    dma = lambda n: pltpu.SemaphoreType.DMA((n,))
    half = NB // 2
    return pl.pallas_call(
        fwd_kernel,
        grid=(NB + TAIL,),
        in_specs=[pl.BlockSpec(memory_space=pl.ANY), row(SHARE), whole((8, D))]
        + [whole((D, SHARE))] * 3
        + [whole((8, SHARE)), whole((SHARE, D)), row(1), whole((8, SEQ)), whole((8, STRIP))],
        out_specs=[pl.BlockSpec((LH, B, STRIP), lambda s: (0, last(s), 0))]
        + [row(SHARE)] * 5
        + [whole((OWN, D // 2))] * 2
        + [row(SHARE)] * 3
        + [whole((OWN, D)), whole((LH, 8, B))],
        scratch_shapes=[
            pltpu.VMEM((B, D), F32),
            pltpu.VMEM((LH, B, SHARE), BF),
            pltpu.VMEM((SEQ, SHARE), BF),
            pltpu.VMEM((LH, SEQ, SHARE), BF),
            pltpu.VMEM((B, STRIP), F32),
            pltpu.VMEM((LH, B, SHARE), F32),
            pltpu.VMEM((B, B), jnp.int32),
        ]
        + [pltpu.VMEM((NB, B, SHARE), BF)] * 3
        + [pltpu.VMEM((NB, B, D // 2), BF)] * 3
        + [pltpu.VMEM((half, B, D // 2), F32)]
        + [pltpu.VMEM((half, B, D // 2), BF)] * 4
        + [dma(NB)] * 8
        + [dma(half)] * 4,
        out_shape=[like((LH, SEQ, STRIP), BF)]
        + [like((SEQ, SHARE), BF)] * 3
        + [like((SEQ, SHARE), F32), like((SEQ, SHARE), BF)]
        + [like((OWN, D // 2), BF)] * 2
        + [like((SEQ, SHARE), BF)] * 3
        + [like((OWN, D), BF), like((LH, 8, B), F32)],
        compiler_params=remote_params(0),
        cost_estimate=pl.CostEstimate(
            flops=16 * 10**9, bytes_accessed=40 * 2**20, transcendentals=8 * 10**6
        ),
        name="attention_forward",
    )(x, x, vec, wq, wk, wv, bqv, wd, lo, pad, alibi)


def mlp_kernel(
    a_own, a_par, xm, d0, d1, d2, d3, vec, bup, wu0, wu1, wd0, wd1,
    mk_ref, ms_ref, gn_ref, h1_ref, gu_ref, su_ref, gd_ref, sd_ref, bs_ref, ru_ref,
    n2_s, n2t_s, dy_s, dyt_s, am_s, ag_s, act_s, gp_s, us_s, s_u, r_u,
    *, bit, chunk,
):
    i = pl.program_id(0)
    core, y, ranks = place()
    partner = {"dp": dp_partner(bit)}

    def send_up(n):
        return remote(us_s.at[n], ru_ref.at[n], s_u.at[n], r_u.at[n], partner)

    @pl.when(i == 0)
    def _():
        greet((partner,))

        def assemble(rb, carry):
            rows = block_rows(rb)
            h1_ref[rows, :] = xm[rows, :].astype(F32)
            for rank, d in zip(ranks, (d0, d1, d2, d3)):
                dy_s[rows, feature_block(rank)] = d[rows, :]
            for part, a in ((core, a_own), (1 - core, a_par)):
                for half in range(2):
                    cols = feature_block(2 * half + part)
                    h1_ref[rows, cols] += a[rows, half * SHARE : (half + 1) * SHARE].astype(F32)
            value = h1_ref[rows, :] + vec[2:3, :]
            h1_ref[rows, :] = value
            mean, rstd = row_stats(value)
            n2 = ((value - mean) * rstd * vec[3:4, :] + vec[4:5, :]).astype(BF)
            n2_s[rows, :] = n2
            n2t_s[:, rows] = n2.T
            dyt_s[:, rows] = dy_s[rows, :].T
            am_s[rows, :] = jnp.zeros((B, D), F32)
            ag_s[rows, :] = jnp.zeros((B, D), F32)
            return carry

        lax.fori_loop(0, OWN // B, assemble, 0)

    def tile(wu, wd, which):
        bias = bup[which : which + 1, pl.ds(pl.multiple_of(lax.rem(i, 2) * TILE, TILE), TILE)]
        scale = math.sqrt(2.0 / math.pi)

        def rows_of(rb, sums):
            rows = pl.ds(pl.multiple_of(rb * B, B), B)
            pre = dot(n2_s[rows, :], wu[...]) + bias
            back = dot_nt(dy_s[rows, :], wd[...])
            square = pre * pre
            th = jnp.tanh(scale * pre * (1.0 + 0.044715 * square))
            half = 0.5 * (1.0 + th)
            act = (pre * half).astype(BF)
            slope = half + 0.5 * pre * (1.0 - th * th) * (scale + (3 * 0.044715 * scale) * square)
            gp = (slope * back).astype(BF)
            act_s[rows, :] = act
            gp_s[rows, :] = gp
            am_s[rows, :] += dot(act, wd[...])
            ag_s[rows, :] += dot_nt(gp, wu[...])
            return sums + jnp.sum(gp.astype(F32), axis=0, keepdims=True)

        sums = lax.fori_loop(0, OWN // B, rows_of, jnp.zeros((1, TILE), F32))
        bs_ref[...] = jnp.broadcast_to(sums, bs_ref.shape)

        def grads(j, carry):
            to = pl.ds(pl.multiple_of(j * 128, 128), 128)
            mine, other = piece(j, bit, chunk)
            gu_ref[to, :] = dot(n2t_s[mine, :], gp_s[...]).astype(BF)
            gd_ref[to, :] = dot(dyt_s[mine, :], act_s[...]).astype(BF)
            us_s[i, to, :] = dot(n2t_s[other, :], gp_s[...]).astype(BF)
            sd_ref[to, :] = dot(dyt_s[other, :], act_s[...]).astype(BF)
            return carry

        lax.fori_loop(0, D // 256, grads, 0)

        @pl.when(i < 3)
        def _():
            send_up(i).start()

    pl.when(i < 2)(lambda: tile(wu0, wd0, 0))
    pl.when(i >= 2)(lambda: tile(wu1, wd1, 1))

    @pl.when(i == 3)
    def _():
        split_store(mk_ref, ms_ref, am_s, core)
        gn_ref[...] = ag_s[...].astype(BF)
        su_ref[...] = us_s[3]
        for n in range(3):
            send_up(n).wait()


def feed_forward(a_own, a_par, xm, ds, vec, bup, wu0, wd0, w_other, bit, chunk):
    whole = lambda shape: pl.BlockSpec(shape, lambda i: (0,) * len(shape))
    low = lambda i: jnp.minimum(i, 1)
    high = lambda i: jnp.maximum(i - 2, 0)
    like = jax.ShapeDtypeStruct
    tile = pl.BlockSpec((D // 2, TILE), lambda i: (0, i))
    return pl.pallas_call(
        functools.partial(mlp_kernel, bit=bit, chunk=chunk),
        grid=(4,),
        in_specs=[whole((OWN, D // 2))] * 2
        + [whole((OWN, D))]
        + [whole((OWN, SHARE))] * 4
        + [
            whole((8, D)),
            whole((8, UNITS)),
            pl.BlockSpec((D, TILE), lambda i: (0, low(i))),
            pl.BlockSpec((D, TILE), lambda i: (0, high(i))),
            pl.BlockSpec((TILE, D), lambda i: (low(i), 0)),
            pl.BlockSpec((TILE, D), lambda i: (high(i), 1)),
        ],
        out_specs=[whole((OWN, D // 2))] * 2
        + [whole((OWN, D))] * 2
        + [
            tile,
            whole((D // 2, TILE)),
            tile,
            tile,
            pl.BlockSpec((8, TILE), lambda i: (0, i)),
            pl.BlockSpec(memory_space=pl.ANY),
        ],
        scratch_shapes=[
            pltpu.VMEM((OWN, D), BF),
            pltpu.VMEM((D, OWN), BF),
            pltpu.VMEM((OWN, D), BF),
            pltpu.VMEM((D, OWN), BF),
            pltpu.VMEM((OWN, D), F32),
            pltpu.VMEM((OWN, D), F32),
            pltpu.VMEM((OWN, TILE), BF),
            pltpu.VMEM((OWN, TILE), BF),
            pltpu.VMEM((4, D // 2, TILE), BF),
            pltpu.SemaphoreType.DMA((3,)),
            pltpu.SemaphoreType.DMA((3,)),
        ],
        out_shape=[like((OWN, D // 2), BF)] * 2
        + [
            like((OWN, D), BF),
            like((OWN, D), F32),
            like((D // 2, 2 * UNITS), BF),
            like((D // 2, TILE), BF),
            like((D // 2, 2 * UNITS), BF),
            like((D // 2, 2 * UNITS), BF),
            like((8, 2 * UNITS), F32),
            like((3, D // 2, TILE), BF),
        ],
        compiler_params=remote_params(1),
        cost_estimate=pl.CostEstimate(
            flops=26 * 10**9, bytes_accessed=40 * 2**20, transcendentals=2 * 10**6
        ),
        name="feed_forward",
    )(a_own, a_par, xm, *ds, vec, bup, wu0, w_other, wd0, w_other)


LEAD = 2
FIRST = (0, 1, 1, 3, 4, 6, 8, 10)
PAIRS = ((0, 2), (1, 7), (3, 5), (4, 6))
FINAL = 3


def last_step(levels):
    return FIRST[-1] + 2 * (levels - 1) + 1


def bwd_kernel(
    x0, x1, x2, x3, x_late, h1, gn, gn_any, mk, ms_any, d0, d1, d2, d3, gu, gd, ru, su_any, sd_any,
    p_ref, q_ref, linv_ref, ctx_ref, k_ref, v_ref, vec, wq, wk, wv, wd,
    out_ref, tg_ref, wu_ref, wdn_ref, ka_ref, sa_ref, kb_ref, sb_ref, cs_ref, bs_ref, n1_ref,
    w_s, gh_s, gm_s, gt_s, qt_s, dl_s, ds_s, res_s, dkt_s, dvt_s, acc_s,
    gn_got, mr_got, o_send, o_got, gh_own, gh_y, gh_f,
    part_keep, part_send, part_got, sum_keep, sum_send, sum_got, ghx_s, st_keep, st_got, st_sum, st_all,
    gk, g1, y_send, y_got, *rest, order, bit_b, chunk,
):
    levels = len(order)
    stages = [rest[3 * n : 3 * n + 3] for n in range(levels - 1)]
    (
        s_gn, r_gn, s_mr, r_mr, s_o, r_o, s_gy, r_gy, s_gf, r_gf, s_pc, r_pc, s_sy, r_sy,
        s_tc, r_tc, s_ty, r_ty, s_g1, r_g1, s_yy, r_yy, l_g, l_w, *g_sems,
    ) = rest[3 * (levels - 1) :]
    step = pl.program_id(0)
    b = NB - 1 - (step - LEAD)
    core, y, ranks = place()
    beside, across = {"tensor": ranks[1]}, {"tensor": ranks[2]}
    partners = [{"dp": dp_partner(bit)} for bit in order]
    half = NB // 2
    last = last_step(levels)
    lanes = head_of_lane((B, SHARE))

    send_gn = lambda j: remote(gn_any.at[block_rows(j)], gn_got.at[j], s_gn.at[j], r_gn.at[j], beside)
    send_mr = lambda j: remote(ms_any.at[block_rows(j)], mr_got.at[j], s_mr.at[j], r_mr.at[j], beside)
    send_o = lambda j: remote(o_send.at[j], o_got.at[j], s_o.at[j], r_o.at[j], across)
    send_gy = lambda j, side: remote(
        gh_own.at[j, :, feature_block(2 * side + core)],
        gh_y.at[j, :, side * SHARE : (side + 1) * SHARE],
        s_gy.at[2 * j + side], r_gy.at[2 * j + side], across,
    )
    send_gf = lambda j: remote(gh_y.at[j], gh_f.at[j], s_gf.at[j], r_gf.at[j], beside)
    send_part = lambda n: remote(part_send.at[lax.rem(n, 4)], part_got.at[n], s_pc.at[n], r_pc.at[n], beside)
    send_sum = lambda n: remote(sum_send.at[n], sum_got.at[n], s_sy.at[n], r_sy.at[n], across)
    send_tc = lambda n: remote(st_keep.at[n], st_got.at[n], s_tc.at[n], r_tc.at[n], beside)
    send_ty = lambda n: remote(st_sum.at[n], st_all.at[n], s_ty.at[n], r_ty.at[n], across)

    def tile_of(p):
        up = p < 3 or p == 7
        n = (p if p < 3 else 3) if up else p - 3
        return slice(n * TILE, (n + 1) * TILE), up

    def send_first(p):
        cols, up = tile_of(p)
        src = su_any if up else sd_any.at[:, cols]
        return remote(src, g1.at[p - 3], s_g1.at[p - 3], r_g1.at[p - 3], partners[0])

    def load_keep(p):
        cols, up = tile_of(p)
        return pltpu.make_async_copy((gu if up else gd).at[:, cols], gk.at[p % 4], l_g.at[p % 4])

    def send_stage(p, n):
        _, send, got = stages[n - 1]
        return remote(
            send.at[p % 4], got.at[p], g_sems[2 * n - 2].at[p], g_sems[2 * n - 1].at[p], partners[n]
        )

    send_last = lambda n: remote(y_send.at[n], y_got.at[n], s_yy.at[n], r_yy.at[n], across)

    def split(p, n):
        if n == 1:
            load_keep(p).wait()
            keep = lambda rows: gk[p % 4, rows, :]
            if p < 3:
                got = lambda rows: ru[p, rows, :]
            else:
                send_first(p).wait_recv()
                got = lambda rows: g1[p - 3, rows, :]
        else:
            send_stage(p, n - 1).wait_recv()
            keep = lambda rows: stages[n - 2][0][p % 4, rows, :]
            got = lambda rows: stages[n - 2][2][p, rows, :]
        size = D >> n
        following = order[n]
        inner = chunk
        for other in order[n + 1 :]:
            inner *= 2 if other < following else 1
        mine = dp_bit(following)
        if p >= 4:
            send_stage(p - 4, n).wait_send()
        for group in range(size // (2 * inner)):
            to = slice(group * inner, (group + 1) * inner)
            for side, ref in ((mine, stages[n - 1][0]), (1 - mine, stages[n - 1][1])):
                rows = pl.ds(pl.multiple_of(group * 2 * inner + side * inner, inner), inner)
                ref[p % 4, to, :] = (keep(rows).astype(F32) + got(rows).astype(F32)).astype(BF)
        send_stage(p, n).start()

    def whole_tile(p):
        send_stage(p, levels - 1).wait_recv()
        keep, _, got = stages[levels - 2]
        total = keep[p % 4].astype(F32) + got[p].astype(F32)
        for n, (own, other) in enumerate(PAIRS):
            cols, up = tile_of(own)
            if p == own:
                (wu_ref if up else wdn_ref)[:, cols] = total
            if p == other:
                y_send[n] = total.astype(BF)
                send_last(n).start()

    def close(n):
        cols, up = tile_of(PAIRS[n][0])
        send_last(n).wait_recv()
        (wu_ref if up else wdn_ref)[:, cols] += y_got[n].astype(F32)

    @pl.when(step == 0)
    def _():
        greet([beside, across] + partners)
        for j in range(half - 1, -1, -1):
            send_gn(j).start()
            send_mr(j).start()
        for p in range(3, 8):
            send_first(p).start()
        for p in range(4):
            load_keep(p).start()
        cs_ref[...] = jnp.zeros(cs_ref.shape, F32)
        bs_ref[...] = jnp.zeros(bs_ref.shape, F32)
        n1_ref[...] = jnp.zeros(n1_ref.shape, F32)
        dkt_s[...] = jnp.zeros(dkt_s.shape, F32)
        dvt_s[...] = jnp.zeros(dvt_s.shape, F32)
        acc_s[...] = jnp.zeros(acc_s.shape, F32)

    @pl.when(step < half)
    def _():
        j = half - 1 - step
        send_gn(j).wait_recv()
        send_mr(j).wait_recv()
        for rank, d in zip(ranks, (d0, d1, d2, d3)):
            w_s[:, feature_block(rank)] = d[...].astype(F32)
        dy = w_s[...]
        value = h1[...]

        def out(side):
            part = pl.ds(pl.multiple_of(side * SHARE, SHARE), SHARE)
            cols = feature_block(2 * side + core)
            total = mk[:, part].astype(F32) + mr_got[j, :, part].astype(F32)
            return (h1[:, cols] + total + vec[5:6, cols]).astype(BF)

        out_ref[block_rows(2 * j + y), :] = out(y)
        o_send[j] = out(1 - y)
        mean, rstd = row_stats(value)
        xhat = (value - mean) * rstd
        grad = gn[...].astype(F32) + gn_got[j].astype(F32)
        scaled = grad * vec[3:4, :]
        first = jnp.sum(scaled, axis=1, keepdims=True) / D
        second = jnp.sum(scaled * xhat, axis=1, keepdims=True) / D
        gh = dy + rstd * (scaled - first - xhat * second)
        for n, columns in enumerate((grad * xhat, grad, gh, dy)):
            cs_ref[n : n + 1, :] += jnp.sum(columns, axis=0, keepdims=True)
        gh_own[j] = gh.astype(BF)
        send_gy(j, 0).start()
        send_gy(j, 1).start()
        send_o(j).start()

    @pl.when((step >= LEAD) & (step < LEAD + NB))
    def _():
        j = b // 2

        @pl.when(lax.rem(b, 2) == y)
        def _():
            gh_s[...] = gh_own[j]

        @pl.when(lax.rem(b, 2) != y)
        def _():
            send_gf(j).wait_recv()
            for part, ref in ((core, gh_y), (1 - core, gh_f)):
                for side in range(2):
                    gh_s[:, feature_block(2 * side + part)] = ref[j, :, side * SHARE : (side + 1) * SHARE]

        gc = dot_nt(gh_s[...], wd[...]).astype(BF).astype(F32)
        scaled = gc * linv_ref[...]
        gcs = scaled.astype(BF)
        product = scaled * ctx_ref[...].astype(F32)
        qt_s[...] = q_ref[...].T.reshape(LH, HD, B)
        gt_s[...] = gcs.T.reshape(LH, HD, B)
        for h in range(LH):
            gm_s[h] = jnp.where(lanes == h, gcs, jnp.zeros_like(gcs))
            delta = jnp.sum(jnp.where(lanes == h, product, 0.0), axis=1, keepdims=True)
            dl_s[h] = jnp.broadcast_to(delta, (B, 128))

    def attend(nb):
        start = pl.multiple_of((b + 1 - nb) * B, B)

        def head(h, carry):
            gm = gm_s[h]
            delta = jnp.concatenate([dl_s[h]] * 2, axis=1)
            for r in range(nb):
                slot = SLOTS - nb + r
                cols = slice(slot * B, (slot + 1) * B)
                dp = dot_nt(gm, v_ref[pl.ds(pl.multiple_of(start + r * B, B), B), :])
                ds_s[:, cols] = (p_ref[h, :, cols].astype(F32) * (dp - delta)).astype(BF)
            live = slice((SLOTS - nb) * B, STRIP)
            keys = pl.ds(start, nb * B)
            res_s[h] = dot(ds_s[:, live], k_ref[keys, :])
            dkt_s[h, :, keys] += dot(qt_s[h], ds_s[:, live])
            dvt_s[h, :, keys] += dot(gt_s[h], p_ref[h, :, live])
            return carry

        lax.fori_loop(0, LH, head, 0)

    pl.when((step >= LEAD) & (b >= SLOTS - 1))(functools.partial(attend, SLOTS))
    for nb in range(SLOTS - 1, 0, -1):
        pl.when(b == nb - 1)(functools.partial(attend, nb))

    @pl.when((step >= LEAD) & (step < LEAD + NB))
    def _():
        dq = res_s[0]
        for h in range(1, LH):
            dq = jnp.where(lanes == h, res_s[h], dq)
        dq = (dq * (1.0 / math.sqrt(HD))).astype(BF)
        here = block_rows(b)
        dk = dkt_s[:, :, here].reshape(SHARE, B).astype(BF).T
        dv = dvt_s[:, :, here].reshape(SHARE, B).astype(BF).T
        bs_ref[0:1, :] += jnp.sum(dq.astype(F32), axis=0, keepdims=True)
        bs_ref[1:2, :] += jnp.sum(dv.astype(F32), axis=0, keepdims=True)

        for rank, x in zip(ranks, (x0, x1, x2, x3)):
            w_s[:, feature_block(rank)] = x[...].astype(F32)
        value = w_s[...]
        mean, rstd = row_stats(value)
        xhat = (value - mean) * rstd
        n1t = (xhat * vec[0:1, :] + vec[1:2, :]).astype(BF).T
        acc_s[:, 0:SHARE] += dot(n1t, dq)
        acc_s[:, SHARE : 2 * SHARE] += dot(n1t, dk)
        acc_s[:, 2 * SHARE : 3 * SHARE] += dot(n1t, dv)
        acc_s[:, 3 * SHARE :] += dot(gh_s[...].T, ctx_ref[...])

        grad = dot_nt(dq, wq[...]) + dot_nt(dk, wk[...]) + dot_nt(dv, wv[...])
        scaled = grad * vec[0:1, :]
        first = jnp.sum(scaled, axis=1, keepdims=True)
        second = jnp.sum(scaled * xhat, axis=1, keepdims=True)
        column = lax.broadcasted_iota(jnp.int32, (B, 128), 1)
        packed = jnp.where(
            column == 0, first, jnp.where(column == 1, second, jnp.where(column == 2, mean, rstd))
        )
        st_keep[b] = packed.T[0:8, :]
        send_tc(b).start()
        w_s[...] = grad

        @pl.when(step >= LEAD + 4)
        def _():
            send_part(b + 4).wait_send()

        for n, side in enumerate((y, 1 - y)):
            cols = slice(n * SHARE, (n + 1) * SHARE)
            part_keep[lax.rem(b, 2), :, cols] = w_s[:, feature_block(2 * side + core)].astype(BF)
            part_send[lax.rem(b, 4), :, cols] = w_s[:, feature_block(2 * side + 1 - core)].astype(BF)
        send_part(b).start()
        ghx_s[lax.rem(b, 4)] = gh_s[:, feature_block(ranks[0])]

    weights = ((0, ka_ref), (1, sa_ref), (2, kb_ref), (3, sb_ref))

    def store_weights(n, ref, part):
        cols = slice(part * 2 * SHARE, (part + 1) * 2 * SHARE)
        return pltpu.make_async_copy(gn_got.at[n, :, cols], ref.at[block_rows(part)], l_w.at[2 * n + part])

    @pl.when(step == LEAD + NB - 1)
    def _():
        for j in range(D // 256):
            to = slice(j % 2 * 128, (j % 2 + 1) * 128)
            into = slice(j // 2 * 2 * SHARE, (j // 2 + 1) * 2 * SHARE)
            for n, (bit, cols) in enumerate(
                ((order[0], slice(0, 2 * SHARE)), (bit_b, slice(2 * SHARE, 4 * SHARE)))
            ):
                for side, rows in enumerate(piece(j, bit, chunk)):
                    gn_got[2 * n + side, to, into] = acc_s[rows, cols].astype(BF)
        for n, ref in weights:
            for part in range(2):
                store_weights(n, ref, part).start()

    @pl.when((step >= LEAD + 1) & (step < LEAD + 1 + NB))
    def _():
        n = b + 1
        send_part(n).wait_recv()
        send_tc(n).wait_recv()
        keep = part_keep[lax.rem(n, 2)].astype(F32)
        sum_keep[lax.rem(n, 4)] = keep[:, :SHARE] + part_got[n, :, :SHARE].astype(F32)
        sum_send[n] = (keep[:, SHARE:] + part_got[n, :, SHARE:].astype(F32)).astype(BF)
        st_sum[n] = st_keep[n] + st_got[n]
        send_sum(n).start()
        send_ty(n).start()

    @pl.when((step >= LEAD + FINAL) & (step < LEAD + FINAL + NB))
    def _():
        n = b + FINAL
        send_sum(n).wait_recv()
        send_ty(n).wait_recv()
        grad = sum_keep[lax.rem(n, 4)] + sum_got[n].astype(F32)
        row = lax.broadcasted_iota(jnp.int32, (8, B), 0)
        stats = jnp.where(row < 2, st_sum[n] + st_all[n], st_keep[n])
        stats = jnp.concatenate([stats] * 16, axis=0).T
        xhat = (x_late[...].astype(F32) - stats[:, 2:3]) * stats[:, 3:4]
        scaled = grad * vec[0:1, feature_block(ranks[0])]
        inner = scaled - stats[:, 0:1] / D - xhat * (stats[:, 1:2] / D)
        tg_ref[...] = ghx_s[lax.rem(n, 4)].astype(F32) + stats[:, 3:4] * inner
        n1_ref[0:1, :] += jnp.sum(grad * xhat, axis=0, keepdims=True)
        n1_ref[1:2, :] += jnp.sum(grad, axis=0, keepdims=True)

    for j in range(half - 1, -1, -1):

        @pl.when(step == half - j)
        def _():
            send_gy(j, 0).wait_recv()
            send_gy(j, 1).wait_recv()
            send_gf(j).start()

    for p in range(8):
        for n in range(1, levels):
            pl.when(step == FIRST[p] + 2 * (n - 1))(functools.partial(split, p, n))
        if p >= 4:
            pl.when(step == FIRST[p - 4] + 1)(lambda p=p: load_keep(p).start())
        pl.when(step == FIRST[p] + 2 * (levels - 1))(functools.partial(whole_tile, p))
    for n, pair in enumerate(PAIRS):
        pl.when(step == max(FIRST[p] for p in pair) + 2 * (levels - 1) + 1)(functools.partial(close, n))

    @pl.when(step == last)
    def _():
        for j in range(half):
            send_o(j).wait_recv()
            out_ref[block_rows(2 * j + 1 - y), :] = o_got[j]
            for copy in (send_gn, send_mr, send_o, send_gf, send_last, send_part):
                copy(j).wait_send()
            for side in range(2):
                send_gy(j, side).wait_send()
            for level in range(1, levels):
                send_stage(4 + j, level).wait_send()
        for n in range(NB):
            for copy in (send_sum, send_tc, send_ty):
                copy(n).wait_send()
        for p in range(3, 8):
            send_first(p).wait_send()
        for n, ref in weights:
            for part in range(2):
                store_weights(n, ref, part).wait()


def attention_backward(
    xs, h1, gn, mk, ms, ds, gu, gd, ru, su, sd, p, q, linv, ctx, k, v, vec, wq, wk, wv, wd,
    order, bit_b, chunk,
):
    levels = len(order)
    half = NB // 2
    steps = max(last_step(levels), LEAD + FINAL + NB - 1) + 1
    assert steps == last_step(levels) + 1
    block = lambda s: jnp.clip(NB - 1 + LEAD - s, 0, NB - 1)
    late = lambda s: jnp.clip(NB - 1 + LEAD + FINAL - s, 0, NB - 1)
    row = lambda width: pl.BlockSpec((B, width), lambda s: (block(s), 0))
    own = lambda width: pl.BlockSpec((B, width), lambda s: (jnp.maximum(half - 1 - s, 0), 0))
    once = pl.Buffered(1)
    whole = lambda *shape: pl.BlockSpec(shape, lambda s: (0,) * len(shape), pipeline_mode=once)
    anywhere = pl.BlockSpec(memory_space=pl.ANY)
    like = jax.ShapeDtypeStruct
    vmem = lambda *shape, dtype=BF: pltpu.VMEM(shape, dtype)
    dma = lambda n: pltpu.SemaphoreType.DMA((n,))
    final_late = pl.BlockSpec((B, SHARE), lambda s: (late(s), 0))
    return pl.pallas_call(
        functools.partial(bwd_kernel, order=order, bit_b=bit_b, chunk=chunk),
        grid=(steps,),
        in_specs=[row(SHARE)] * 4
        + [final_late, own(D), own(D), anywhere, own(D // 2), anywhere]
        + [own(SHARE)] * 4
        + [anywhere] * 2
        + [whole(3, D // 2, TILE), anywhere, anywhere]
        + [pl.BlockSpec((LH, B, STRIP), lambda s: (0, block(s), 0))]
        + [row(SHARE)] * 3
        + [whole(SEQ, SHARE)] * 2
        + [whole(8, D)]
        + [whole(D, SHARE)] * 3
        + [whole(SHARE, D)],
        out_specs=[whole(SEQ, SHARE), final_late]
        + [whole(chunk, UNITS)] * 2
        + [anywhere] * 4
        + [whole(8, D), whole(8, SHARE), whole(8, SHARE)],
        scratch_shapes=[
            vmem(B, D, dtype=F32),
            vmem(B, D),
            vmem(LH, B, SHARE),
            vmem(LH, HD, B),
            vmem(LH, HD, B),
            vmem(LH, B, 128, dtype=F32),
            vmem(B, STRIP),
            vmem(LH, B, SHARE, dtype=F32),
            vmem(LH, HD, SEQ, dtype=F32),
            vmem(LH, HD, SEQ, dtype=F32),
            vmem(D, 4 * SHARE, dtype=F32),
            vmem(half, B, D),
            vmem(half, B, D // 2),
            vmem(half, B, SHARE),
            vmem(half, B, SHARE),
            vmem(half, B, D),
            vmem(half, B, D // 2),
            vmem(half, B, D // 2),
            vmem(2, B, D // 2),
            vmem(4, B, D // 2),
            vmem(NB, B, D // 2),
            vmem(4, B, SHARE, dtype=F32),
            vmem(NB, B, SHARE),
            vmem(NB, B, SHARE),
            vmem(4, B, SHARE),
            vmem(NB, 8, B, dtype=F32),
            vmem(NB, 8, B, dtype=F32),
            vmem(NB, 8, B, dtype=F32),
            vmem(NB, 8, B, dtype=F32),
            vmem(4, D // 2, TILE),
            vmem(5, D // 2, TILE),
            vmem(half, chunk, TILE),
            vmem(half, chunk, TILE),
        ]
        + [vmem(slots, D >> (n + 1), TILE) for n in range(1, levels) for slots in (4, 4, 8)]
        + [dma(half)] * 6
        + [dma(NB)] * 2
        + [dma(half)] * 2
        + [dma(NB)] * 8
        + [dma(5)] * 2
        + [dma(half)] * 3
        + [dma(8)]
        + [dma(8)] * (2 * (levels - 1)),
        out_shape=[like((SEQ, SHARE), BF), like((SEQ, SHARE), F32)]
        + [like((chunk, UNITS), F32)] * 2
        + [like((D // 2, 2 * SHARE), BF)] * 4
        + [like((8, D), F32), like((8, SHARE), F32), like((8, SHARE), F32)],
        compiler_params=remote_params(2),
        cost_estimate=pl.CostEstimate(
            flops=30 * 10**9, bytes_accessed=50 * 2**20, transcendentals=0
        ),
        name="backward",
    )(
        *xs, xs[0], h1, gn, gn, mk, ms, *ds, gu, gd, ru, su, sd, p, q, linv, ctx, k, v, vec, wq, wk, wv, wd
    )


def swap(value, axis, bit):
    size = lax.axis_size(axis)
    return lax.ppermute(value, axis, [(i, i ^ bit) for i in range(size)])


def dp_bits():
    bits, bit = [], 1
    while bit < lax.axis_size("dp"):
        bits.append(bit)
        bit *= 2
    return bits


def dp_total(value):
    for bit in dp_bits():
        value = value + swap(value, "dp", bit)
    return value


def pick(value, axis, index):
    return lax.dynamic_index_in_dim(value, index, axis, keepdims=False)


def sum_kernel(bit, km, rm, ko, ro, keep_ref, send_ref):
    for a, b, ref in ((km, rm, keep_ref), (ko, ro, send_ref)):
        ref[...] = (a[...].astype(F32) + b[...].astype(F32)).astype(ref.dtype)


def sum_and_split(bit, keep, other, inner, after=()):
    rows, cols = keep.shape
    step = min(inner, 128)
    per = inner // step
    block = lambda side: pl.BlockSpec(
        (step, cols),
        lambda i, bit: (i // per * 2 * per + (bit[0] if side else 1 - bit[0]) * per + i % per, 0),
    )
    out = pl.BlockSpec((step, cols), lambda i, bit: (i, 0))
    return pl.pallas_call(
        ordered(sum_kernel, len(after)),
        grid_spec=pltpu.PrefetchScalarGridSpec(
            num_scalar_prefetch=1,
            grid=(rows // 2 // step,),
            in_specs=waits(after) + [block(True), block(True), block(False), block(False)],
            out_specs=[out, out],
        ),
        out_shape=[jax.ShapeDtypeStruct((rows // 2, cols), BF)] * 2,
        compiler_params=params(),
        cost_estimate=pl.CostEstimate(flops=rows * cols, bytes_accessed=6 * rows * cols, transcendentals=0),
        name="sum_and_split",
    )(bit, *after, keep, other, keep, other)


def dp_scatter(keep, send, order, after=()):
    rank = lax.axis_index("dp")
    chunk = D // lax.axis_size("dp")
    for n, bit in enumerate(order):
        other = swap(send, "dp", bit)
        if n == len(order) - 1:
            yield keep.astype(F32) + other.astype(F32)
            return
        following = order[n + 1]
        inner = chunk
        for b in order[n + 2 :]:
            inner *= 2 if b < following else 1
        wait = yield send
        mine = ((rank // following) % 2)[None]
        keep, send = sum_and_split(mine, keep, other, inner, wait or ())


def finish(steps, after=()):
    try:
        while True:
            value = steps.send(after)
    except StopIteration:
        return value


def shards(
    tokens,
    out_grad,
    segments,
    padding,
    norm1_gain,
    norm1_bias,
    w_query,
    b_query,
    w_key,
    w_value,
    b_value,
    w_dense,
    dense_bias,
    norm2_gain,
    norm2_bias,
    w_up,
    b_up,
    w_down,
    down_bias,
):
    t = lax.axis_index("tensor")
    rank = lax.axis_index("dp")
    size = lax.axis_size("dp")
    core, y = t % 2, t // 2
    core_swap = lambda value: swap(value, "tensor", 1)
    y_swap = lambda value: swap(value, "tensor", 2)
    rows8 = lambda value: jnp.pad(value, ((0, 8 - value.shape[0]), (0, 0)))

    vectors = jnp.stack([norm1_gain, norm1_bias, dense_bias, norm2_gain, norm2_bias, down_bias])
    vec = lax.dynamic_update_slice(jnp.zeros((6, D), BF), vectors, (0, t * SHARE))
    vec = vec + core_swap(vec)
    vec = rows8((vec + y_swap(vec)).astype(F32))

    part = D // size
    cut = lambda w: lax.dynamic_slice_in_dim(w, rank * part, part, 0)
    w_part = y_swap(jnp.concatenate([cut(w_up), cut(w_down)], axis=1))
    w_other = lax.all_gather(w_part, "dp", axis=0, tiled=True)
    b_up_pair = jnp.stack([b_up, y_swap(b_up)]).astype(F32)

    seg = segments.reshape(SEQ)
    index = jnp.arange(SEQ, dtype=jnp.int32)
    first = jnp.zeros((SEQ,), jnp.int32)
    for value in range(1, 4):
        first = jnp.where(seg == value, jnp.sum((seg < value).astype(jnp.int32)), first)
    lowest = jnp.maximum(first, index - (WIN - 1))
    pad_row = rows8(jnp.where(padding.reshape(1, SEQ) == 1, 0.0, NEG).astype(F32))
    heads = t * LH + jnp.arange(LH)
    slopes = jnp.exp2(-8.0 * (heads.astype(F32) + 1.0) / HEADS)
    alibi = rows8(slopes[:, None] * (jnp.arange(STRIP) - (STRIP - 1)).astype(F32)[None, :])

    by_y = lambda value, which: pick(value.reshape(NB // 2, 2, B, value.shape[-1]), 1, which).reshape(
        OWN, value.shape[-1]
    )
    d_own = by_y(out_grad, y)
    d_send = by_y(out_grad, 1 - y)

    p, q, k, v, linv, ctx, a_own, a_par, x1, x2, x3, xm, hm = attention_forward(
        tokens, vec, w_query, w_key, w_value,
        rows8(jnp.stack([b_query, b_value]).astype(F32)), w_dense,
        lowest.reshape(SEQ, 1), pad_row, alibi,
    )
    xs = [tokens, x1, x2, x3]

    d_y = y_swap(d_send)
    ds = [d_own, core_swap(d_own), d_y, core_swap(d_y)]

    bits = dp_bits()
    order_a = bits if size == 8 else bits[::-1]
    order_b = [2, 4, 1] if size == 8 else [bits[-2], bits[-1], *bits[:-2][::-1]]
    mk, ms, gn, h1, gu, su, gd, sd, bs, ru = feed_forward(
        a_own, a_par, xm, ds, vec, rows8(b_up_pair), w_up, w_down, w_other, order_a[0], part
    )
    output, tokens_grad, w_up_grad, w_down_grad, ka, sa, kb, sb, cs, qv, n1s = attention_backward(
        xs, h1, gn, mk, ms, ds, gu, gd, ru, su, sd, p, q, linv, ctx, k, v, vec,
        w_query, w_key, w_value, w_dense, order_a, order_b[0], part,
    )
    w_down_grad = w_down_grad.T

    steps_a = dp_scatter(ka, sa, order_a)
    steps_b = dp_scatter(kb, sb, order_b)
    next(steps_a), next(steps_b)
    g_qk = finish(steps_a, ())
    g_vd = finish(steps_b, ())

    cs4 = pick(cs[0:4].reshape(4, 2, 2, SHARE), 2, core)
    early = jnp.concatenate([pick(cs4, 1, y).reshape(-1), bs[0, :UNITS]])
    apart = jnp.concatenate([pick(cs4, 1, 1 - y).reshape(-1), bs[0, UNITS:]])
    early = early + y_swap(apart)
    late = jnp.concatenate([n1s[0], n1s[1], qv[0], qv[1]])
    packed = jnp.concatenate([early, late, jnp.pad(jnp.max(hm, axis=(1, 2)), (0, 124))])
    summed = lax.broadcasted_iota(jnp.int32, packed.shape, 0) < packed.shape[0] - 128
    for bit in bits:
        other = swap(packed, "dp", bit)
        packed = jnp.where(summed, packed + other, jnp.maximum(packed, other))
    early, late, head_max = jnp.split(packed, (8 * SHARE, 12 * SHARE))
    head_max = head_max[:LH]
    of = lambda value, n: value[n * SHARE : (n + 1) * SHARE]

    column_scale = jnp.repeat(jnp.sqrt(TAU / jnp.maximum(head_max, TAU)), HD)
    return (
        output,
        tokens_grad,
        of(late, 0),
        of(late, 1),
        g_qk[:, :SHARE],
        of(late, 2),
        g_qk[:, SHARE:],
        g_vd[:, :SHARE],
        of(late, 3),
        g_vd[:, SHARE:].T,
        of(early, 2),
        of(early, 0),
        of(early, 1),
        w_up_grad,
        early[4 * SHARE :],
        w_down_grad,
        of(early, 3),
        head_max,
        w_query.astype(F32) * column_scale,
        b_query.astype(F32) * column_scale,
        w_key.astype(F32) * column_scale,
    )


def solution(mesh):
    in_specs = (
        P("dp", "tensor"),
        P("dp", "tensor"),
        P("dp", None),
        P("dp", None),
        P("tensor"),
        P("tensor"),
        P(None, "tensor"),
        P("tensor"),
        P(None, "tensor"),
        P(None, "tensor"),
        P("tensor"),
        P("tensor", None),
        P("tensor"),
        P("tensor"),
        P("tensor"),
        P(None, "tensor"),
        P("tensor"),
        P("tensor", None),
        P("tensor"),
    )
    out_specs = (
        P("dp", "tensor"),
        P("dp", "tensor"),
        P("tensor"),
        P("tensor"),
        P("dp", "tensor"),
        P("tensor"),
        P("dp", "tensor"),
        P("dp", "tensor"),
        P("tensor"),
        P("tensor", "dp"),
        P("tensor"),
        P("tensor"),
        P("tensor"),
        P("dp", "tensor"),
        P("tensor"),
        P("tensor", "dp"),
        P("tensor"),
        P("tensor"),
        P(None, "tensor"),
        P("tensor"),
        P(None, "tensor"),
    )
    return jax.shard_map(shards, mesh=mesh, in_specs=in_specs, out_specs=out_specs, check_vma=False)
```

time: 369 us -> 344 us (0.932)
  Pallas kernels: 194 us -> 241 us
  waiting for transfers between devices: 81.4 us -> 36.1 us
  starting transfers between devices: 36.6 us -> 20.3 us
  other arithmetic: 19.7 us -> 12.1 us
    pallas_call x3 -> x2, Pallas kernels: 105 us -> 163 us  [the longest x1 105 us: attention_backward(): pl.pallas_call(functools.partial(bwd_kernel, order=order, bit_b=bit_b, ch...]
    ppermute x35 -> x17, waiting for transfers between devices: 81.3 us -> 36.1 us  [swap(): return lax.ppermute(value, axis, [(i, i ^ bit) for i in range(size)])]
    ppermute x35 -> x17, starting transfers between devices: 36.5 us -> 20.2 us  [swap(): return lax.ppermute(value, axis, [(i, i ^ bit) for i in range(size)])]
    pallas_call x8 -> x4, Pallas kernels: 19.9 us -> 7.81 us  [sum_and_split(): pl.pallas_call(ordered(sum_kernel, len(after)), grid_spec=pltpu.PrefetchS...]
    reduce_sum x1 -> x0, other arithmetic: 5.14 us -> none  [shards(): jnp.sum(g_first, axis=0)]
    unnamed x94 -> x55, local copies, waits for them, and re-layouts: 10.3 us -> 9.84 us
  transfers between devices with their start and end apart: 36 -> 18, of which waited for: 13 -> 10; matrix products, arithmetic and copies ran while one was open for 7% -> 5% of each run, Pallas kernels for 39% -> 23%
where the time goes in v3:
time: 344 us; the launch traced here: 343 us
  Pallas kernels  241 us (70%)
  waiting for transfers between devices  36.1 us (10%)
  starting transfers between devices  20.3 us (6%)
  local copies, waits for them, and re-layouts  18.7 us (5%)
  between operations  14.6 us (4%)
  other arithmetic  12.1 us (4%)
    pallas_call x1, Pallas kernels, attention_backward(): pl.pallas_call(functools.partial(bwd_kernel, order=order, bit_b=bit_b, ch...  105 us
    pallas_call x1, Pallas kernels, attention_forward(): pl.pallas_call(fwd_kernel, grid=(NB + TAIL,), in_specs=[pl.BlockSpec(memo...  70.5 us
    pallas_call x1, Pallas kernels, feed_forward(): pl.pallas_call(functools.partial(mlp_kernel, bit=bit, chunk=chunk), grid=...  57.7 us
    ppermute x17, waiting for transfers between devices, swap(): return lax.ppermute(value, axis, [(i, i ^ bit) for i in range(size)])  36.1 us
    ppermute x17, starting transfers between devices, swap(): return lax.ppermute(value, axis, [(i, i ^ bit) for i in range(size)])  20.2 us
    unnamed x55, local copies, waits for them, and re-layouts  9.84 us
    pallas_call x4, Pallas kernels, sum_and_split(): pl.pallas_call(ordered(sum_kernel, len(after)), grid_spec=pltpu.PrefetchS...  7.81 us
  transfers between devices with their start and end apart: 18, of which 10 were waited for; matrix products, arithmetic and copies ran while one was open for 5% of the time, Pallas kernels for 23%

profile of v3, /device:TPU:0, one launch (start us, length us, event | category | flops | bytes accessed | tf_op | source)
XLA Modules:
  0.0 343.0 jit_solution(7082397679421084628)
XLA Ops:
  7.3 1.2 constant_dynamic-slice_fusion.2
  8.6 3.0 collective-permute-start.6
  11.6 11.9 %collective-permute-done.6 = bf16[128,2048]{1,0:T(8,128)(2,1)S(1)} collective-permute-done((bf16[128,2048]{1,0:T(8,128)(2,1)S(1)}, bf16[128,2048]{1,0:T(8,128)(2,1)S(1)}, u32[]{:S(2)}, u32[]{:S(2)}) %collective-permute-start.6) | collective-permute-done | bytes 524320 | tf_op jit(solution)/shard_map/ppermute | solution.py:956
  24.4 1.8 collective-permute-start.5
  27.9 2.0 fusion.4
  30.3 1.1 add_maximum_fusion.lo
  33.3 1.7 collective-permute-start.1
  35.7 5.5 %collective-permute-done.1 = bf16[6,1024]{1,0:T(8,128)(2,1)S(1)} collective-permute-done((bf16[6,1024]{1,0:T(8,128)(2,1)S(1)}, bf16[6,1024]{1,0:T(8,128)(2,1)S(1)}, u32[]{:S(2)}, u32[]{:S(2)}) %collective-permute-start.1) | collective-permute-done | bytes 12320 | tf_op jit(solution)/shard_map/ppermute | solution.py:956
  41.9 70.5 %attention_forward.1 = (bf16[4,2048,1280]{2,1,0:T(8,128)(2,1)}, bf16[2048,256]{1,0:T(8,128)(2,1)}, bf16[2048,256]{1,0:T(8,128)(2,1)}, bf16[2048,256]{1,0:T(8,128...) custom-call(bf16[2048,256]{1,0:T(8,128)(2,1)} %x_late.1, ...), custom_call_target="tpu_custom_call" | custom-call | flops 16000000000 | bytes 41943040 | tf_op jit(solution)/shard_map/attention_forward/pallas_call | solution.py:322
  113.4 57.7 %feed_forward.1 = (bf16[1024,512]{1,0:T(8,128)(2,1)}, bf16[1024,512]{1,0:T(8,128)(2,1)}, bf16[1024,1024]{1,0:T(8,128)(2,1)}, f32[1024,1024]{1,0:T(8,128)}, bf16[...) custom-call(bf16[1024,512]{1,0:T(8,128)(2,1)} %get-tuple-element.66., ...), custom_call_target="tpu_custom_call" | custom-call | flops 25999998976 | bytes 41943040 | tf_op jit(solution)/shard_map/feed_forward/pallas_call | solution.py:457
  171.0 105.2 %backward.1 = (bf16[2048,256]{1,0:T(8,128)(2,1)}, f32[2048,256]{1,0:T(8,128)}, f32[128,1024]{1,0:T(8,128)}, f32[128,1024]{1,0:T(8,128)}, bf16[512,512]{1,0:T(8,1...) custom-call(bf16[2048,256]{1,0:T(8,128)(2,1)} %x_late.1, ...), custom_call_target="tpu_custom_call" | custom-call | flops 30000001024 | bytes 52428800 | tf_op jit(solution)/shard_map/backward/pallas_call | solution.py:878
  278.7 2.6 collective-permute-start.7
  283.8 3.1 collective-permute-done.8
  287.7 3.0 collective-permute-done.9
  291.6 2.0 copy.54
  293.6 2.1 collective-permute-start.14
  296.4 1.1 collective-permute-done.11.refs_1_.refs_3_
  298.3 2.0 sum_and_split.4
  300.3 1.5 collective-permute-start.12
  301.8 2.5 convert_multiply_fusion
  304.3 4.1 %collective-permute-done.14.refs_1_.refs_3_ = bf16[512,512]{1,0:T(8,128)(2,1)S(1)} collective-permute-done((bf16[512,512]{1,0:T(8,128)(2,1)}, bf16[512,512]{1,0:T(8,128)(2,1)S(1)}, u32[]{:S(2)}, u32[]{:S(2)}) %collective-permute-start.14) | collective-permute-done | bytes 524320 | tf_op jit(solution)/shard_map/ppermute | solution.py:956
  309.3 2.1 sum_and_split.6
  313.6 1.9 sum_and_split.5
  315.5 2.5 collective-permute-start.13
  318.6 4.3 %collective-permute-done.15.refs_1_.refs_3_ = bf16[256,512]{1,0:T(8,128)(2,1)S(1)} collective-permute-done((bf16[256,512]{1,0:T(8,128)(2,1)}, bf16[256,512]{1,0:T(8,128)(2,1)S(1)}, u32[]{:S(2)}, u32[]{:S(2)}) %collective-permute-start.15) | collective-permute-done | bytes 262176 | tf_op jit(solution)/shard_map/ppermute | solution.py:956
  323.6 1.8 sum_and_split.7
  325.4 1.8 collective-permute-start.16
  327.2 0.9 convert_add_fusion.1
  328.9 1.8 collective-permute-done.16
  330.6 0.9 convert_add_fusion
  333.0 1.0 copy.67
  334.0 1.3 copy.68
  (122 shorter events, 22.4 us)
Async XLA Ops:
  7.2 19.0 %copy-start.16 = (bf16[256]{0:T(256)(128)(2,1)S(1)}, bf16[256]{0:T(256)(128)(2,1)}, u32[]{:S(2)}) copy-start(bf16[256]{0:T(256)(128)(2,1)} %param.23) | copy-start | bytes 1540
  7.2 19.0 %copy-start.17 = (bf16[256]{0:T(256)(128)(2,1)S(1)}, bf16[256]{0:T(256)(128)(2,1)}, u32[]{:S(2)}) copy-start(bf16[256]{0:T(256)(128)(2,1)} %param.24) | copy-start | bytes 1540
  7.2 19.0 %copy-start.18 = (bf16[256]{0:T(256)(128)(2,1)S(1)}, bf16[256]{0:T(256)(128)(2,1)}, u32[]{:S(2)}) copy-start(bf16[256]{0:T(256)(128)(2,1)} %param.31) | copy-start | bytes 1540
  7.2 19.0 %copy-start.19 = (bf16[256]{0:T(256)(128)(2,1)S(1)}, bf16[256]{0:T(256)(128)(2,1)}, u32[]{:S(2)}) copy-start(bf16[256]{0:T(256)(128)(2,1)} %param.32) | copy-start | bytes 1540
  7.2 19.0 %copy-start.20 = (bf16[256]{0:T(256)(128)(2,1)S(1)}, bf16[256]{0:T(256)(128)(2,1)}, u32[]{:S(2)}) copy-start(bf16[256]{0:T(256)(128)(2,1)} %param.33) | copy-start | bytes 1540
  7.3 19.0 %copy-start.21 = (bf16[256]{0:T(256)(128)(2,1)S(1)}, bf16[256]{0:T(256)(128)(2,1)}, u32[]{:S(2)}) copy-start(bf16[256]{0:T(256)(128)(2,1)} %param.37) | copy-start | bytes 1540
  7.3 19.2 %copy-start.4 = (bf16[2048,256]{1,0:T(8,128)(2,1)S(1)}, bf16[2048,256]{1,0:T(8,128)(2,1)}, u32[]{:S(2)}) copy-start(bf16[2048,256]{1,0:T(8,128)(2,1)} %param.20) | copy-start | bytes 3145732
  7.3 106.1 %all-gather.2.cloned.1.call-start = ((), (), s32[]{:S(2)}) async-start(), calls=%async_computation | async-start | bytes 4718592 | tf_op jit(solution)/shard_map/all_gather | solution.py:1068
  8.5 18.7 %copy-start.22 = (bf16[256]{0:T(256)(128)(2,1)S(1)}, bf16[256]{0:T(256)(128)(2,1)}, u32[]{:S(2)}) copy-start(bf16[256]{0:T(256)(128)(2,1)} %param.29) | copy-start | bytes 1540
  8.5 18.7 %copy-start.11 = (s32[1,2048]{1,0:T(1,128)S(1)}, s32[1,2048]{1,0:T(1,128)}, u32[]{:S(2)}) copy-start(s32[1,2048]{1,0:T(1,128)} %param.21) | copy-start | bytes 24580
  8.6 21.7 %copy-start.12 = (s32[1,2048]{1,0:T(1,128)S(1)}, s32[1,2048]{1,0:T(1,128)}, u32[]{:S(2)}) copy-start(s32[1,2048]{1,0:T(1,128)} %param.22) | copy-start | bytes 24580
  8.6 15.0 %collective-permute-start.6 = (bf16[128,2048]{1,0:T(8,128)(2,1)S(1)}, bf16[128,2048]{1,0:T(8,128)(2,1)S(1)}, u32[]{:S(2)}, u32[]{:S(2)}) collective-permute-start(bf16[128,2048]{1,0:T(8,128)(2,1)S(1)} %pad_maximum_fusion), channel_id=1, source_target_pairs={{0,2},{1,3},{2,0},{3,1},{4,6},{5,7},{6,4},{7,5},{8,10},{9,11},{10,... | collective-permute-start | bytes 1572872 | tf_op jit(solution)/shard_map/ppermute | solution.py:956
  24.4 8.9 %collective-permute-start.5 = (bf16[1024]{0:T(1024)(128)(2,1)S(1)}, bf16[1024]{0:T(1024)(128)(2,1)S(1)}, u32[]{:S(2)}, u32[]{:S(2)}) collective-permute-start(bf16[1024]{0:T(1024)(128)(2,1)S(1)} %copy-done.13), channel_id=1, source_target_pairs={{0,2},{1,3},{2,0},{3,1},{4,6},{5,7},{6,4},{7,5},{8,10},{9,11},{10,... | collective-permute-start | bytes 6152 | tf_op jit(solution)/shard_map/ppermute | solution.py:956
  26.3 7.0 %collective-permute-start = (bf16[6,1024]{1,0:T(8,128)(2,1)S(1)}, bf16[6,1024]{1,0:T(8,128)(2,1)S(1)}, u32[]{:S(2)}, u32[]{:S(2)}) collective-permute-start(bf16[6,1024]{1,0:T(8,128)(2,1)S(1)} %constant_dynamic-update-slice_fusion.5), channel_id=1, source_target_pairs={{0,1},{1,0},{2,3},{3,2},{4,5},{5,4},{6,7},{7,6},{8,9},{9,8},{10,11... | collective-permute-start | bytes 36872 | tf_op jit(solution)/shard_map/ppermute | solution.py:956
  26.5 85.9 %copy-start.10 = (bf16[4,1,256,256]{3,2,1,0:T(8,128)(2,1)}, bf16[4,1,256,256]{3,2,1,0:T(8,128)(2,1)S(1)}, u32[]{:S(2)}) copy-start(bf16[4,1,256,256]{3,2,1,0:T(8,128)(2,1)S(1)} %get-tuple-element.174) | copy-start | bytes 1572868
  26.5 15.3 %collective-permute-start.3 = (bf16[1024,256]{1,0:T(8,128)(2,1)S(1)}, bf16[1024,256]{1,0:T(8,128)(2,1)S(1)}, u32[]{:S(2)}, u32[]{:S(2)}) collective-permute-start(bf16[1024,256]{1,0:T(8,128)(2,1)S(1)} %bitcast.28), channel_id=1, source_target_pairs={{0,2},{1,3},{2,0},{3,1},{4,6},{5,7},{6,4},{7,5},{8,10},{9,11},{10,... | collective-permute-start | bytes 1572872 | tf_op jit(solution)/shard_map/ppermute | solution.py:956
  26.9 86.4 %collective-permute-start.2 = (bf16[1024,256]{1,0:T(8,128)(2,1)S(1)}, bf16[1024,256]{1,0:T(8,128)(2,1)}, u32[]{:S(2)}, u32[]{:S(2)}) collective-permute-start(bf16[1024,256]{1,0:T(8,128)(2,1)S(1)} %bitcast.25), channel_id=1, source_target_pairs={{0,1},{1,0},{2,3},{3,2},{4,5},{5,4},{6,7},{7,6},{8,9},{9,8},{10,11... | collective-permute-start | bytes 1572872 | tf_op jit(solution)/shard_map/ppermute | solution.py:956
  33.3 7.9 %collective-permute-start.1 = (bf16[6,1024]{1,0:T(8,128)(2,1)S(1)}, bf16[6,1024]{1,0:T(8,128)(2,1)S(1)}, u32[]{:S(2)}, u32[]{:S(2)}) collective-permute-start(bf16[6,1024]{1,0:T(8,128)(2,1)S(1)} %add_dynamic-update-slice_fusion), channel_id=1, source_target_pairs={{0,2},{1,3},{2,0},{3,1},{4,6},{5,7},{6,4},{7,5},{8,10},{9,11},{10,... | collective-permute-start | bytes 36872 | tf_op jit(solution)/shard_map/ppermute | solution.py:956
  41.9 70.6 %copy-start.15 = (bf16[1024,256]{1,0:T(8,128)(2,1)}, bf16[1024,256]{1,0:T(8,128)(2,1)S(1)}, u32[]{:S(2)}) copy-start(bf16[1024,256]{1,0:T(8,128)(2,1)S(1)} %collective-permute-done.3.d2) | copy-start | bytes 1572868
  41.9 71.4 %collective-permute-start.4 = (bf16[1024,256]{1,0:T(8,128)(2,1)S(1)}, bf16[1024,256]{1,0:T(8,128)(2,1)}, u32[]{:S(2)}, u32[]{:S(2)}) collective-permute-start(bf16[1024,256]{1,0:T(8,128)(2,1)S(1)} %collective-permute-done.3.d2), channel_id=1, source_target_pairs={{0,1},{1,0},{2,3},{3,2},{4,5},{5,4},{6,7},{7,6},{8,9},{9,8},{10,11... | collective-permute-start | bytes 1572872 | tf_op jit(solution)/shard_map/ppermute | solution.py:956
  276.3 25.5 %copy-start.9 = (bf16[1024,256]{1,0:T(8,128)(2,1)S(1)}, bf16[1024,256]{1,0:T(8,128)(2,1)}, u32[]{:S(2)}) copy-start(bf16[1024,256]{1,0:T(8,128)(2,1)} %wq.3) | copy-start | bytes 1572868
  278.7 4.3 %collective-permute-start.7 = (f32[2048]{0:T(1024)S(1)}, f32[2048]{0:T(1024)S(1)}, u32[]{:S(2)}, u32[]{:S(2)}) collective-permute-start(f32[2048]{0:T(1024)S(1)} %pad_maximum_fusion.1), channel_id=1, source_target_pairs={{0,2},{1,3},{2,0},{3,1},{4,6},{5,7},{6,4},{7,5},{8,10},{9,11},{10,... | collective-permute-start | bytes 24584 | tf_op jit(solution)/shard_map/ppermute | solution.py:956
  283.0 3.9 %collective-permute-start.8 = (f32[3200]{0:T(1024)S(1)}, f32[3200]{0:T(1024)S(1)}, u32[]{:S(2)}, u32[]{:S(2)}) collective-permute-start(f32[3200]{0:T(1024)S(1)} %constant_dynamic-update-slice_fusion), channel_id=1, source_target_pairs={{0,4},{4,0},{8,12},{12,8},{16,20},{20,16},{24,28},{28,24},{1,5},{5... | collective-permute-start | bytes 38408 | tf_op jit(solution)/shard_map/ppermute | solution.py:956
  286.9 3.7 %collective-permute-start.9 = (f32[3200]{0:T(1024)S(1)}, f32[3200]{0:T(1024)S(1)}, u32[]{:S(2)}, u32[]{:S(2)}) collective-permute-start(f32[3200]{0:T(1024)S(1)} %maximum_select_fusion.2), channel_id=1, source_target_pairs={{0,8},{4,12},{8,0},{12,4},{16,24},{20,28},{24,16},{28,20},{1,9},{5... | collective-permute-start | bytes 38408 | tf_op jit(solution)/shard_map/ppermute | solution.py:956
  286.9 10.6 %collective-permute-start.11 = (bf16[512,512]{1,0:T(8,128)(2,1)}, bf16[512,512]{1,0:T(8,128)(2,1)S(1)}, u32[]{:S(2)}, u32[]{:S(2)}) collective-permute-start(bf16[512,512]{1,0:T(8,128)(2,1)} %get-tuple-element.92), channel_id=1, source_target_pairs={{0,4},{4,0},{8,12},{12,8},{16,20},{20,16},{24,28},{28,24},{1,5},{5... | collective-permute-start | bytes 1572872 | tf_op jit(solution)/shard_map/ppermute | solution.py:956
  290.7 5.1 %collective-permute-start.10 = (f32[3200]{0:T(1024)S(1)}, f32[3200]{0:T(1024)S(1)}, u32[]{:S(2)}, u32[]{:S(2)}) collective-permute-start(f32[3200]{0:T(1024)S(1)} %maximum_select_fusion.1), channel_id=1, source_target_pairs={{0,16},{4,20},{8,24},{12,28},{16,0},{20,4},{24,8},{28,12},{1,17},{... | collective-permute-start | bytes 38408 | tf_op jit(solution)/shard_map/ppermute | solution.py:956
  293.6 14.8 %collective-permute-start.14 = (bf16[512,512]{1,0:T(8,128)(2,1)}, bf16[512,512]{1,0:T(8,128)(2,1)S(1)}, u32[]{:S(2)}, u32[]{:S(2)}) collective-permute-start(bf16[512,512]{1,0:T(8,128)(2,1)} %get-tuple-element.98), channel_id=1, source_target_pairs={{0,8},{4,12},{8,0},{12,4},{16,24},{20,28},{24,16},{28,20},{1,9},{5... | collective-permute-start | bytes 1572872 | tf_op jit(solution)/shard_map/ppermute | solution.py:956
  300.3 12.6 %collective-permute-start.12 = (bf16[256,512]{1,0:T(8,128)(2,1)}, bf16[256,512]{1,0:T(8,128)(2,1)S(1)}, u32[]{:S(2)}, u32[]{:S(2)}) collective-permute-start(bf16[256,512]{1,0:T(8,128)(2,1)} %get-tuple-element.94), channel_id=1, source_target_pairs={{0,8},{4,12},{8,0},{12,4},{16,24},{20,28},{24,16},{28,20},{1,9},{5... | collective-permute-start | bytes 786440 | tf_op jit(solution)/shard_map/ppermute | solution.py:956
  311.3 11.6 %collective-permute-start.15 = (bf16[256,512]{1,0:T(8,128)(2,1)}, bf16[256,512]{1,0:T(8,128)(2,1)S(1)}, u32[]{:S(2)}, u32[]{:S(2)}) collective-permute-start(bf16[256,512]{1,0:T(8,128)(2,1)} %get-tuple-element.100), channel_id=1, source_target_pairs={{0,16},{4,20},{8,24},{12,28},{16,0},{20,4},{24,8},{28,12},{1,17},{... | collective-permute-start | bytes 786440 | tf_op jit(solution)/shard_map/ppermute | solution.py:956
  313.6 19.4 %copy-start.3 = (bf16[2048,256]{1,0:T(8,128)(2,1)S(1)}, bf16[2048,256]{1,0:T(8,128)(2,1)}, u32[]{:S(2)}) copy-start(bf16[2048,256]{1,0:T(8,128)(2,1)} %get-tuple-element.220) | copy-start | bytes 3145732
  315.5 11.7 %collective-permute-start.13 = (bf16[128,512]{1,0:T(8,128)(2,1)}, bf16[128,512]{1,0:T(8,128)(2,1)S(1)}, u32[]{:S(2)}, u32[]{:S(2)}) collective-permute-start(bf16[128,512]{1,0:T(8,128)(2,1)} %get-tuple-element.96), channel_id=1, source_target_pairs={{0,16},{4,20},{8,24},{12,28},{16,0},{20,4},{24,8},{28,12},{1,17},{... | collective-permute-start | bytes 393224 | tf_op jit(solution)/shard_map/ppermute | solution.py:956
  325.4 5.2 %collective-permute-start.16 = (bf16[128,512]{1,0:T(8,128)(2,1)}, bf16[128,512]{1,0:T(8,128)(2,1)S(1)}, u32[]{:S(2)}, u32[]{:S(2)}) collective-permute-start(bf16[128,512]{1,0:T(8,128)(2,1)} %get-tuple-element.102), channel_id=1, source_target_pairs={{0,4},{4,0},{8,12},{12,8},{16,20},{20,16},{24,28},{28,24},{1,5},{5... | collective-permute-start | bytes 393224 | tf_op jit(solution)/shard_map/ppermute | solution.py:956
  (9 other events, 46.8 us)
Sparse Core Ops, SparseCore 0:
  24.5 74.8 all-gather.1

commit v4 on v3

--- a/solution.py
+++ b/solution.py
@@ -133,11 +133,13 @@
 
 
 def fwd_kernel(
-    x_any, x_own, vec, wq, wk, wv, bqv, wd, lo, pad, alibi,
-    p_ref, q_ref, k_ref, v_ref, linv_ref, ctx_ref, a_ref, b_ref, x1_ref, x2_ref, x3_ref, xm_ref, hm_ref,
+    x_any, g_any, x_own, own_vec, wq, wk, wv, bqv, wd, lo, pad, alibi,
+    p_ref, q_ref, k_ref, v_ref, linv_ref, ctx_ref, a_ref, b_ref, x1_ref, x2_ref, x3_ref, xm_ref, hm_ref, vec, bup_ref, dy_any,
     xs, qm_s, k_s, va_s, u_s, res_s, lo_s,
     xc, xy, xf, part_keep, part_send, part_got, sum_keep, sum_send, sum_got, whole_own, whole_got,
+    v_all,
     s_xc, r_xc, s_xy, r_xy, s_xf, r_xf, s_pc, r_pc, s_sy, r_sy, s_wc, r_wc,
+    s_v, r_v, l_d, s_dc, r_dc, s_dy, r_dy, s_df, r_df,
 ):
     step = pl.program_id(0)
     core, y, ranks = place()
@@ -163,12 +165,41 @@
     def whole_to_core(j):
         return remote(whole_own.at[j], whole_got.at[j], s_wc.at[j], r_wc.at[j], beside)
 
+    def vectors(r):
+        return remote(v_all.at[0], v_all.at[r], s_v.at[r - 1], r_v.at[r - 1], {"tensor": ranks[r]})
+
+    mine = feature_block(ranks[0])
+
+    def dy_own(j):
+        return pltpu.make_async_copy(g_any.at[rows(2 * j + y)], dy_any.at[rows(j), mine], l_d.at[j])
+
+    def dy_core(j):
+        return remote(g_any.at[rows(2 * j + y)], dy_any.at[rows(j), mine], s_dc.at[j], r_dc.at[j], beside)
+
+    def dy_y(j):
+        return remote(g_any.at[rows(2 * j + 1 - y)], dy_any.at[rows(j), mine], s_dy.at[j], r_dy.at[j], across)
+
+    def dy_forward(j):
+        block = dy_any.at[rows(j), feature_block(ranks[2])]
+        return remote(block, block, s_df.at[j], r_df.at[j], beside)
+
     @pl.when(step == 0)
     def _():
-        greet((beside, across))
+        v_all[0] = own_vec[...]
+        greet((beside, across, {"tensor": ranks[3]}))
+        for r in range(1, 4):
+            vectors(r).start()
         for b in range(3):
             to_y(b).start()
             to_core(b).start()
+        for r in range(1, 4):
+            vectors(r).wait_recv()
+        for r in range(4):
+            vec[:, feature_block(ranks[r])] = v_all[r, 0:8, :]
+        bup_ref[...] = jnp.zeros(bup_ref.shape, F32)
+        for n, r in enumerate((0, 2)):
+            for part in range(4):
+                bup_ref[n : n + 1, part * SHARE : (part + 1) * SHARE] = v_all[r, 8 + part : 9 + part, :]
         to_y(0).wait_recv()
         forward(0).start()
         hm_ref[...] = jnp.full(hm_ref.shape, NEG, F32)
@@ -183,6 +214,19 @@
     row_i = lax.broadcasted_iota(jnp.int32, (B, B), 0)
     col_i = lax.broadcasted_iota(jnp.int32, (B, B), 1)
     lanes = head_of_lane((B, SHARE))
+
+    for j in range(NB // 2):
+
+        @pl.when(step == j + 4)
+        def _():
+            dy_own(j).start()
+            dy_core(j).start()
+            dy_y(j).start()
+
+        @pl.when(step == j + 7)
+        def _():
+            dy_y(j).wait_recv()
+            dy_forward(j).start()
 
     @pl.when(step < NB - 1)
     def _():
@@ -310,9 +354,15 @@
         for j in range(NB // 2):
             sum_to_y(j).wait_send()
             whole_to_core(j).wait_send()
-
-
-def attention_forward(x, vec, wq, wk, wv, bqv, wd, lo, pad, alibi):
+            dy_own(j).wait()
+            dy_core(j).wait()
+            dy_y(j).wait_send()
+            dy_forward(j).wait()
+        for r in range(1, 4):
+            vectors(r).wait_send()
+
+
+def attention_forward(x, g, own_vec, wq, wk, wv, bqv, wd, lo, pad, alibi):
     last = lambda s: jnp.minimum(s, NB - 1)
     row = lambda width: pl.BlockSpec((B, width), lambda s: (last(s), 0))
     whole = lambda shape: pl.BlockSpec(shape, lambda s: (0,) * len(shape))
@@ -322,14 +372,16 @@
     return pl.pallas_call(
         fwd_kernel,
         grid=(NB + TAIL,),
-        in_specs=[pl.BlockSpec(memory_space=pl.ANY), row(SHARE), whole((8, D))]
+        in_specs=[pl.BlockSpec(memory_space=pl.ANY)] * 2
+        + [row(SHARE), whole((16, SHARE))]
         + [whole((D, SHARE))] * 3
         + [whole((8, SHARE)), whole((SHARE, D)), row(1), whole((8, SEQ)), whole((8, STRIP))],
         out_specs=[pl.BlockSpec((LH, B, STRIP), lambda s: (0, last(s), 0))]
         + [row(SHARE)] * 5
         + [whole((OWN, D // 2))] * 2
         + [row(SHARE)] * 3
-        + [whole((OWN, D)), whole((LH, 8, B))],
+        + [whole((OWN, D)), whole((LH, 8, B)), whole((8, D)), whole((8, UNITS))]
+        + [pl.BlockSpec(memory_space=pl.ANY)],
         scratch_shapes=[
             pltpu.VMEM((B, D), F32),
             pltpu.VMEM((LH, B, SHARE), BF),
@@ -343,44 +395,46 @@
         + [pltpu.VMEM((NB, B, D // 2), BF)] * 3
         + [pltpu.VMEM((half, B, D // 2), F32)]
         + [pltpu.VMEM((half, B, D // 2), BF)] * 4
+        + [pltpu.VMEM((4, 16, SHARE), F32)]
         + [dma(NB)] * 8
-        + [dma(half)] * 4,
+        + [dma(half)] * 4
+        + [dma(3)] * 2
+        + [dma(half)] * 7,
         out_shape=[like((LH, SEQ, STRIP), BF)]
         + [like((SEQ, SHARE), BF)] * 3
         + [like((SEQ, SHARE), F32), like((SEQ, SHARE), BF)]
         + [like((OWN, D // 2), BF)] * 2
         + [like((SEQ, SHARE), BF)] * 3
-        + [like((OWN, D), BF), like((LH, 8, B), F32)],
+        + [like((OWN, D), BF), like((LH, 8, B), F32), like((8, D), F32), like((8, UNITS), F32)]
+        + [like((OWN, D), BF)],
         compiler_params=remote_params(0),
         cost_estimate=pl.CostEstimate(
             flops=16 * 10**9, bytes_accessed=40 * 2**20, transcendentals=8 * 10**6
         ),
         name="attention_forward",
-    )(x, x, vec, wq, wk, wv, bqv, wd, lo, pad, alibi)
+    )(x, g, x, own_vec, wq, wk, wv, bqv, wd, lo, pad, alibi)
 
 
 def mlp_kernel(
-    a_own, a_par, xm, d0, d1, d2, d3, vec, bup, wu0, wu1, wd0, wd1,
+    a_own, a_par, xm, dy_s, vec, bup, wu0, wu1, wd0, wd1,
     mk_ref, ms_ref, gn_ref, h1_ref, gu_ref, su_ref, gd_ref, sd_ref, bs_ref, ru_ref,
-    n2_s, n2t_s, dy_s, dyt_s, am_s, ag_s, act_s, gp_s, us_s, s_u, r_u,
-    *, bit, chunk,
+    n2_s, n2t_s, dyt_s, am_s, ag_s, act_s, gp_s, us_s, s_u, r_u,
+    *, bits, chunk,
 ):
     i = pl.program_id(0)
     core, y, ranks = place()
-    partner = {"dp": dp_partner(bit)}
-
-    def send_up(n):
-        return remote(us_s.at[n], ru_ref.at[n], s_u.at[n], r_u.at[n], partner)
+    partners = [{"dp": dp_partner(bit)} for bit in bits]
+
+    def send_tile(n, kind):
+        return remote(us_s.at[n], ru_ref.at[n], s_u.at[n], r_u.at[n], partners[kind])
 
     @pl.when(i == 0)
     def _():
-        greet((partner,))
+        greet(partners)
 
         def assemble(rb, carry):
             rows = block_rows(rb)
             h1_ref[rows, :] = xm[rows, :].astype(F32)
-            for rank, d in zip(ranks, (d0, d1, d2, d3)):
-                dy_s[rows, feature_block(rank)] = d[rows, :]
             for part, a in ((core, a_own), (1 - core, a_par)):
                 for half in range(2):
                     cols = feature_block(2 * half + part)
@@ -421,20 +475,23 @@
         sums = lax.fori_loop(0, OWN // B, rows_of, jnp.zeros((1, TILE), F32))
         bs_ref[...] = jnp.broadcast_to(sums, bs_ref.shape)
 
-        def grads(j, carry):
-            to = pl.ds(pl.multiple_of(j * 128, 128), 128)
-            mine, other = piece(j, bit, chunk)
-            gu_ref[to, :] = dot(n2t_s[mine, :], gp_s[...]).astype(BF)
-            gd_ref[to, :] = dot(dyt_s[mine, :], act_s[...]).astype(BF)
-            us_s[i, to, :] = dot(n2t_s[other, :], gp_s[...]).astype(BF)
-            sd_ref[to, :] = dot(dyt_s[other, :], act_s[...]).astype(BF)
-            return carry
-
-        lax.fori_loop(0, D // 256, grads, 0)
-
-        @pl.when(i < 3)
-        def _():
-            send_up(i).start()
+        def grads(left, right, keep, send, bit):
+            def rows_of(j, carry):
+                to = pl.ds(pl.multiple_of(j * 128, 128), 128)
+                mine, other = piece(j, bit, chunk)
+                keep[to, :] = dot(left[mine, :], right[...]).astype(BF)
+                send[to, :] = dot(left[other, :], right[...]).astype(BF)
+                return carry
+
+            lax.fori_loop(0, D // 256, rows_of, 0)
+
+        first = which == 0
+        grads(n2t_s, gp_s, gu_ref, us_s.at[i] if first else su_ref, bits[0])
+        if first:
+            send_tile(i, 0).start()
+        grads(dyt_s, act_s, gd_ref, us_s.at[2 + i] if first else sd_ref, bits[1] if first else bits[0])
+        if first:
+            send_tile(2 + i, 1).start()
 
     pl.when(i < 2)(lambda: tile(wu0, wd0, 0))
     pl.when(i >= 2)(lambda: tile(wu1, wd1, 1))
@@ -443,23 +500,21 @@
     def _():
         split_store(mk_ref, ms_ref, am_s, core)
         gn_ref[...] = ag_s[...].astype(BF)
-        su_ref[...] = us_s[3]
-        for n in range(3):
-            send_up(n).wait()
-
-
-def feed_forward(a_own, a_par, xm, ds, vec, bup, wu0, wd0, w_other, bit, chunk):
+        for n in range(4):
+            send_tile(n, n // 2).wait()
+
+
+def feed_forward(a_own, a_par, xm, dy, vec, bup, wu0, wd0, w_other, bits, chunk):
     whole = lambda shape: pl.BlockSpec(shape, lambda i: (0,) * len(shape))
     low = lambda i: jnp.minimum(i, 1)
     high = lambda i: jnp.maximum(i - 2, 0)
     like = jax.ShapeDtypeStruct
     tile = pl.BlockSpec((D // 2, TILE), lambda i: (0, i))
     return pl.pallas_call(
-        functools.partial(mlp_kernel, bit=bit, chunk=chunk),
+        functools.partial(mlp_kernel, bits=bits, chunk=chunk),
         grid=(4,),
         in_specs=[whole((OWN, D // 2))] * 2
-        + [whole((OWN, D))]
-        + [whole((OWN, SHARE))] * 4
+        + [whole((OWN, D))] * 2
         + [
             whole((8, D)),
             whole((8, UNITS)),
@@ -472,123 +527,149 @@
         + [whole((OWN, D))] * 2
         + [
             tile,
-            whole((D // 2, TILE)),
+            pl.BlockSpec((D // 2, TILE), lambda i: (0, high(i))),
             tile,
-            tile,
+            pl.BlockSpec((D // 2, TILE), lambda i: (0, high(i))),
             pl.BlockSpec((8, TILE), lambda i: (0, i)),
             pl.BlockSpec(memory_space=pl.ANY),
         ],
         scratch_shapes=[
             pltpu.VMEM((OWN, D), BF),
             pltpu.VMEM((D, OWN), BF),
-            pltpu.VMEM((OWN, D), BF),
             pltpu.VMEM((D, OWN), BF),
             pltpu.VMEM((OWN, D), F32),
             pltpu.VMEM((OWN, D), F32),
             pltpu.VMEM((OWN, TILE), BF),
             pltpu.VMEM((OWN, TILE), BF),
             pltpu.VMEM((4, D // 2, TILE), BF),
-            pltpu.SemaphoreType.DMA((3,)),
-            pltpu.SemaphoreType.DMA((3,)),
+            pltpu.SemaphoreType.DMA((4,)),
+            pltpu.SemaphoreType.DMA((4,)),
         ],
         out_shape=[like((OWN, D // 2), BF)] * 2
         + [
             like((OWN, D), BF),
             like((OWN, D), F32),
             like((D // 2, 2 * UNITS), BF),
-            like((D // 2, TILE), BF),
+            like((D // 2, UNITS), BF),
             like((D // 2, 2 * UNITS), BF),
-            like((D // 2, 2 * UNITS), BF),
+            like((D // 2, UNITS), BF),
             like((8, 2 * UNITS), F32),
-            like((3, D // 2, TILE), BF),
+            like((4, D // 2, TILE), BF),
         ],
         compiler_params=remote_params(1),
         cost_estimate=pl.CostEstimate(
             flops=26 * 10**9, bytes_accessed=40 * 2**20, transcendentals=2 * 10**6
         ),
         name="feed_forward",
-    )(a_own, a_par, xm, *ds, vec, bup, wu0, w_other, wd0, w_other)
+    )(a_own, a_par, xm, dy, vec, bup, wu0, w_other, wd0, w_other)
 
 
 LEAD = 2
-FIRST = (0, 1, 1, 3, 4, 6, 8, 10)
-PAIRS = ((0, 2), (1, 7), (3, 5), (4, 6))
 FINAL = 3
+TILES = (("u", 0), ("u", 1), ("d", 0), ("d", 1), ("u", 2), ("d", 2), ("d", 3), ("u", 3), ("a", 0), ("a", 1))
+OTHER_ORDER = (2, 3, 9)
+FIRST = (0, 1, 0, 2, 3, 4, 6, 7)
+USE = sorted(range(8), key=lambda p: (FIRST[p], p)) + [8, 9]
+PAIRS = ((0, 4), (1, 7), (2, 5), (3, 6))
+DRAIN = LEAD + FINAL + NB
+
+
+def step_of(p, n):
+    return FIRST[p] + 3 * (n - 1) if p < 8 else DRAIN + n - 1
 
 
 def last_step(levels):
-    return FIRST[-1] + 2 * (levels - 1) + 1
+    return max(step_of(7, levels), step_of(8, levels))
 
 
 def bwd_kernel(
-    x0, x1, x2, x3, x_late, h1, gn, gn_any, mk, ms_any, d0, d1, d2, d3, gu, gd, ru, su_any, sd_any,
+    x0, x1, x2, x3, x_late, h1, gn, gn_any, mk, ms_any, dy_in, gu, gd, ru, su_any, sd_any, up_sums, hm,
     p_ref, q_ref, linv_ref, ctx_ref, k_ref, v_ref, vec, wq, wk, wv, wd,
-    out_ref, tg_ref, wu_ref, wdn_ref, ka_ref, sa_ref, kb_ref, sb_ref, cs_ref, bs_ref, n1_ref,
+    oo_ref, os_ref, tg_ref, wu_ref, wdn_ref, wqk_ref, wvd_ref, vt_ref,
     w_s, gh_s, gm_s, gt_s, qt_s, dl_s, ds_s, res_s, dkt_s, dvt_s, acc_s,
-    gn_got, mr_got, o_send, o_got, gh_own, gh_y, gh_f,
+    gn_got, mr_got, gh_own, gh_y, gh_f,
     part_keep, part_send, part_got, sum_keep, sum_send, sum_got, ghx_s, st_keep, st_got, st_sum, st_all,
-    gk, g1, y_send, y_got, *rest, order, bit_b, chunk,
+    gk, ru_s, g1, y_send, y_got, cs_ref, bs_ref, n1_ref, v_keep, v_send, v_away, v_sum, v_got,
+    *rest, orders, chunk,
 ):
-    levels = len(order)
+    levels = len(orders[0])
     stages = [rest[3 * n : 3 * n + 3] for n in range(levels - 1)]
     (
-        s_gn, r_gn, s_mr, r_mr, s_o, r_o, s_gy, r_gy, s_gf, r_gf, s_pc, r_pc, s_sy, r_sy,
-        s_tc, r_tc, s_ty, r_ty, s_g1, r_g1, s_yy, r_yy, l_g, l_w, *g_sems,
+        s_gn, r_gn, s_mr, r_mr, s_gy, r_gy, s_gf, r_gf, s_pc, r_pc, s_sy, r_sy,
+        s_tc, r_tc, s_ty, r_ty, s_g1, r_g1, s_yy, r_yy, l_g, l_r, s_gw, r_gw, s_va, r_va, s_vt, r_vt, *g_sems,
     ) = rest[3 * (levels - 1) :]
     step = pl.program_id(0)
     b = NB - 1 - (step - LEAD)
     core, y, ranks = place()
     beside, across = {"tensor": ranks[1]}, {"tensor": ranks[2]}
-    partners = [{"dp": dp_partner(bit)} for bit in order]
+    order_of = lambda p: orders[1 if p in OTHER_ORDER else 0]
+    partner = lambda bit: {"dp": dp_partner(bit)}
     half = NB // 2
     last = last_step(levels)
     lanes = head_of_lane((B, SHARE))
 
     send_gn = lambda j: remote(gn_any.at[block_rows(j)], gn_got.at[j], s_gn.at[j], r_gn.at[j], beside)
     send_mr = lambda j: remote(ms_any.at[block_rows(j)], mr_got.at[j], s_mr.at[j], r_mr.at[j], beside)
-    send_o = lambda j: remote(o_send.at[j], o_got.at[j], s_o.at[j], r_o.at[j], across)
     send_gy = lambda j, side: remote(
         gh_own.at[j, :, feature_block(2 * side + core)],
         gh_y.at[j, :, side * SHARE : (side + 1) * SHARE],
         s_gy.at[2 * j + side], r_gy.at[2 * j + side], across,
     )
     send_gf = lambda j: remote(gh_y.at[j], gh_f.at[j], s_gf.at[j], r_gf.at[j], beside)
-    send_part = lambda n: remote(part_send.at[lax.rem(n, 4)], part_got.at[n], s_pc.at[n], r_pc.at[n], beside)
+    send_part = lambda n: remote(part_send.at[lax.rem(n, 3)], part_got.at[n], s_pc.at[n], r_pc.at[n], beside)
     send_sum = lambda n: remote(sum_send.at[n], sum_got.at[n], s_sy.at[n], r_sy.at[n], across)
     send_tc = lambda n: remote(st_keep.at[n], st_got.at[n], s_tc.at[n], r_tc.at[n], beside)
     send_ty = lambda n: remote(st_sum.at[n], st_all.at[n], s_ty.at[n], r_ty.at[n], across)
 
     def tile_of(p):
-        up = p < 3 or p == 7
-        n = (p if p < 3 else 3) if up else p - 3
-        return slice(n * TILE, (n + 1) * TILE), up
+        kind, n = TILES[p]
+        return slice(n * TILE, (n + 1) * TILE), kind == "u"
 
     def send_first(p):
         cols, up = tile_of(p)
-        src = su_any if up else sd_any.at[:, cols]
-        return remote(src, g1.at[p - 3], s_g1.at[p - 3], r_g1.at[p - 3], partners[0])
+        src = (su_any if up else sd_any).at[:, slice(cols.start - UNITS, cols.stop - UNITS)]
+        return remote(src, g1.at[p - 4], s_g1.at[p - 4], r_g1.at[p - 4], partner(order_of(p)[0]))
+
+    def send_weights(p, part):
+        n = 2 * (p - 8) + part
+        return remote(
+            gn_got.at[p - 8, :, slice(part * TILE, (part + 1) * TILE)], g1.at[p - 4, block_rows(part)],
+            s_gw.at[n], r_gw.at[n], partner(order_of(p)[0]),
+        )
+
+    slot = [USE.index(p) % 2 for p in range(10)]
 
     def load_keep(p):
         cols, up = tile_of(p)
-        return pltpu.make_async_copy((gu if up else gd).at[:, cols], gk.at[p % 4], l_g.at[p % 4])
+        return pltpu.make_async_copy((gu if up else gd).at[:, cols], gk.at[slot[p]], l_g.at[slot[p]])
+
+    def load_got(p):
+        return pltpu.make_async_copy(ru.at[p], ru_s.at[slot[p]], l_r.at[slot[p]])
 
     def send_stage(p, n):
         _, send, got = stages[n - 1]
         return remote(
-            send.at[p % 4], got.at[p], g_sems[2 * n - 2].at[p], g_sems[2 * n - 1].at[p], partners[n]
+            send.at[p % 4], got.at[p], g_sems[2 * n - 2].at[p], g_sems[2 * n - 1].at[p], partner(order_of(p)[n])
         )
 
     send_last = lambda n: remote(y_send.at[n], y_got.at[n], s_yy.at[n], r_yy.at[n], across)
 
     def split(p, n):
+        order = order_of(p)
         if n == 1:
-            load_keep(p).wait()
-            keep = lambda rows: gk[p % 4, rows, :]
-            if p < 3:
-                got = lambda rows: ru[p, rows, :]
+            keep = lambda rows: gk[slot[p], rows, :]
+            if p < 4:
+                load_got(p).wait()
+                got = lambda rows: ru_s[slot[p], rows, :]
             else:
+                got = lambda rows: g1[p - 4, rows, :]
+            if p < 8:
+                load_keep(p).wait()
+            if 4 <= p < 8:
                 send_first(p).wait_recv()
-                got = lambda rows: g1[p - 3, rows, :]
+            if p >= 8:
+                send_weights(p, 0).wait_recv()
+                send_weights(p, 1).wait_recv()
         else:
             send_stage(p, n - 1).wait_recv()
             keep = lambda rows: stages[n - 2][0][p % 4, rows, :]
@@ -612,6 +693,8 @@
         send_stage(p, levels - 1).wait_recv()
         keep, _, got = stages[levels - 2]
         total = keep[p % 4].astype(F32) + got[p].astype(F32)
+        if p >= 8:
+            (wqk_ref, wvd_ref)[p - 8][...] = total
         for n, (own, other) in enumerate(PAIRS):
             cols, up = tile_of(own)
             if p == own:
@@ -627,14 +710,15 @@
 
     @pl.when(step == 0)
     def _():
-        greet([beside, across] + partners)
+        greet([beside, across] + [partner(bit) for bit in orders[0]])
         for j in range(half - 1, -1, -1):
             send_gn(j).start()
             send_mr(j).start()
-        for p in range(3, 8):
+        for p in range(4, 8):
             send_first(p).start()
-        for p in range(4):
+        for p in USE[:2]:
             load_keep(p).start()
+            load_got(p).start()
         cs_ref[...] = jnp.zeros(cs_ref.shape, F32)
         bs_ref[...] = jnp.zeros(bs_ref.shape, F32)
         n1_ref[...] = jnp.zeros(n1_ref.shape, F32)
@@ -647,9 +731,7 @@
         j = half - 1 - step
         send_gn(j).wait_recv()
         send_mr(j).wait_recv()
-        for rank, d in zip(ranks, (d0, d1, d2, d3)):
-            w_s[:, feature_block(rank)] = d[...].astype(F32)
-        dy = w_s[...]
+        dy = dy_in[...].astype(F32)
         value = h1[...]
 
         def out(side):
@@ -658,8 +740,8 @@
             total = mk[:, part].astype(F32) + mr_got[j, :, part].astype(F32)
             return (h1[:, cols] + total + vec[5:6, cols]).astype(BF)
 
-        out_ref[block_rows(2 * j + y), :] = out(y)
-        o_send[j] = out(1 - y)
+        oo_ref[...] = out(y)
+        os_ref[...] = out(1 - y)
         mean, rstd = row_stats(value)
         xhat = (value - mean) * rstd
         grad = gn[...].astype(F32) + gn_got[j].astype(F32)
@@ -672,7 +754,6 @@
         gh_own[j] = gh.astype(BF)
         send_gy(j, 0).start()
         send_gy(j, 1).start()
-        send_o(j).start()
 
     @pl.when((step >= LEAD) & (step < LEAD + NB))
     def _():
@@ -759,36 +840,46 @@
         send_tc(b).start()
         w_s[...] = grad
 
-        @pl.when(step >= LEAD + 4)
+        @pl.when(step >= LEAD + 3)
         def _():
-            send_part(b + 4).wait_send()
+            send_part(b + 3).wait_send()
 
         for n, side in enumerate((y, 1 - y)):
             cols = slice(n * SHARE, (n + 1) * SHARE)
             part_keep[lax.rem(b, 2), :, cols] = w_s[:, feature_block(2 * side + core)].astype(BF)
-            part_send[lax.rem(b, 4), :, cols] = w_s[:, feature_block(2 * side + 1 - core)].astype(BF)
+            part_send[lax.rem(b, 3), :, cols] = w_s[:, feature_block(2 * side + 1 - core)].astype(BF)
         send_part(b).start()
         ghx_s[lax.rem(b, 4)] = gh_s[:, feature_block(ranks[0])]
 
-    weights = ((0, ka_ref), (1, sa_ref), (2, kb_ref), (3, sb_ref))
-
-    def store_weights(n, ref, part):
-        cols = slice(part * 2 * SHARE, (part + 1) * 2 * SHARE)
-        return pltpu.make_async_copy(gn_got.at[n, :, cols], ref.at[block_rows(part)], l_w.at[2 * n + part])
-
     @pl.when(step == LEAD + NB - 1)
     def _():
-        for j in range(D // 256):
-            to = slice(j % 2 * 128, (j % 2 + 1) * 128)
-            into = slice(j // 2 * 2 * SHARE, (j // 2 + 1) * 2 * SHARE)
-            for n, (bit, cols) in enumerate(
-                ((order[0], slice(0, 2 * SHARE)), (bit_b, slice(2 * SHARE, 4 * SHARE)))
-            ):
-                for side, rows in enumerate(piece(j, bit, chunk)):
-                    gn_got[2 * n + side, to, into] = acc_s[rows, cols].astype(BF)
-        for n, ref in weights:
+        for p in (8, 9):
+            cols = slice((p - 8) * TILE, (p - 7) * TILE)
+            for j in range(D // 256):
+                mine, other = piece(j, order_of(p)[0], chunk)
+                gk[slot[p], j * 128 : (j + 1) * 128, :] = acc_s[mine, cols].astype(BF)
+                into = slice(j // 2 * TILE, (j // 2 + 1) * TILE)
+                gn_got[p - 8, j % 2 * 128 : (j % 2 + 1) * 128, into] = acc_s[other, cols].astype(BF)
             for part in range(2):
-                store_weights(n, ref, part).start()
+                send_weights(p, part).start()
+
+    send_away = lambda: remote(v_send, v_away, s_va.at[0], r_va.at[0], across)
+    send_total = lambda n: remote(
+        v_sum.at[n], v_got.at[n], s_vt.at[n], r_vt.at[n], partner(orders[0][n])
+    )
+
+    @pl.when(step == half)
+    def _():
+        for ref, rank, side in ((v_keep, ranks[0], 0), (v_send, ranks[2], UNITS)):
+            ref[0:4, :] = cs_ref[0:4, feature_block(rank)]
+            for n in range(4):
+                ref[4 + n : 5 + n, :] = up_sums[0:1, side + n * SHARE : side + (n + 1) * SHARE]
+        send_away().start()
+
+    @pl.when(step == half + 4)
+    def _():
+        send_away().wait_recv()
+        v_sum[0, 0:8, :] = v_keep[...] + v_away[...]
 
     @pl.when((step >= LEAD + 1) & (step < LEAD + 1 + NB))
     def _():
@@ -796,7 +887,7 @@
         send_part(n).wait_recv()
         send_tc(n).wait_recv()
         keep = part_keep[lax.rem(n, 2)].astype(F32)
-        sum_keep[lax.rem(n, 4)] = keep[:, :SHARE] + part_got[n, :, :SHARE].astype(F32)
+        sum_keep[lax.rem(n, 3)] = keep[:, :SHARE] + part_got[n, :, :SHARE].astype(F32)
         sum_send[n] = (keep[:, SHARE:] + part_got[n, :, SHARE:].astype(F32)).astype(BF)
         st_sum[n] = st_keep[n] + st_got[n]
         send_sum(n).start()
@@ -807,7 +898,7 @@
         n = b + FINAL
         send_sum(n).wait_recv()
         send_ty(n).wait_recv()
-        grad = sum_keep[lax.rem(n, 4)] + sum_got[n].astype(F32)
+        grad = sum_keep[lax.rem(n, 3)] + sum_got[n].astype(F32)
         row = lax.broadcasted_iota(jnp.int32, (8, B), 0)
         stats = jnp.where(row < 2, st_sum[n] + st_all[n], st_keep[n])
         stats = jnp.concatenate([stats] * 16, axis=0).T
@@ -818,6 +909,32 @@
         n1_ref[0:1, :] += jnp.sum(grad * xhat, axis=0, keepdims=True)
         n1_ref[1:2, :] += jnp.sum(grad, axis=0, keepdims=True)
 
+    row16 = lax.broadcasted_iota(jnp.int32, (16, SHARE), 0)
+
+    @pl.when(step == DRAIN - 1)
+    def _():
+        v_sum[0, 8:10, :] = n1_ref[0:2, :]
+        v_sum[0, 10:12, :] = bs_ref[0:2, :]
+        lane = lax.broadcasted_iota(jnp.int32, (4, SHARE), 1)
+        top = jnp.full((4, SHARE), NEG, F32)
+        for h in range(LH):
+            top = jnp.where(lane == h, jnp.max(hm[h]), top)
+        v_sum[0, 12:16, :] = top
+        send_total(0).start()
+
+    for n in range(levels):
+
+        @pl.when(step == DRAIN + n)
+        def _():
+            send_total(n).wait_recv()
+            mine, other = v_sum[n], v_got[n]
+            total = jnp.where(row16 < 12, mine + other, jnp.maximum(mine, other))
+            if n == levels - 1:
+                vt_ref[...] = total
+            else:
+                v_sum[n + 1] = total
+                send_total(n + 1).start()
+
     for j in range(half - 1, -1, -1):
 
         @pl.when(step == half - j)
@@ -826,44 +943,50 @@
             send_gy(j, 1).wait_recv()
             send_gf(j).start()
 
-    for p in range(8):
+    for p in range(10):
         for n in range(1, levels):
-            pl.when(step == FIRST[p] + 2 * (n - 1))(functools.partial(split, p, n))
-        if p >= 4:
-            pl.when(step == FIRST[p - 4] + 1)(lambda p=p: load_keep(p).start())
-        pl.when(step == FIRST[p] + 2 * (levels - 1))(functools.partial(whole_tile, p))
-    for n, pair in enumerate(PAIRS):
-        pl.when(step == max(FIRST[p] for p in pair) + 2 * (levels - 1) + 1)(functools.partial(close, n))
+            pl.when(step == step_of(p, n))(functools.partial(split, p, n))
+        pl.when(step == step_of(p, levels))(functools.partial(whole_tile, p))
+
+    def load_next(p):
+        load_keep(p).start()
+        if p < 4:
+            load_got(p).start()
+
+    for n in range(2, 8):
+        pl.when(step == FIRST[USE[n - 2]])(functools.partial(load_next, USE[n]))
 
     @pl.when(step == last)
     def _():
         for j in range(half):
-            send_o(j).wait_recv()
-            out_ref[block_rows(2 * j + 1 - y), :] = o_got[j]
-            for copy in (send_gn, send_mr, send_o, send_gf, send_last, send_part):
+            close(j)
+            for copy in (send_gn, send_mr, send_gf, send_last):
                 copy(j).wait_send()
             for side in range(2):
                 send_gy(j, side).wait_send()
             for level in range(1, levels):
-                send_stage(4 + j, level).wait_send()
+                send_stage(6 + j, level).wait_send()
         for n in range(NB):
             for copy in (send_sum, send_tc, send_ty):
                 copy(n).wait_send()
-        for p in range(3, 8):
+        for n in range(3):
+            send_part(n).wait_send()
+        for p in range(4, 8):
             send_first(p).wait_send()
-        for n, ref in weights:
+        for p in (8, 9):
             for part in range(2):
-                store_weights(n, ref, part).wait()
+                send_weights(p, part).wait_send()
+        send_away().wait_send()
+        for n in range(levels):
+            send_total(n).wait_send()
 
 
 def attention_backward(
-    xs, h1, gn, mk, ms, ds, gu, gd, ru, su, sd, p, q, linv, ctx, k, v, vec, wq, wk, wv, wd,
-    order, bit_b, chunk,
+    xs, h1, gn, mk, ms, dy, gu, gd, ru, su, sd, up_sums, hm, p, q, linv, ctx, k, v, vec, wq, wk, wv, wd,
+    orders, chunk,
 ):
-    levels = len(order)
+    levels = len(orders[0])
     half = NB // 2
-    steps = max(last_step(levels), LEAD + FINAL + NB - 1) + 1
-    assert steps == last_step(levels) + 1
     block = lambda s: jnp.clip(NB - 1 + LEAD - s, 0, NB - 1)
     late = lambda s: jnp.clip(NB - 1 + LEAD + FINAL - s, 0, NB - 1)
     row = lambda width: pl.BlockSpec((B, width), lambda s: (block(s), 0))
@@ -876,23 +999,24 @@
     dma = lambda n: pltpu.SemaphoreType.DMA((n,))
     final_late = pl.BlockSpec((B, SHARE), lambda s: (late(s), 0))
     return pl.pallas_call(
-        functools.partial(bwd_kernel, order=order, bit_b=bit_b, chunk=chunk),
-        grid=(steps,),
+        functools.partial(bwd_kernel, orders=orders, chunk=chunk),
+        grid=(last_step(levels) + 1,),
         in_specs=[row(SHARE)] * 4
         + [final_late, own(D), own(D), anywhere, own(D // 2), anywhere]
-        + [own(SHARE)] * 4
+        + [own(D)]
         + [anywhere] * 2
-        + [whole(3, D // 2, TILE), anywhere, anywhere]
+        + [anywhere] * 3
+        + [whole(8, 2 * UNITS), whole(LH, 8, B)]
         + [pl.BlockSpec((LH, B, STRIP), lambda s: (0, block(s), 0))]
         + [row(SHARE)] * 3
         + [whole(SEQ, SHARE)] * 2
         + [whole(8, D)]
         + [whole(D, SHARE)] * 3
         + [whole(SHARE, D)],
-        out_specs=[whole(SEQ, SHARE), final_late]
+        out_specs=[own(SHARE), own(SHARE), final_late]
         + [whole(chunk, UNITS)] * 2
-        + [anywhere] * 4
-        + [whole(8, D), whole(8, SHARE), whole(8, SHARE)],
+        + [whole(chunk, TILE)] * 2
+        + [whole(16, SHARE)],
         scratch_shapes=[
             vmem(B, D, dtype=F32),
             vmem(B, D),
@@ -907,15 +1031,13 @@
             vmem(D, 4 * SHARE, dtype=F32),
             vmem(half, B, D),
             vmem(half, B, D // 2),
-            vmem(half, B, SHARE),
-            vmem(half, B, SHARE),
             vmem(half, B, D),
             vmem(half, B, D // 2),
             vmem(half, B, D // 2),
             vmem(2, B, D // 2),
-            vmem(4, B, D // 2),
+            vmem(3, B, D // 2),
             vmem(NB, B, D // 2),
-            vmem(4, B, SHARE, dtype=F32),
+            vmem(3, B, SHARE, dtype=F32),
             vmem(NB, B, SHARE),
             vmem(NB, B, SHARE),
             vmem(4, B, SHARE),
@@ -923,31 +1045,44 @@
             vmem(NB, 8, B, dtype=F32),
             vmem(NB, 8, B, dtype=F32),
             vmem(NB, 8, B, dtype=F32),
-            vmem(4, D // 2, TILE),
-            vmem(5, D // 2, TILE),
+            vmem(2, D // 2, TILE),
+            vmem(2, D // 2, TILE),
+            vmem(6, D // 2, TILE),
             vmem(half, chunk, TILE),
             vmem(half, chunk, TILE),
+            vmem(8, D, dtype=F32),
+            vmem(8, SHARE, dtype=F32),
+            vmem(8, SHARE, dtype=F32),
+            vmem(8, SHARE, dtype=F32),
+            vmem(8, SHARE, dtype=F32),
+            vmem(8, SHARE, dtype=F32),
+            vmem(levels, 16, SHARE, dtype=F32),
+            vmem(levels, 16, SHARE, dtype=F32),
         ]
-        + [vmem(slots, D >> (n + 1), TILE) for n in range(1, levels) for slots in (4, 4, 8)]
-        + [dma(half)] * 6
+        + [vmem(slots, D >> (n + 1), TILE) for n in range(1, levels) for slots in (4, 4, 10)]
+        + [dma(half)] * 4
         + [dma(NB)] * 2
         + [dma(half)] * 2
         + [dma(NB)] * 8
-        + [dma(5)] * 2
-        + [dma(half)] * 3
-        + [dma(8)]
-        + [dma(8)] * (2 * (levels - 1)),
-        out_shape=[like((SEQ, SHARE), BF), like((SEQ, SHARE), F32)]
+        + [dma(4)] * 2
+        + [dma(half)] * 2
+        + [dma(2)] * 2
+        + [dma(4)] * 2
+        + [dma(1)] * 2
+        + [dma(levels)] * 2
+        + [dma(10)] * (2 * (levels - 1)),
+        out_shape=[like((OWN, SHARE), BF)] * 2
+        + [like((SEQ, SHARE), F32)]
         + [like((chunk, UNITS), F32)] * 2
-        + [like((D // 2, 2 * SHARE), BF)] * 4
-        + [like((8, D), F32), like((8, SHARE), F32), like((8, SHARE), F32)],
+        + [like((chunk, TILE), F32)] * 2
+        + [like((16, SHARE), F32)],
         compiler_params=remote_params(2),
         cost_estimate=pl.CostEstimate(
             flops=30 * 10**9, bytes_accessed=50 * 2**20, transcendentals=0
         ),
         name="backward",
     )(
-        *xs, xs[0], h1, gn, gn, mk, ms, *ds, gu, gd, ru, su, sd, p, q, linv, ctx, k, v, vec, wq, wk, wv, wd
+        *xs, xs[0], h1, gn, gn, mk, ms, dy, gu, gd, ru, su, sd, up_sums, hm, p, q, linv, ctx, k, v, vec, wq, wk, wv, wd
     )
 
 
@@ -964,68 +1099,8 @@
     return bits
 
 
-def dp_total(value):
-    for bit in dp_bits():
-        value = value + swap(value, "dp", bit)
-    return value
-
-
 def pick(value, axis, index):
     return lax.dynamic_index_in_dim(value, index, axis, keepdims=False)
-
-
-def sum_kernel(bit, km, rm, ko, ro, keep_ref, send_ref):
-    for a, b, ref in ((km, rm, keep_ref), (ko, ro, send_ref)):
-        ref[...] = (a[...].astype(F32) + b[...].astype(F32)).astype(ref.dtype)
-
-
-def sum_and_split(bit, keep, other, inner, after=()):
-    rows, cols = keep.shape
-    step = min(inner, 128)
-    per = inner // step
-    block = lambda side: pl.BlockSpec(
-        (step, cols),
-        lambda i, bit: (i // per * 2 * per + (bit[0] if side else 1 - bit[0]) * per + i % per, 0),
-    )
-    out = pl.BlockSpec((step, cols), lambda i, bit: (i, 0))
-    return pl.pallas_call(
-        ordered(sum_kernel, len(after)),
-        grid_spec=pltpu.PrefetchScalarGridSpec(
-            num_scalar_prefetch=1,
-            grid=(rows // 2 // step,),
-            in_specs=waits(after) + [block(True), block(True), block(False), block(False)],
-            out_specs=[out, out],
-        ),
-        out_shape=[jax.ShapeDtypeStruct((rows // 2, cols), BF)] * 2,
-        compiler_params=params(),
-        cost_estimate=pl.CostEstimate(flops=rows * cols, bytes_accessed=6 * rows * cols, transcendentals=0),
-        name="sum_and_split",
-    )(bit, *after, keep, other, keep, other)
-
-
-def dp_scatter(keep, send, order, after=()):
-    rank = lax.axis_index("dp")
-    chunk = D // lax.axis_size("dp")
-    for n, bit in enumerate(order):
-        other = swap(send, "dp", bit)
-        if n == len(order) - 1:
-            yield keep.astype(F32) + other.astype(F32)
-            return
-        following = order[n + 1]
-        inner = chunk
-        for b in order[n + 2 :]:
-            inner *= 2 if b < following else 1
-        wait = yield send
-        mine = ((rank // following) % 2)[None]
-        keep, send = sum_and_split(mine, keep, other, inner, wait or ())
-
-
-def finish(steps, after=()):
-    try:
-        while True:
-            value = steps.send(after)
-    except StopIteration:
-        return value
 
 
 def shards(
@@ -1057,17 +1132,18 @@
     y_swap = lambda value: swap(value, "tensor", 2)
     rows8 = lambda value: jnp.pad(value, ((0, 8 - value.shape[0]), (0, 0)))
 
-    vectors = jnp.stack([norm1_gain, norm1_bias, dense_bias, norm2_gain, norm2_bias, down_bias])
-    vec = lax.dynamic_update_slice(jnp.zeros((6, D), BF), vectors, (0, t * SHARE))
-    vec = vec + core_swap(vec)
-    vec = rows8((vec + y_swap(vec)).astype(F32))
+    own_vec = jnp.concatenate(
+        [
+            jnp.stack([norm1_gain, norm1_bias, dense_bias, norm2_gain, norm2_bias, down_bias, down_bias, down_bias]),
+            b_up.reshape(4, SHARE),
+            b_up.reshape(4, SHARE),
+        ]
+    ).astype(F32)
 
     part = D // size
     cut = lambda w: lax.dynamic_slice_in_dim(w, rank * part, part, 0)
     w_part = y_swap(jnp.concatenate([cut(w_up), cut(w_down)], axis=1))
     w_other = lax.all_gather(w_part, "dp", axis=0, tiled=True)
-    b_up_pair = jnp.stack([b_up, y_swap(b_up)]).astype(F32)
-
     seg = segments.reshape(SEQ)
     index = jnp.arange(SEQ, dtype=jnp.int32)
     first = jnp.zeros((SEQ,), jnp.int32)
@@ -1079,73 +1155,48 @@
     slopes = jnp.exp2(-8.0 * (heads.astype(F32) + 1.0) / HEADS)
     alibi = rows8(slopes[:, None] * (jnp.arange(STRIP) - (STRIP - 1)).astype(F32)[None, :])
 
-    by_y = lambda value, which: pick(value.reshape(NB // 2, 2, B, value.shape[-1]), 1, which).reshape(
-        OWN, value.shape[-1]
-    )
-    d_own = by_y(out_grad, y)
-    d_send = by_y(out_grad, 1 - y)
-
-    p, q, k, v, linv, ctx, a_own, a_par, x1, x2, x3, xm, hm = attention_forward(
-        tokens, vec, w_query, w_key, w_value,
+    p, q, k, v, linv, ctx, a_own, a_par, x1, x2, x3, xm, hm, vec, b_up_pair, dy = attention_forward(
+        tokens, out_grad, own_vec, w_query, w_key, w_value,
         rows8(jnp.stack([b_query, b_value]).astype(F32)), w_dense,
         lowest.reshape(SEQ, 1), pad_row, alibi,
     )
     xs = [tokens, x1, x2, x3]
 
-    d_y = y_swap(d_send)
-    ds = [d_own, core_swap(d_own), d_y, core_swap(d_y)]
-
     bits = dp_bits()
     order_a = bits if size == 8 else bits[::-1]
     order_b = [2, 4, 1] if size == 8 else [bits[-2], bits[-1], *bits[:-2][::-1]]
-    mk, ms, gn, h1, gu, su, gd, sd, bs, ru = feed_forward(
-        a_own, a_par, xm, ds, vec, rows8(b_up_pair), w_up, w_down, w_other, order_a[0], part
+    mk, ms, gn, h1, gu, su, gd, sd, up_sums, ru = feed_forward(
+        a_own, a_par, xm, dy, vec, b_up_pair, w_up, w_down, w_other, (order_a[0], order_b[0]), part
     )
-    output, tokens_grad, w_up_grad, w_down_grad, ka, sa, kb, sb, cs, qv, n1s = attention_backward(
-        xs, h1, gn, mk, ms, ds, gu, gd, ru, su, sd, p, q, linv, ctx, k, v, vec,
-        w_query, w_key, w_value, w_dense, order_a, order_b[0], part,
+    out_own, out_send, tokens_grad, w_up_grad, w_down_grad, g_qk, g_vd, sums = attention_backward(
+        xs, h1, gn, mk, ms, dy, gu, gd, ru, su, sd, up_sums, hm, p, q, linv, ctx, k, v, vec,
+        w_query, w_key, w_value, w_dense, (order_a, order_b), part,
     )
     w_down_grad = w_down_grad.T
-
-    steps_a = dp_scatter(ka, sa, order_a)
-    steps_b = dp_scatter(kb, sb, order_b)
-    next(steps_a), next(steps_b)
-    g_qk = finish(steps_a, ())
-    g_vd = finish(steps_b, ())
-
-    cs4 = pick(cs[0:4].reshape(4, 2, 2, SHARE), 2, core)
-    early = jnp.concatenate([pick(cs4, 1, y).reshape(-1), bs[0, :UNITS]])
-    apart = jnp.concatenate([pick(cs4, 1, 1 - y).reshape(-1), bs[0, UNITS:]])
-    early = early + y_swap(apart)
-    late = jnp.concatenate([n1s[0], n1s[1], qv[0], qv[1]])
-    packed = jnp.concatenate([early, late, jnp.pad(jnp.max(hm, axis=(1, 2)), (0, 124))])
-    summed = lax.broadcasted_iota(jnp.int32, packed.shape, 0) < packed.shape[0] - 128
-    for bit in bits:
-        other = swap(packed, "dp", bit)
-        packed = jnp.where(summed, packed + other, jnp.maximum(packed, other))
-    early, late, head_max = jnp.split(packed, (8 * SHARE, 12 * SHARE))
-    head_max = head_max[:LH]
-    of = lambda value, n: value[n * SHARE : (n + 1) * SHARE]
-
+    out_y = y_swap(out_send)
+    pair = jnp.stack([out_own, out_y]).reshape(2, NB // 2, B, SHARE)
+    output = jnp.where(y == 0, pair, pair[::-1]).transpose(1, 0, 2, 3).reshape(SEQ, SHARE)
+
+    head_max = sums[12, :LH]
     column_scale = jnp.repeat(jnp.sqrt(TAU / jnp.maximum(head_max, TAU)), HD)
     return (
         output,
         tokens_grad,
-        of(late, 0),
-        of(late, 1),
+        sums[8],
+        sums[9],
         g_qk[:, :SHARE],
-        of(late, 2),
+        sums[10],
         g_qk[:, SHARE:],
         g_vd[:, :SHARE],
-        of(late, 3),
+        sums[11],
         g_vd[:, SHARE:].T,
-        of(early, 2),
-        of(early, 0),
-        of(early, 1),
+        sums[2],
+        sums[0],
+        sums[1],
         w_up_grad,
-        early[4 * SHARE :],
+        sums[4:8].reshape(UNITS),
         w_down_grad,
-        of(early, 3),
+        sums[3],
         head_max,
         w_query.astype(F32) * column_scale,
         b_query.astype(F32) * column_scale,

time: 344 us -> 309 us (0.90)
  starting transfers between devices: 20.3 us -> 3.27 us
  waiting for transfers between devices: 36.1 us -> 19.1 us
  Pallas kernels: 241 us -> 246 us
    ppermute x17 -> x2, starting transfers between devices: 20.2 us -> 3.23 us  [swap(): return lax.ppermute(value, axis, [(i, i ^ bit) for i in range(size)])]
    ppermute x17 -> x2, waiting for transfers between devices: 36.1 us -> 19.1 us  [swap(): return lax.ppermute(value, axis, [(i, i ^ bit) for i in range(size)])]
    pallas_call x1, Pallas kernels: 70.5 us -> 76.6 us  [attention_forward(): pl.pallas_call(fwd_kernel, grid=(NB + TAIL,), in_specs=[pl.BlockSpec(memo...]
    unnamed x55 -> x42, local copies, waits for them, and re-layouts: 9.84 us -> 7.92 us
    pallas_call x6 -> x2, Pallas kernels: 171 us -> 170 us  [the longest x1 117 us: attention_backward(): pl.pallas_call(functools.partial(bwd_kernel, orders=orders, chunk=chunk),...]
  transfers between devices with their start and end apart: 18 -> 3, of which waited for: 10 -> 2; matrix products, arithmetic and copies ran while one was open for 5% -> 3% of each run, Pallas kernels for 23% -> 25%
where the time goes in v4:
time: 309 us; the launch traced here: 308 us
  Pallas kernels  246 us (80%)
  waiting for transfers between devices  19.1 us (6%)
  local copies, waits for them, and re-layouts  16.7 us (5%)
  between operations  14.4 us (5%)
  other arithmetic  8.73 us (3%)
  starting transfers between devices  3.27 us (1%)
    pallas_call x1, Pallas kernels, attention_backward(): pl.pallas_call(functools.partial(bwd_kernel, orders=orders, chunk=chunk),...  117 us
    pallas_call x1, Pallas kernels, attention_forward(): pl.pallas_call(fwd_kernel, grid=(NB + TAIL,), in_specs=[pl.BlockSpec(memo...  76.6 us
    pallas_call x1, Pallas kernels, feed_forward(): pl.pallas_call(functools.partial(mlp_kernel, bits=bits, chunk=chunk), gri...  52.4 us
    ppermute x2, waiting for transfers between devices, swap(): return lax.ppermute(value, axis, [(i, i ^ bit) for i in range(size)])  19.1 us
    unnamed x42, local copies, waits for them, and re-layouts  7.92 us
  transfers between devices with their start and end apart: 3, of which 2 were waited for; matrix products, arithmetic and copies ran while one was open for 3% of the time, Pallas kernels for 25%

profile of v4, /device:TPU:0, one launch (start us, length us, event | category | flops | bytes accessed | tf_op | source)
XLA Modules:
  0.0 308.4 jit_solution(16272760507454496900)
XLA Ops:
  7.4 1.1 constant_dynamic-slice_fusion
  8.5 3.0 collective-permute-start
  11.5 11.9 %collective-permute-done = bf16[128,2048]{1,0:T(8,128)(2,1)S(1)} collective-permute-done((bf16[128,2048]{1,0:T(8,128)(2,1)S(1)}, bf16[128,2048]{1,0:T(8,128)(2,1)S(1)}, u32[]{:S(2)}, u32[]{:S(2)}) %collective-permute-start) | collective-permute-done | bytes 524320 | tf_op jit(solution)/shard_map/ppermute | solution.py:1091
  23.4 0.8 copy-done.1
  24.5 0.6 convert_element_type.45.own_vec
  25.2 0.6 pad.17.alibi
  25.9 0.6 pad.16
  26.5 0.7 fusion.2
  27.2 2.0 fusion.1
  29.2 0.4 copy.48
  29.5 0.6 fusion.8.bqv
  30.1 1.1 add_maximum_fusion.lo
  31.2 76.6 %attention_forward.1 = (bf16[4,2048,1280]{2,1,0:T(8,128)(2,1)}, bf16[2048,256]{1,0:T(8,128)(2,1)}, bf16[2048,256]{1,0:T(8,128)(2,1)}, bf16[2048,256]{1,0:T(8,128...) custom-call(bf16[2048,256]{1,0:T(8,128)(2,1)} %x_late.1, ...), custom_call_target="tpu_custom_call" | custom-call | flops 16000000000 | bytes 41943040 | tf_op jit(solution)/shard_map/attention_forward/pallas_call | solution.py:372
  107.9 52.4 %feed_forward.1 = (bf16[1024,512]{1,0:T(8,128)(2,1)}, bf16[1024,512]{1,0:T(8,128)(2,1)}, bf16[1024,1024]{1,0:T(8,128)(2,1)}, f32[1024,1024]{1,0:T(8,128)}, bf16[...) custom-call(bf16[1024,512]{1,0:T(8,128)(2,1)} %get-tuple-element.58., ...), custom_call_target="tpu_custom_call" | custom-call | flops 25999998976 | bytes 41943040 | tf_op jit(solution)/shard_map/feed_forward/pallas_call | solution.py:513
  160.4 117.1 %backward.1 = (bf16[1024,256]{1,0:T(8,128)(2,1)}, bf16[1024,256]{1,0:T(8,128)(2,1)}, f32[2048,256]{1,0:T(8,128)}, f32[128,1024]{1,0:T(8,128)}, f32[128,1024]{1,0...) custom-call(bf16[2048,256]{1,0:T(8,128)(2,1)} %x_late.1, ...), custom_call_target="tpu_custom_call" | custom-call | flops 30000001024 | bytes 52428800 | tf_op jit(solution)/shard_map/backward/pallas_call | solution.py:1001
  277.5 1.3 divide_sqrt_fusion
  278.8 0.7 slice_bitcast_fusion.1
  279.5 1.4 fusion.10
  281.1 0.6 copy.52
  281.7 1.7 fusion.9
  283.4 1.6 slice_bitcast_fusion
  285.0 0.8 copy.50
  285.8 2.1 copy.51
  287.9 0.2 collective-permute-start.1
  288.1 0.6 convert_multiply_fusion.2
  288.6 1.5 convert_multiply_fusion
  290.1 7.2 %collective-permute-done.1 = bf16[1024,256]{1,0:T(8,128)(2,1)S(1)} collective-permute-done((bf16[1024,256]{1,0:T(8,128)(2,1)S(1)}, bf16[1024,256]{1,0:T(8,128)(2,1)S(1)}, u32[]{:S(2)}, u32[]{:S(2)}) %collective-permute-start.1) | collective-permute-done | bytes 524320 | tf_op jit(solution)/shard_map/ppermute | solution.py:1091
  297.4 0.2 fusion
  297.6 1.0 copy.49
  298.6 0.7 copy-done
  299.4 1.3 copy.55
  300.8 0.8 copy.56
  (55 shorter events, 0.7 us)
Async XLA Ops:
  7.2 17.1 %copy-start.11 = (bf16[256]{0:T(256)(128)(2,1)S(1)}, bf16[256]{0:T(256)(128)(2,1)}, u32[]{:S(2)}) copy-start(bf16[256]{0:T(256)(128)(2,1)} %param.23) | copy-start | bytes 1540
  7.2 17.1 %copy-start.12 = (bf16[256]{0:T(256)(128)(2,1)S(1)}, bf16[256]{0:T(256)(128)(2,1)}, u32[]{:S(2)}) copy-start(bf16[256]{0:T(256)(128)(2,1)} %param.24) | copy-start | bytes 1540
  7.2 17.1 %copy-start.13 = (bf16[256]{0:T(256)(128)(2,1)S(1)}, bf16[256]{0:T(256)(128)(2,1)}, u32[]{:S(2)}) copy-start(bf16[256]{0:T(256)(128)(2,1)} %param.29) | copy-start | bytes 1540
  7.2 17.1 %copy-start.14 = (bf16[256]{0:T(256)(128)(2,1)S(1)}, bf16[256]{0:T(256)(128)(2,1)}, u32[]{:S(2)}) copy-start(bf16[256]{0:T(256)(128)(2,1)} %param.31) | copy-start | bytes 1540
  7.2 17.1 %copy-start.15 = (bf16[256]{0:T(256)(128)(2,1)S(1)}, bf16[256]{0:T(256)(128)(2,1)}, u32[]{:S(2)}) copy-start(bf16[256]{0:T(256)(128)(2,1)} %param.32) | copy-start | bytes 1540
  7.2 17.1 %copy-start.16 = (bf16[256]{0:T(256)(128)(2,1)S(1)}, bf16[256]{0:T(256)(128)(2,1)}, u32[]{:S(2)}) copy-start(bf16[256]{0:T(256)(128)(2,1)} %param.33) | copy-start | bytes 1540
  7.3 17.1 %copy-start.17 = (bf16[256]{0:T(256)(128)(2,1)S(1)}, bf16[256]{0:T(256)(128)(2,1)}, u32[]{:S(2)}) copy-start(bf16[256]{0:T(256)(128)(2,1)} %param.37) | copy-start | bytes 1540
  7.3 17.2 %copy-start.9 = (bf16[256]{0:T(256)(128)(2,1)S(1)}, bf16[256]{0:T(256)(128)(2,1)}, u32[]{:S(2)}) copy-start(bf16[256]{0:T(256)(128)(2,1)} %param.26) | copy-start | bytes 1540
  7.3 17.2 %copy-start.8 = (bf16[1024]{0:T(1024)(128)(2,1)S(1)}, bf16[1024]{0:T(1024)(128)(2,1)}, u32[]{:S(2)}) copy-start(bf16[1024]{0:T(1024)(128)(2,1)} %param.35) | copy-start | bytes 6148
  7.3 18.6 %copy-start.7 = (s32[1,2048]{1,0:T(1,128)S(1)}, s32[1,2048]{1,0:T(1,128)}, u32[]{:S(2)}) copy-start(s32[1,2048]{1,0:T(1,128)} %param.22) | copy-start | bytes 24580
  7.3 19.2 %copy-start.6 = (s32[1,2048]{1,0:T(1,128)S(1)}, s32[1,2048]{1,0:T(1,128)}, u32[]{:S(2)}) copy-start(s32[1,2048]{1,0:T(1,128)} %param.21) | copy-start | bytes 24580
  7.3 100.6 %all-gather.2.cloned.1.call-start = ((), (), s32[]{:S(2)}) async-start(), calls=%async_computation | async-start | bytes 4718592 | tf_op jit(solution)/shard_map/all_gather | solution.py:1146
  8.5 15.0 %collective-permute-start = (bf16[128,2048]{1,0:T(8,128)(2,1)S(1)}, bf16[128,2048]{1,0:T(8,128)(2,1)S(1)}, u32[]{:S(2)}, u32[]{:S(2)}) collective-permute-start(bf16[128,2048]{1,0:T(8,128)(2,1)S(1)} %pad_maximum_fusion.1), channel_id=1, source_target_pairs={{0,2},{1,3},{2,0},{3,1},{4,6},{5,7},{6,4},{7,5},{8,10},{9,11},{10,... | collective-permute-start | bytes 1572872 | tf_op jit(solution)/shard_map/ppermute | solution.py:1091
  23.4 0.8 copy-start.1
  277.4 10.4 %copy-start.10 = (bf16[1024,256]{1,0:T(8,128)(2,1)S(1)}, bf16[1024,256]{1,0:T(8,128)(2,1)}, u32[]{:S(2)}) copy-start(bf16[1024,256]{1,0:T(8,128)(2,1)} %get-tuple-element.82) | copy-start | bytes 1572868
  277.5 11.2 %copy-start.3 = (bf16[1024,256]{1,0:T(8,128)(2,1)S(1)}, bf16[1024,256]{1,0:T(8,128)(2,1)}, u32[]{:S(2)}) copy-start(bf16[1024,256]{1,0:T(8,128)(2,1)} %wq.3) | copy-start | bytes 1572868
  277.5 11.2 %copy-start.4 = (bf16[1024,256]{1,0:T(8,128)(2,1)S(1)}, bf16[1024,256]{1,0:T(8,128)(2,1)}, u32[]{:S(2)}) copy-start(bf16[1024,256]{1,0:T(8,128)(2,1)} %wk.3) | copy-start | bytes 1572868
  285.8 11.5 %copy-start.5 = (bf16[1024,256]{1,0:T(8,128)(2,1)S(1)}, bf16[1024,256]{1,0:T(8,128)(2,1)}, u32[]{:S(2)}) copy-start(bf16[1024,256]{1,0:T(8,128)(2,1)} %get-tuple-element.81) | copy-start | bytes 1572868
  287.9 9.4 %collective-permute-start.1 = (bf16[1024,256]{1,0:T(8,128)(2,1)S(1)}, bf16[1024,256]{1,0:T(8,128)(2,1)S(1)}, u32[]{:S(2)}, u32[]{:S(2)}) collective-permute-start(bf16[1024,256]{1,0:T(8,128)(2,1)S(1)} %copy-done.10), channel_id=1, source_target_pairs={{0,2},{1,3},{2,0},{3,1},{4,6},{5,7},{6,4},{7,5},{8,10},{9,11},{10,... | collective-permute-start | bytes 1572872 | tf_op jit(solution)/shard_map/ppermute | solution.py:1091
  297.4 2.0 copy-start
  299.4 1.4 copy-start.2
Sparse Core Ops, SparseCore 0:
  24.4 74.8 all-gather.1

commit v5 on v4

--- a/solution.py
+++ b/solution.py
@@ -295,7 +295,7 @@
             res_s[h] = dot(p_ref[h, :, (SLOTS - nb) * B :], va_s[h, pl.ds(start, nb * B), :])
             return carry
 
-        lax.fori_loop(0, LH, head, 0)
+        lax.fori_loop(0, LH, head, 0, unroll=True)
 
     for nb in range(1, SLOTS):
         pl.when(step == nb - 1)(functools.partial(attend, nb))
@@ -418,7 +418,7 @@
 def mlp_kernel(
     a_own, a_par, xm, dy_s, vec, bup, wu0, wu1, wd0, wd1,
     mk_ref, ms_ref, gn_ref, h1_ref, gu_ref, su_ref, gd_ref, sd_ref, bs_ref, ru_ref,
-    n2_s, n2t_s, dyt_s, am_s, ag_s, act_s, gp_s, us_s, s_u, r_u,
+    n2_s, n2t_s, dyt_s, dyo_s, am_s, ag_s, act_s, gp_s, us_s, s_u, r_u,
     *, bits, chunk,
 ):
     i = pl.program_id(0)
@@ -444,8 +444,13 @@
             mean, rstd = row_stats(value)
             n2 = ((value - mean) * rstd * vec[3:4, :] + vec[4:5, :]).astype(BF)
             n2_s[rows, :] = n2
-            n2t_s[:, rows] = n2.T
-            dyt_s[:, rows] = dy_s[rows, :].T
+            for source, turned, bit in (
+                (n2_s, n2t_s, bits[0]), (dy_s, dyt_s, bits[0]), (dy_s, dyo_s, bits[1])
+            ):
+                for j in range(D // 256):
+                    for side, cols in enumerate(piece(j, bit, chunk)):
+                        to = slice(side * (D // 2) + j * 128, side * (D // 2) + (j + 1) * 128)
+                        turned[to, rows] = source[rows, cols].T
             am_s[rows, :] = jnp.zeros((B, D), F32)
             ag_s[rows, :] = jnp.zeros((B, D), F32)
             return carry
@@ -475,21 +480,15 @@
         sums = lax.fori_loop(0, OWN // B, rows_of, jnp.zeros((1, TILE), F32))
         bs_ref[...] = jnp.broadcast_to(sums, bs_ref.shape)
 
-        def grads(left, right, keep, send, bit):
-            def rows_of(j, carry):
-                to = pl.ds(pl.multiple_of(j * 128, 128), 128)
-                mine, other = piece(j, bit, chunk)
-                keep[to, :] = dot(left[mine, :], right[...]).astype(BF)
-                send[to, :] = dot(left[other, :], right[...]).astype(BF)
-                return carry
-
-            lax.fori_loop(0, D // 256, rows_of, 0)
+        def grads(left, right, keep, send):
+            keep[...] = dot(left[0 : D // 2, :], right[...]).astype(BF)
+            send[...] = dot(left[D // 2 :, :], right[...]).astype(BF)
 
         first = which == 0
-        grads(n2t_s, gp_s, gu_ref, us_s.at[i] if first else su_ref, bits[0])
+        grads(n2t_s, gp_s, gu_ref, us_s.at[i] if first else su_ref)
         if first:
             send_tile(i, 0).start()
-        grads(dyt_s, act_s, gd_ref, us_s.at[2 + i] if first else sd_ref, bits[1] if first else bits[0])
+        grads(dyo_s if first else dyt_s, act_s, gd_ref, us_s.at[2 + i] if first else sd_ref)
         if first:
             send_tile(2 + i, 1).start()
 
@@ -537,6 +536,7 @@
             pltpu.VMEM((OWN, D), BF),
             pltpu.VMEM((D, OWN), BF),
             pltpu.VMEM((D, OWN), BF),
+            pltpu.VMEM((D, OWN), BF),
             pltpu.VMEM((OWN, D), F32),
             pltpu.VMEM((OWN, D), F32),
             pltpu.VMEM((OWN, TILE), BF),
@@ -585,9 +585,9 @@
 def bwd_kernel(
     x0, x1, x2, x3, x_late, h1, gn, gn_any, mk, ms_any, dy_in, gu, gd, ru, su_any, sd_any, up_sums, hm,
     p_ref, q_ref, linv_ref, ctx_ref, k_ref, v_ref, vec, wq, wk, wv, wd,
-    oo_ref, os_ref, tg_ref, wu_ref, wdn_ref, wqk_ref, wvd_ref, vt_ref,
+    out_any, os_any, tg_ref, wu_ref, wdn_ref, wqk_ref, wvd_ref, vt_ref,
     w_s, gh_s, gm_s, gt_s, qt_s, dl_s, ds_s, res_s, dkt_s, dvt_s, acc_s,
-    gn_got, mr_got, gh_own, gh_y, gh_f,
+    o_s, gn_got, mr_got, gh_own, gh_y, gh_f,
     part_keep, part_send, part_got, sum_keep, sum_send, sum_got, ghx_s, st_keep, st_got, st_sum, st_all,
     gk, ru_s, g1, y_send, y_got, cs_ref, bs_ref, n1_ref, v_keep, v_send, v_away, v_sum, v_got,
     *rest, orders, chunk,
@@ -596,7 +596,7 @@
     stages = [rest[3 * n : 3 * n + 3] for n in range(levels - 1)]
     (
         s_gn, r_gn, s_mr, r_mr, s_gy, r_gy, s_gf, r_gf, s_pc, r_pc, s_sy, r_sy,
-        s_tc, r_tc, s_ty, r_ty, s_g1, r_g1, s_yy, r_yy, l_g, l_r, s_gw, r_gw, s_va, r_va, s_vt, r_vt, *g_sems,
+        s_tc, r_tc, s_ty, r_ty, s_g1, r_g1, s_yy, r_yy, l_g, l_r, s_gw, r_gw, s_va, r_va, s_vt, r_vt, l_o, s_o, r_o, *g_sems,
     ) = rest[3 * (levels - 1) :]
     step = pl.program_id(0)
     b = NB - 1 - (step - LEAD)
@@ -616,6 +616,14 @@
         s_gy.at[2 * j + side], r_gy.at[2 * j + side], across,
     )
     send_gf = lambda j: remote(gh_y.at[j], gh_f.at[j], s_gf.at[j], r_gf.at[j], beside)
+    store_out = lambda j, side: pltpu.make_async_copy(
+        o_s.at[lax.rem(j, 2), side],
+        (out_any.at[block_rows(2 * j + y)], os_any.at[block_rows(j)])[side],
+        l_o.at[2 * lax.rem(j, 2) + side],
+    )
+    send_out = lambda j: remote(
+        os_any.at[block_rows(j)], out_any.at[block_rows(2 * j + y)], s_o.at[j], r_o.at[j], across
+    )
     send_part = lambda n: remote(part_send.at[lax.rem(n, 3)], part_got.at[n], s_pc.at[n], r_pc.at[n], beside)
     send_sum = lambda n: remote(sum_send.at[n], sum_got.at[n], s_sy.at[n], r_sy.at[n], across)
     send_tc = lambda n: remote(st_keep.at[n], st_got.at[n], s_tc.at[n], r_tc.at[n], beside)
@@ -740,8 +748,15 @@
             total = mk[:, part].astype(F32) + mr_got[j, :, part].astype(F32)
             return (h1[:, cols] + total + vec[5:6, cols]).astype(BF)
 
-        oo_ref[...] = out(y)
-        os_ref[...] = out(1 - y)
+
+        @pl.when(step >= 2)
+        def _():
+            for side in range(2):
+                store_out(j + 2, side).wait()
+
+        for side, which in enumerate((y, 1 - y)):
+            o_s[lax.rem(j, 2), side] = out(which)
+            store_out(j, side).start()
         mean, rstd = row_stats(value)
         xhat = (value - mean) * rstd
         grad = gn[...].astype(F32) + gn_got[j].astype(F32)
@@ -799,7 +814,7 @@
             dvt_s[h, :, keys] += dot(gt_s[h], p_ref[h, :, live])
             return carry
 
-        lax.fori_loop(0, LH, head, 0)
+        lax.fori_loop(0, LH, head, 0, unroll=2)
 
     pl.when((step >= LEAD) & (b >= SLOTS - 1))(functools.partial(attend, SLOTS))
     for nb in range(SLOTS - 1, 0, -1):
@@ -862,6 +877,8 @@
                 gn_got[p - 8, j % 2 * 128 : (j % 2 + 1) * 128, into] = acc_s[other, cols].astype(BF)
             for part in range(2):
                 send_weights(p, part).start()
+        for j in range(half):
+            send_out(j).start()
 
     send_away = lambda: remote(v_send, v_away, s_va.at[0], r_va.at[0], across)
     send_total = lambda n: remote(
@@ -870,6 +887,9 @@
 
     @pl.when(step == half)
     def _():
+        for j in range(2):
+            for side in range(2):
+                store_out(j, side).wait()
         for ref, rank, side in ((v_keep, ranks[0], 0), (v_send, ranks[2], UNITS)):
             ref[0:4, :] = cs_ref[0:4, feature_block(rank)]
             for n in range(4):
@@ -960,6 +980,7 @@
     def _():
         for j in range(half):
             close(j)
+            send_out(j).wait()
             for copy in (send_gn, send_mr, send_gf, send_last):
                 copy(j).wait_send()
             for side in range(2):
@@ -1013,7 +1034,7 @@
         + [whole(8, D)]
         + [whole(D, SHARE)] * 3
         + [whole(SHARE, D)],
-        out_specs=[own(SHARE), own(SHARE), final_late]
+        out_specs=[anywhere, anywhere, final_late]
         + [whole(chunk, UNITS)] * 2
         + [whole(chunk, TILE)] * 2
         + [whole(16, SHARE)],
@@ -1029,6 +1050,7 @@
             vmem(LH, HD, SEQ, dtype=F32),
             vmem(LH, HD, SEQ, dtype=F32),
             vmem(D, 4 * SHARE, dtype=F32),
+            vmem(2, 2, B, SHARE),
             vmem(half, B, D),
             vmem(half, B, D // 2),
             vmem(half, B, D),
@@ -1070,8 +1092,9 @@
         + [dma(4)] * 2
         + [dma(1)] * 2
         + [dma(levels)] * 2
+        + [dma(half)] * 3
         + [dma(10)] * (2 * (levels - 1)),
-        out_shape=[like((OWN, SHARE), BF)] * 2
+        out_shape=[like((SEQ, SHARE), BF), like((OWN, SHARE), BF)]
         + [like((SEQ, SHARE), F32)]
         + [like((chunk, UNITS), F32)] * 2
         + [like((chunk, TILE), F32)] * 2
@@ -1143,7 +1166,6 @@
     part = D // size
     cut = lambda w: lax.dynamic_slice_in_dim(w, rank * part, part, 0)
     w_part = y_swap(jnp.concatenate([cut(w_up), cut(w_down)], axis=1))
-    w_other = lax.all_gather(w_part, "dp", axis=0, tiled=True)
     seg = segments.reshape(SEQ)
     index = jnp.arange(SEQ, dtype=jnp.int32)
     first = jnp.zeros((SEQ,), jnp.int32)
@@ -1155,10 +1177,16 @@
     slopes = jnp.exp2(-8.0 * (heads.astype(F32) + 1.0) / HEADS)
     alibi = rows8(slopes[:, None] * (jnp.arange(STRIP) - (STRIP - 1)).astype(F32)[None, :])
 
+    b_qv = rows8(jnp.stack([b_query, b_value]).astype(F32))
+    lows = lowest.reshape(SEQ, 1)
+    w_part, own_vec, b_qv, lows, pad_row, alibi = lax.optimization_barrier(
+        (w_part, own_vec, b_qv, lows, pad_row, alibi)
+    )
+    w_other = lax.all_gather(w_part, "dp", axis=0, tiled=True)
+
     p, q, k, v, linv, ctx, a_own, a_par, x1, x2, x3, xm, hm, vec, b_up_pair, dy = attention_forward(
         tokens, out_grad, own_vec, w_query, w_key, w_value,
-        rows8(jnp.stack([b_query, b_value]).astype(F32)), w_dense,
-        lowest.reshape(SEQ, 1), pad_row, alibi,
+        b_qv, w_dense, lows, pad_row, alibi,
     )
     xs = [tokens, x1, x2, x3]
 
@@ -1168,15 +1196,11 @@
     mk, ms, gn, h1, gu, su, gd, sd, up_sums, ru = feed_forward(
         a_own, a_par, xm, dy, vec, b_up_pair, w_up, w_down, w_other, (order_a[0], order_b[0]), part
     )
-    out_own, out_send, tokens_grad, w_up_grad, w_down_grad, g_qk, g_vd, sums = attention_backward(
+    output, _, tokens_grad, w_up_grad, w_down_grad, g_qk, g_vd, sums = attention_backward(
         xs, h1, gn, mk, ms, dy, gu, gd, ru, su, sd, up_sums, hm, p, q, linv, ctx, k, v, vec,
         w_query, w_key, w_value, w_dense, (order_a, order_b), part,
     )
     w_down_grad = w_down_grad.T
-    out_y = y_swap(out_send)
-    pair = jnp.stack([out_own, out_y]).reshape(2, NB // 2, B, SHARE)
-    output = jnp.where(y == 0, pair, pair[::-1]).transpose(1, 0, 2, 3).reshape(SEQ, SHARE)
-
     head_max = sums[12, :LH]
     column_scale = jnp.repeat(jnp.sqrt(TAU / jnp.maximum(head_max, TAU)), HD)
     return (

time: 309 us -> 283 us (0.916)
  Pallas kernels: 246 us -> 233 us
  waiting for transfers between devices: 19.1 us -> 10.2 us
    ppermute x2 -> x1, waiting for transfers between devices: 19.1 us -> 4.97 us  [swap(): return lax.ppermute(value, axis, [(i, i ^ bit) for i in range(size)])]
    pallas_call x1, Pallas kernels: 76.6 us -> 69.8 us  [attention_forward(): pl.pallas_call(fwd_kernel, grid=(NB + TAIL,), in_specs=[pl.BlockSpec(memo...]
    all_gather x1, waiting for transfers between devices: 0.02 us -> 5.18 us  [shards(): w_other = lax.all_gather(w_part, 'dp', axis=0, tiled=True)]
    pallas_call x1, Pallas kernels: 52.4 us -> 48.3 us  [feed_forward(): pl.pallas_call(functools.partial(mlp_kernel, bits=bits, chunk=chunk), gri...]
    unnamed x42 -> x45, local copies, waits for them, and re-layouts: 7.92 us -> 8.11 us
  transfers between devices with their start and end apart: 3 -> 2, of which waited for: 2 -> 2; matrix products, arithmetic and copies ran while one was open for 3% -> 2% of each run, Pallas kernels for 25% -> 25%
where the time goes in v5:
time: 283 us; the launch traced here: 282 us
  Pallas kernels  233 us (82%)
  between operations  14.4 us (5%)
  local copies, waits for them, and re-layouts  13.9 us (5%)
  waiting for transfers between devices  10.2 us (4%)
  other arithmetic  8.41 us (3%)
  starting transfers between devices  3.07 us (1%)
    pallas_call x1, Pallas kernels, attention_backward(): pl.pallas_call(functools.partial(bwd_kernel, orders=orders, chunk=chunk),...  114 us
    pallas_call x1, Pallas kernels, attention_forward(): pl.pallas_call(fwd_kernel, grid=(NB + TAIL,), in_specs=[pl.BlockSpec(memo...  69.8 us
    pallas_call x1, Pallas kernels, feed_forward(): pl.pallas_call(functools.partial(mlp_kernel, bits=bits, chunk=chunk), gri...  48.3 us
    unnamed x45, local copies, waits for them, and re-layouts  8.11 us
  transfers between devices with their start and end apart: 2, of which 2 were waited for; matrix products, arithmetic and copies ran while one was open for 2% of the time, Pallas kernels for 25%

profile of v5, /device:TPU:0, one launch (start us, length us, event | category | flops | bytes accessed | tf_op | source)
XLA Modules:
  0.0 282.5 jit_solution(7632621977927388929)
XLA Ops:
  7.4 1.1 constant_dynamic-slice_fusion
  8.5 3.0 %collective-permute-start = (bf16[128,2048]{1,0:T(8,128)(2,1)S(1)}, bf16[128,2048]{1,0:T(8,128)(2,1)S(1)}, u32[]{:S(2)}, u32[]{:S(2)}) collective-permute-start(bf16[128,2048]{1,0:T(8,128)(2,1)S(1)} %pad_maximum_fusion), channel_id=1, source_target_pairs={{0,2},{1,3},{2,0},{3,1},{4,6},{5,7},{6,4},{7,5},{8,10},{9,11},{10,... | collective-permute-start | bytes 1572872 | tf_op jit(solution)/shard_map/ppermute | solution.py:1114
  11.6 0.7 fusion.1
  12.3 0.1 broadcast_multiply_fusion
  12.4 2.0 fusion
  14.3 0.6 fusion.7.bqv
  15.1 0.6 convert_element_type.45.own_vec
  15.7 0.6 pad.18.alibi
  16.3 0.6 pad.17
  17.0 0.4 copy.42
  17.4 1.1 add_maximum_fusion.lo
  18.5 5.0 %collective-permute-done = bf16[128,2048]{1,0:T(8,128)(2,1)S(1)} collective-permute-done((bf16[128,2048]{1,0:T(8,128)(2,1)S(1)}, bf16[128,2048]{1,0:T(8,128)(2,1)S(1)}, u32[]{:S(2)}, u32[]{:S(2)}) %collective-permute-start) | collective-permute-done | bytes 524320 | tf_op jit(solution)/shard_map/ppermute | solution.py:1114
  23.4 0.8 copy-done.2
  24.3 69.8 %attention_forward.1 = (bf16[4,2048,1280]{2,1,0:T(8,128)(2,1)}, bf16[2048,256]{1,0:T(8,128)(2,1)}, bf16[2048,256]{1,0:T(8,128)(2,1)}, bf16[2048,256]{1,0:T(8,128...) custom-call(bf16[2048,256]{1,0:T(8,128)(2,1)} %x_late.1, ...), custom_call_target="tpu_custom_call" | custom-call | flops 16000000000 | bytes 41943040 | tf_op jit(solution)/shard_map/attention_forward/pallas_call | solution.py:372
  94.1 5.2 %all-gather.2.cloned.1.call-done.wu1.wd1 = bf16[1024,2048]{1,0:T(8,128)(2,1)} async-done(((bf16[128,2048]{1,0:T(8,128)(2,1)}), bf16[1024,2048]{1,0:T(8,128)(2,1)}) %all-gather.2.cloned.1.call-update) | async-done | bytes 4194320 | tf_op jit(solution)/shard_map/all_gather | solution.py:1185
  99.3 48.3 %feed_forward.1 = (bf16[1024,512]{1,0:T(8,128)(2,1)}, bf16[1024,512]{1,0:T(8,128)(2,1)}, bf16[1024,1024]{1,0:T(8,128)(2,1)}, f32[1024,1024]{1,0:T(8,128)}, bf16[...) custom-call(bf16[1024,512]{1,0:T(8,128)(2,1)} %get-tuple-element.68., ...), custom_call_target="tpu_custom_call" | custom-call | flops 25999998976 | bytes 41943040 | tf_op jit(solution)/shard_map/feed_forward/pallas_call | solution.py:512
  147.6 114.4 %backward.1 = (bf16[2048,256]{1,0:T(8,128)(2,1)}, bf16[1024,256]{1,0:T(8,128)(2,1)}, f32[2048,256]{1,0:T(8,128)}, f32[128,1024]{1,0:T(8,128)}, f32[128,1024]{1,0...) custom-call(bf16[2048,256]{1,0:T(8,128)(2,1)} %x_late.1, ...), custom_call_target="tpu_custom_call" | custom-call | flops 30000001024 | bytes 52428800 | tf_op jit(solution)/shard_map/backward/pallas_call | solution.py:1022
  262.1 1.2 divide_sqrt_fusion
  263.3 0.7 slice_bitcast_fusion.1
  264.0 1.4 fusion.9
  265.5 0.1 mul.46
  265.6 0.6 convert_multiply_fusion.2
  266.2 1.5 convert_multiply_fusion
  267.7 0.6 copy.45
  268.3 0.7 fusion.8
  269.0 0.7 slice_bitcast_fusion
  269.7 0.8 copy.43
  270.4 2.0 copy.44
  272.5 1.0 copy.49
  273.4 1.3 copy.50
  274.8 0.1 copy-done.3
  274.8 0.8 copy.51
  (53 shorter events, 0.4 us)
Async XLA Ops:
  7.2 4.3 %copy-start.12 = (bf16[256]{0:T(256)(128)(2,1)S(1)}, bf16[256]{0:T(256)(128)(2,1)}, u32[]{:S(2)}) copy-start(bf16[256]{0:T(256)(128)(2,1)} %param.29) | copy-start | bytes 1540
  7.2 4.3 %copy-start.11 = (bf16[256]{0:T(256)(128)(2,1)S(1)}, bf16[256]{0:T(256)(128)(2,1)}, u32[]{:S(2)}) copy-start(bf16[256]{0:T(256)(128)(2,1)} %param.26) | copy-start | bytes 1540
  7.2 4.4 %copy-start.8 = (s32[1,2048]{1,0:T(1,128)S(1)}, s32[1,2048]{1,0:T(1,128)}, u32[]{:S(2)}) copy-start(s32[1,2048]{1,0:T(1,128)} %param.21) | copy-start | bytes 24580
  7.2 5.0 %copy-start.9 = (s32[1,2048]{1,0:T(1,128)S(1)}, s32[1,2048]{1,0:T(1,128)}, u32[]{:S(2)}) copy-start(s32[1,2048]{1,0:T(1,128)} %param.22) | copy-start | bytes 24580
  7.2 7.7 %copy-start.13 = (bf16[256]{0:T(256)(128)(2,1)S(1)}, bf16[256]{0:T(256)(128)(2,1)}, u32[]{:S(2)}) copy-start(bf16[256]{0:T(256)(128)(2,1)} %param.23) | copy-start | bytes 1540
  7.2 7.7 %copy-start.14 = (bf16[256]{0:T(256)(128)(2,1)S(1)}, bf16[256]{0:T(256)(128)(2,1)}, u32[]{:S(2)}) copy-start(bf16[256]{0:T(256)(128)(2,1)} %param.24) | copy-start | bytes 1540
  7.3 7.7 %copy-start.15 = (bf16[256]{0:T(256)(128)(2,1)S(1)}, bf16[256]{0:T(256)(128)(2,1)}, u32[]{:S(2)}) copy-start(bf16[256]{0:T(256)(128)(2,1)} %param.31) | copy-start | bytes 1540
  7.3 7.7 %copy-start.16 = (bf16[256]{0:T(256)(128)(2,1)S(1)}, bf16[256]{0:T(256)(128)(2,1)}, u32[]{:S(2)}) copy-start(bf16[256]{0:T(256)(128)(2,1)} %param.32) | copy-start | bytes 1540
  7.3 7.7 %copy-start.17 = (bf16[256]{0:T(256)(128)(2,1)S(1)}, bf16[256]{0:T(256)(128)(2,1)}, u32[]{:S(2)}) copy-start(bf16[256]{0:T(256)(128)(2,1)} %param.33) | copy-start | bytes 1540
  7.3 7.7 %copy-start.18 = (bf16[256]{0:T(256)(128)(2,1)S(1)}, bf16[256]{0:T(256)(128)(2,1)}, u32[]{:S(2)}) copy-start(bf16[256]{0:T(256)(128)(2,1)} %param.37) | copy-start | bytes 1540
  7.3 7.7 %copy-start.10 = (bf16[1024]{0:T(1024)(128)(2,1)S(1)}, bf16[1024]{0:T(1024)(128)(2,1)}, u32[]{:S(2)}) copy-start(bf16[1024]{0:T(1024)(128)(2,1)} %param.35) | copy-start | bytes 6148
  7.3 92.0 %all-gather.2.cloned.1.call-start = ((), (), s32[]{:S(2)}) async-start(), calls=%async_computation | async-start | bytes 4718592 | tf_op jit(solution)/shard_map/all_gather | solution.py:1185
  8.5 15.0 %collective-permute-start = (bf16[128,2048]{1,0:T(8,128)(2,1)S(1)}, bf16[128,2048]{1,0:T(8,128)(2,1)S(1)}, u32[]{:S(2)}, u32[]{:S(2)}) collective-permute-start(bf16[128,2048]{1,0:T(8,128)(2,1)S(1)} %pad_maximum_fusion), channel_id=1, source_target_pairs={{0,2},{1,3},{2,0},{3,1},{4,6},{5,7},{6,4},{7,5},{8,10},{9,11},{10,... | collective-permute-start | bytes 1572872 | tf_op jit(solution)/shard_map/ppermute | solution.py:1114
  23.4 0.8 copy-start.2
  147.6 118.6 %copy-start.4 = (bf16[1024,256]{1,0:T(8,128)(2,1)S(1)}, bf16[1024,256]{1,0:T(8,128)(2,1)}, u32[]{:S(2)}) copy-start(bf16[1024,256]{1,0:T(8,128)(2,1)} %wq.3) | copy-start | bytes 1572868
  147.6 118.6 %copy-start.5 = (bf16[1024,256]{1,0:T(8,128)(2,1)S(1)}, bf16[1024,256]{1,0:T(8,128)(2,1)}, u32[]{:S(2)}) copy-start(bf16[1024,256]{1,0:T(8,128)(2,1)} %wk.3) | copy-start | bytes 1572868
  262.1 6.2 %copy-start.7 = (f32[128,512]{1,0:T(8,128)S(1)}, f32[128,512]{1,0:T(8,128)}, u32[]{:S(2)}) copy-start(f32[128,512]{1,0:T(8,128)} %get-tuple-element.95) | copy-start | bytes 786436
  262.1 6.9 %copy-start.6 = (f32[128,512]{1,0:T(8,128)S(1)}, f32[128,512]{1,0:T(8,128)}, u32[]{:S(2)}) copy-start(f32[128,512]{1,0:T(8,128)} %get-tuple-element.96) | copy-start | bytes 786436
  266.2 6.3 %copy-start.1 = (bf16[2048,256]{1,0:T(8,128)(2,1)S(1)}, bf16[2048,256]{1,0:T(8,128)(2,1)}, u32[]{:S(2)}) copy-start(bf16[2048,256]{1,0:T(8,128)(2,1)} %get-tuple-element.183) | copy-start | bytes 3145732
  269.0 4.4 %copy-start = (f32[2048,256]{1,0:T(8,128)S(1)}, f32[2048,256]{1,0:T(8,128)}, u32[]{:S(2)}) copy-start(f32[2048,256]{1,0:T(8,128)} %get-tuple-element.184) | copy-start | bytes 6291460
  273.4 1.4 copy-start.3
Sparse Core Ops, SparseCore 0:
  24.4 74.8 all-gather.1

commit v6 on v5

--- a/solution.py
+++ b/solution.py
@@ -189,7 +189,7 @@
         greet((beside, across, {"tensor": ranks[3]}))
         for r in range(1, 4):
             vectors(r).start()
-        for b in range(3):
+        for b in range(5):
             to_y(b).start()
             to_core(b).start()
         for r in range(1, 4):
@@ -204,9 +204,9 @@
         forward(0).start()
         hm_ref[...] = jnp.full(hm_ref.shape, NEG, F32)
 
-    for b in range(3, NB):
-
-        @pl.when(step == b - 2)
+    for b in range(5, NB):
+
+        @pl.when(step == b - 4)
         def _():
             to_y(b).start()
             to_core(b).start()
@@ -566,20 +566,26 @@
 
 LEAD = 2
 FINAL = 3
-TILES = (("u", 0), ("u", 1), ("d", 0), ("d", 1), ("u", 2), ("d", 2), ("d", 3), ("u", 3), ("a", 0), ("a", 1))
-OTHER_ORDER = (2, 3, 9)
+TILES = (("u", 0), ("u", 1), ("d", 0), ("d", 1), ("u", 2), ("d", 2), ("d", 3), ("u", 3), *(("a", n) for n in range(4)))
+OTHER_ORDER = (2, 3, 11)
 FIRST = (0, 1, 0, 2, 3, 4, 6, 7)
-USE = sorted(range(8), key=lambda p: (FIRST[p], p)) + [8, 9]
+USE = sorted(range(8), key=lambda p: (FIRST[p], p))
+SLOT = [USE.index(p) % 2 for p in range(8)] + [0, 0, 1, 1]
 PAIRS = ((0, 4), (1, 7), (2, 5), (3, 6))
 DRAIN = LEAD + FINAL + NB
 
 
-def step_of(p, n):
-    return FIRST[p] + 3 * (n - 1) if p < 8 else DRAIN + n - 1
+def step_of(p, n, levels):
+    if p < 8:
+        return FIRST[p] + 3 * (n - 1)
+    if n <= 2:
+        return ((11, 12, 13, 11), (13, 14, 14, 13))[n - 1][p - 8]
+    free = step_of(p - 4, n + 1, levels) if n < levels else 0
+    return max(step_of(p, n - 1, levels) + 1, free)
 
 
 def last_step(levels):
-    return max(step_of(7, levels), step_of(8, levels))
+    return max(DRAIN + levels - 1, max(step_of(p, levels, levels) for p in range(7, 12)))
 
 
 def bwd_kernel(
@@ -633,6 +639,10 @@
         kind, n = TILES[p]
         return slice(n * TILE, (n + 1) * TILE), kind == "u"
 
+    span = lambda p: slice(0, TILE) if p < 8 else slice((p - 8) % 2 * SHARE, ((p - 8) % 2 + 1) * SHARE)
+    wide = lambda p: slice(0, TILE if p < 8 else SHARE)
+    shared = lambda p: p if p < 8 else 8 + (p - 8) // 2
+
     def send_first(p):
         cols, up = tile_of(p)
         src = (su_any if up else sd_any).at[:, slice(cols.start - UNITS, cols.stop - UNITS)]
@@ -641,11 +651,12 @@
     def send_weights(p, part):
         n = 2 * (p - 8) + part
         return remote(
-            gn_got.at[p - 8, :, slice(part * TILE, (part + 1) * TILE)], g1.at[p - 4, block_rows(part)],
+            gn_got.at[p - 8, :, slice(part * SHARE, (part + 1) * SHARE)],
+            g1.at[4 + (p - 8) // 2, block_rows(part), span(p)],
             s_gw.at[n], r_gw.at[n], partner(order_of(p)[0]),
         )
 
-    slot = [USE.index(p) % 2 for p in range(10)]
+    slot = SLOT
 
     def load_keep(p):
         cols, up = tile_of(p)
@@ -657,7 +668,7 @@
     def send_stage(p, n):
         _, send, got = stages[n - 1]
         return remote(
-            send.at[p % 4], got.at[p], g_sems[2 * n - 2].at[p], g_sems[2 * n - 1].at[p], partner(order_of(p)[n])
+            send.at[p % 4, :, wide(p)], got.at[shared(p), :, span(p)], g_sems[2 * n - 2].at[p], g_sems[2 * n - 1].at[p], partner(order_of(p)[n])
         )
 
     send_last = lambda n: remote(y_send.at[n], y_got.at[n], s_yy.at[n], r_yy.at[n], across)
@@ -665,12 +676,12 @@
     def split(p, n):
         order = order_of(p)
         if n == 1:
-            keep = lambda rows: gk[slot[p], rows, :]
+            keep = lambda rows: gk[slot[p], rows, span(p)]
             if p < 4:
                 load_got(p).wait()
                 got = lambda rows: ru_s[slot[p], rows, :]
             else:
-                got = lambda rows: g1[p - 4, rows, :]
+                got = lambda rows: g1[shared(p) - 4, rows, span(p)]
             if p < 8:
                 load_keep(p).wait()
             if 4 <= p < 8:
@@ -680,8 +691,8 @@
                 send_weights(p, 1).wait_recv()
         else:
             send_stage(p, n - 1).wait_recv()
-            keep = lambda rows: stages[n - 2][0][p % 4, rows, :]
-            got = lambda rows: stages[n - 2][2][p, rows, :]
+            keep = lambda rows: stages[n - 2][0][p % 4, rows, wide(p)]
+            got = lambda rows: stages[n - 2][2][shared(p), rows, span(p)]
         size = D >> n
         following = order[n]
         inner = chunk
@@ -694,15 +705,15 @@
             to = slice(group * inner, (group + 1) * inner)
             for side, ref in ((mine, stages[n - 1][0]), (1 - mine, stages[n - 1][1])):
                 rows = pl.ds(pl.multiple_of(group * 2 * inner + side * inner, inner), inner)
-                ref[p % 4, to, :] = (keep(rows).astype(F32) + got(rows).astype(F32)).astype(BF)
+                ref[p % 4, to, wide(p)] = (keep(rows).astype(F32) + got(rows).astype(F32)).astype(BF)
         send_stage(p, n).start()
 
     def whole_tile(p):
         send_stage(p, levels - 1).wait_recv()
         keep, _, got = stages[levels - 2]
-        total = keep[p % 4].astype(F32) + got[p].astype(F32)
+        total = keep[p % 4, :, wide(p)].astype(F32) + got[shared(p), :, span(p)].astype(F32)
         if p >= 8:
-            (wqk_ref, wvd_ref)[p - 8][...] = total
+            (wqk_ref, wvd_ref)[(p - 8) // 2][:, span(p)] = total
         for n, (own, other) in enumerate(PAIRS):
             cols, up = tile_of(own)
             if p == own:
@@ -730,6 +741,9 @@
         cs_ref[...] = jnp.zeros(cs_ref.shape, F32)
         bs_ref[...] = jnp.zeros(bs_ref.shape, F32)
         n1_ref[...] = jnp.zeros(n1_ref.shape, F32)
+
+    @pl.when(step == 1)
+    def _():
         dkt_s[...] = jnp.zeros(dkt_s.shape, F32)
         dvt_s[...] = jnp.zeros(dvt_s.shape, F32)
         acc_s[...] = jnp.zeros(acc_s.shape, F32)
@@ -868,12 +882,12 @@
 
     @pl.when(step == LEAD + NB - 1)
     def _():
-        for p in (8, 9):
-            cols = slice((p - 8) * TILE, (p - 7) * TILE)
+        for p in (11, 8, 9, 10):
+            cols = slice((p - 8) * SHARE, (p - 7) * SHARE)
             for j in range(D // 256):
                 mine, other = piece(j, order_of(p)[0], chunk)
-                gk[slot[p], j * 128 : (j + 1) * 128, :] = acc_s[mine, cols].astype(BF)
-                into = slice(j // 2 * TILE, (j // 2 + 1) * TILE)
+                gk[slot[p], j * 128 : (j + 1) * 128, span(p)] = acc_s[mine, cols].astype(BF)
+                into = slice(j // 2 * SHARE, (j // 2 + 1) * SHARE)
                 gn_got[p - 8, j % 2 * 128 : (j % 2 + 1) * 128, into] = acc_s[other, cols].astype(BF)
             for part in range(2):
                 send_weights(p, part).start()
@@ -963,10 +977,10 @@
             send_gy(j, 1).wait_recv()
             send_gf(j).start()
 
-    for p in range(10):
+    for p in range(12):
         for n in range(1, levels):
-            pl.when(step == step_of(p, n))(functools.partial(split, p, n))
-        pl.when(step == step_of(p, levels))(functools.partial(whole_tile, p))
+            pl.when(step == step_of(p, n, levels))(functools.partial(split, p, n))
+        pl.when(step == step_of(p, levels, levels))(functools.partial(whole_tile, p))
 
     def load_next(p):
         load_keep(p).start()
@@ -986,7 +1000,7 @@
             for side in range(2):
                 send_gy(j, side).wait_send()
             for level in range(1, levels):
-                send_stage(6 + j, level).wait_send()
+                send_stage(8 + j, level).wait_send()
         for n in range(NB):
             for copy in (send_sum, send_tc, send_ty):
                 copy(n).wait_send()
@@ -994,7 +1008,7 @@
             send_part(n).wait_send()
         for p in range(4, 8):
             send_first(p).wait_send()
-        for p in (8, 9):
+        for p in range(8, 12):
             for part in range(2):
                 send_weights(p, part).wait_send()
         send_away().wait_send()
@@ -1089,11 +1103,11 @@
         + [dma(4)] * 2
         + [dma(half)] * 2
         + [dma(2)] * 2
-        + [dma(4)] * 2
+        + [dma(8)] * 2
         + [dma(1)] * 2
         + [dma(levels)] * 2
         + [dma(half)] * 3
-        + [dma(10)] * (2 * (levels - 1)),
+        + [dma(12)] * (2 * (levels - 1)),
         out_shape=[like((SEQ, SHARE), BF), like((OWN, SHARE), BF)]
         + [like((SEQ, SHARE), F32)]
         + [like((chunk, UNITS), F32)] * 2

time: 283 us -> 281 us (level)
  Pallas kernels: 233 us -> 228 us
  transfers between devices with their start and end apart: 2 -> 2, of which waited for: 2 -> 2; matrix products, arithmetic and copies ran while one was open for 2% -> 2% of each run, Pallas kernels for 25% -> 24%
where the time goes in v6:
time: 281 us; the launch traced here: 280 us
  Pallas kernels  228 us (81%)
  between operations  14.4 us (5%)
  local copies, waits for them, and re-layouts  13.9 us (5%)
  waiting for transfers between devices  12.3 us (4%)
  other arithmetic  8.41 us (3%)
  starting transfers between devices  3.07 us (1%)
    pallas_call x1, Pallas kernels, attention_backward(): pl.pallas_call(functools.partial(bwd_kernel, orders=orders, chunk=chunk),...  112 us
    pallas_call x1, Pallas kernels, attention_forward(): pl.pallas_call(fwd_kernel, grid=(NB + TAIL,), in_specs=[pl.BlockSpec(memo...  67.7 us
    pallas_call x1, Pallas kernels, feed_forward(): pl.pallas_call(functools.partial(mlp_kernel, bits=bits, chunk=chunk), gri...  48.4 us
    unnamed x45, local copies, waits for them, and re-layouts  8.11 us
    all_gather x1, waiting for transfers between devices, shards(): w_other = lax.all_gather(w_part, 'dp', axis=0, tiled=True)  7.3 us
  transfers between devices with their start and end apart: 2, of which 2 were waited for; matrix products, arithmetic and copies ran while one was open for 2% of the time, Pallas kernels for 24%

profile of v6, /device:TPU:0, one launch (start us, length us, event | category | flops | bytes accessed | tf_op | source)
XLA Modules:
  0.0 280.4 jit_solution(16889255050048229945)
XLA Ops:
  7.4 1.1 constant_dynamic-slice_fusion
  8.5 3.0 %collective-permute-start = (bf16[128,2048]{1,0:T(8,128)(2,1)S(1)}, bf16[128,2048]{1,0:T(8,128)(2,1)S(1)}, u32[]{:S(2)}, u32[]{:S(2)}) collective-permute-start(bf16[128,2048]{1,0:T(8,128)(2,1)S(1)} %pad_maximum_fusion), channel_id=1, source_target_pairs={{0,2},{1,3},{2,0},{3,1},{4,6},{5,7},{6,4},{7,5},{8,10},{9,11},{10,... | collective-permute-start | bytes 1572872 | tf_op jit(solution)/shard_map/ppermute | solution.py:1128
  11.6 0.7 fusion.1
  12.3 0.1 broadcast_multiply_fusion
  12.4 2.0 fusion
  14.3 0.6 fusion.7.bqv
  15.1 0.6 convert_element_type.45.own_vec
  15.7 0.6 pad.18.alibi
  16.3 0.6 pad.17
  17.0 0.4 copy.42
  17.4 1.1 add_maximum_fusion.lo
  18.5 5.0 %collective-permute-done = bf16[128,2048]{1,0:T(8,128)(2,1)S(1)} collective-permute-done((bf16[128,2048]{1,0:T(8,128)(2,1)S(1)}, bf16[128,2048]{1,0:T(8,128)(2,1)S(1)}, u32[]{:S(2)}, u32[]{:S(2)}) %collective-permute-start) | collective-permute-done | bytes 524320 | tf_op jit(solution)/shard_map/ppermute | solution.py:1128
  23.4 0.8 copy-done.2
  24.3 67.7 %attention_forward.1 = (bf16[4,2048,1280]{2,1,0:T(8,128)(2,1)}, bf16[2048,256]{1,0:T(8,128)(2,1)}, bf16[2048,256]{1,0:T(8,128)(2,1)}, bf16[2048,256]{1,0:T(8,128...) custom-call(bf16[2048,256]{1,0:T(8,128)(2,1)} %x_late.1, ...), custom_call_target="tpu_custom_call" | custom-call | flops 16000000000 | bytes 41943040 | tf_op jit(solution)/shard_map/attention_forward/pallas_call | solution.py:372
  92.0 7.3 %all-gather.2.cloned.1.call-done.wu1.wd1 = bf16[1024,2048]{1,0:T(8,128)(2,1)} async-done(((bf16[128,2048]{1,0:T(8,128)(2,1)}), bf16[1024,2048]{1,0:T(8,128)(2,1)}) %all-gather.2.cloned.1.call-update) | async-done | bytes 4194320 | tf_op jit(solution)/shard_map/all_gather | solution.py:1199
  99.3 48.4 %feed_forward.1 = (bf16[1024,512]{1,0:T(8,128)(2,1)}, bf16[1024,512]{1,0:T(8,128)(2,1)}, bf16[1024,1024]{1,0:T(8,128)(2,1)}, f32[1024,1024]{1,0:T(8,128)}, bf16[...) custom-call(bf16[1024,512]{1,0:T(8,128)(2,1)} %get-tuple-element.68., ...), custom_call_target="tpu_custom_call" | custom-call | flops 25999998976 | bytes 41943040 | tf_op jit(solution)/shard_map/feed_forward/pallas_call | solution.py:512
  147.7 112.3 %backward.1 = (bf16[2048,256]{1,0:T(8,128)(2,1)}, bf16[1024,256]{1,0:T(8,128)(2,1)}, f32[2048,256]{1,0:T(8,128)}, f32[128,1024]{1,0:T(8,128)}, f32[128,1024]{1,0...) custom-call(bf16[2048,256]{1,0:T(8,128)(2,1)} %x_late.1, ...), custom_call_target="tpu_custom_call" | custom-call | flops 30000001024 | bytes 52428800 | tf_op jit(solution)/shard_map/backward/pallas_call | solution.py:1036
  260.0 1.2 divide_sqrt_fusion
  261.2 0.7 slice_bitcast_fusion.1
  261.9 1.4 fusion.9
  263.5 0.1 mul.46
  263.5 0.6 convert_multiply_fusion.2
  264.1 1.5 convert_multiply_fusion
  265.6 0.6 copy.45
  266.2 0.7 fusion.8
  266.9 0.7 slice_bitcast_fusion
  267.6 0.8 copy.43
  268.3 2.0 copy.44
  270.4 1.0 copy.49
  271.4 1.3 copy.50
  272.7 0.1 copy-done.3
  272.8 0.8 copy.51
  (53 shorter events, 0.4 us)
Async XLA Ops:
  7.2 4.3 %copy-start.12 = (bf16[256]{0:T(256)(128)(2,1)S(1)}, bf16[256]{0:T(256)(128)(2,1)}, u32[]{:S(2)}) copy-start(bf16[256]{0:T(256)(128)(2,1)} %param.29) | copy-start | bytes 1540
  7.2 4.3 %copy-start.11 = (bf16[256]{0:T(256)(128)(2,1)S(1)}, bf16[256]{0:T(256)(128)(2,1)}, u32[]{:S(2)}) copy-start(bf16[256]{0:T(256)(128)(2,1)} %param.26) | copy-start | bytes 1540
  7.2 4.4 %copy-start.8 = (s32[1,2048]{1,0:T(1,128)S(1)}, s32[1,2048]{1,0:T(1,128)}, u32[]{:S(2)}) copy-start(s32[1,2048]{1,0:T(1,128)} %param.21) | copy-start | bytes 24580
  7.2 5.0 %copy-start.9 = (s32[1,2048]{1,0:T(1,128)S(1)}, s32[1,2048]{1,0:T(1,128)}, u32[]{:S(2)}) copy-start(s32[1,2048]{1,0:T(1,128)} %param.22) | copy-start | bytes 24580
  7.2 7.7 %copy-start.13 = (bf16[256]{0:T(256)(128)(2,1)S(1)}, bf16[256]{0:T(256)(128)(2,1)}, u32[]{:S(2)}) copy-start(bf16[256]{0:T(256)(128)(2,1)} %param.23) | copy-start | bytes 1540
  7.2 7.7 %copy-start.14 = (bf16[256]{0:T(256)(128)(2,1)S(1)}, bf16[256]{0:T(256)(128)(2,1)}, u32[]{:S(2)}) copy-start(bf16[256]{0:T(256)(128)(2,1)} %param.24) | copy-start | bytes 1540
  7.3 7.7 %copy-start.15 = (bf16[256]{0:T(256)(128)(2,1)S(1)}, bf16[256]{0:T(256)(128)(2,1)}, u32[]{:S(2)}) copy-start(bf16[256]{0:T(256)(128)(2,1)} %param.31) | copy-start | bytes 1540
  7.3 7.7 %copy-start.16 = (bf16[256]{0:T(256)(128)(2,1)S(1)}, bf16[256]{0:T(256)(128)(2,1)}, u32[]{:S(2)}) copy-start(bf16[256]{0:T(256)(128)(2,1)} %param.32) | copy-start | bytes 1540
  7.3 7.7 %copy-start.17 = (bf16[256]{0:T(256)(128)(2,1)S(1)}, bf16[256]{0:T(256)(128)(2,1)}, u32[]{:S(2)}) copy-start(bf16[256]{0:T(256)(128)(2,1)} %param.33) | copy-start | bytes 1540
  7.3 7.7 %copy-start.18 = (bf16[256]{0:T(256)(128)(2,1)S(1)}, bf16[256]{0:T(256)(128)(2,1)}, u32[]{:S(2)}) copy-start(bf16[256]{0:T(256)(128)(2,1)} %param.37) | copy-start | bytes 1540
  7.3 7.7 %copy-start.10 = (bf16[1024]{0:T(1024)(128)(2,1)S(1)}, bf16[1024]{0:T(1024)(128)(2,1)}, u32[]{:S(2)}) copy-start(bf16[1024]{0:T(1024)(128)(2,1)} %param.35) | copy-start | bytes 6148
  7.3 92.0 %all-gather.2.cloned.1.call-start = ((), (), s32[]{:S(2)}) async-start(), calls=%async_computation | async-start | bytes 4718592 | tf_op jit(solution)/shard_map/all_gather | solution.py:1199
  8.5 15.0 %collective-permute-start = (bf16[128,2048]{1,0:T(8,128)(2,1)S(1)}, bf16[128,2048]{1,0:T(8,128)(2,1)S(1)}, u32[]{:S(2)}, u32[]{:S(2)}) collective-permute-start(bf16[128,2048]{1,0:T(8,128)(2,1)S(1)} %pad_maximum_fusion), channel_id=1, source_target_pairs={{0,2},{1,3},{2,0},{3,1},{4,6},{5,7},{6,4},{7,5},{8,10},{9,11},{10,... | collective-permute-start | bytes 1572872 | tf_op jit(solution)/shard_map/ppermute | solution.py:1128
  23.4 0.8 copy-start.2
  147.6 116.5 %copy-start.4 = (bf16[1024,256]{1,0:T(8,128)(2,1)S(1)}, bf16[1024,256]{1,0:T(8,128)(2,1)}, u32[]{:S(2)}) copy-start(bf16[1024,256]{1,0:T(8,128)(2,1)} %wq.3) | copy-start | bytes 1572868
  147.6 116.5 %copy-start.5 = (bf16[1024,256]{1,0:T(8,128)(2,1)S(1)}, bf16[1024,256]{1,0:T(8,128)(2,1)}, u32[]{:S(2)}) copy-start(bf16[1024,256]{1,0:T(8,128)(2,1)} %wk.3) | copy-start | bytes 1572868
  260.0 6.2 %copy-start.7 = (f32[128,512]{1,0:T(8,128)S(1)}, f32[128,512]{1,0:T(8,128)}, u32[]{:S(2)}) copy-start(f32[128,512]{1,0:T(8,128)} %get-tuple-element.95) | copy-start | bytes 786436
  260.0 6.9 %copy-start.6 = (f32[128,512]{1,0:T(8,128)S(1)}, f32[128,512]{1,0:T(8,128)}, u32[]{:S(2)}) copy-start(f32[128,512]{1,0:T(8,128)} %get-tuple-element.96) | copy-start | bytes 786436
  264.1 6.3 %copy-start.1 = (bf16[2048,256]{1,0:T(8,128)(2,1)S(1)}, bf16[2048,256]{1,0:T(8,128)(2,1)}, u32[]{:S(2)}) copy-start(bf16[2048,256]{1,0:T(8,128)(2,1)} %get-tuple-element.183) | copy-start | bytes 3145732
  266.9 4.4 %copy-start = (f32[2048,256]{1,0:T(8,128)S(1)}, f32[2048,256]{1,0:T(8,128)}, u32[]{:S(2)}) copy-start(f32[2048,256]{1,0:T(8,128)} %get-tuple-element.184) | copy-start | bytes 6291460
  271.4 1.4 copy-start.3
Sparse Core Ops, SparseCore 0:
  24.4 74.8 all-gather.1

commit v7 on v6

--- a/solution.py
+++ b/solution.py
@@ -595,7 +595,7 @@
     w_s, gh_s, gm_s, gt_s, qt_s, dl_s, ds_s, res_s, dkt_s, dvt_s, acc_s,
     o_s, gn_got, mr_got, gh_own, gh_y, gh_f,
     part_keep, part_send, part_got, sum_keep, sum_send, sum_got, ghx_s, st_keep, st_got, st_sum, st_all,
-    gk, ru_s, g1, y_send, y_got, cs_ref, bs_ref, n1_ref, v_keep, v_send, v_away, v_sum, v_got,
+    gk, ru_s, g1, y_send, y_got, y_keep, cs_ref, bs_ref, n1_ref, v_keep, v_send, v_away, v_sum, v_got,
     *rest, orders, chunk,
 ):
     levels = len(orders[0])
@@ -717,7 +717,10 @@
         for n, (own, other) in enumerate(PAIRS):
             cols, up = tile_of(own)
             if p == own:
-                (wu_ref if up else wdn_ref)[:, cols] = total
+                if up:
+                    wu_ref[:, cols] = total
+                else:
+                    y_keep[n - 2] = total
             if p == other:
                 y_send[n] = total.astype(BF)
                 send_last(n).start()
@@ -725,7 +728,10 @@
     def close(n):
         cols, up = tile_of(PAIRS[n][0])
         send_last(n).wait_recv()
-        (wu_ref if up else wdn_ref)[:, cols] += y_got[n].astype(F32)
+        if up:
+            wu_ref[:, cols] += y_got[n].astype(F32)
+        else:
+            wdn_ref[cols, :] = (y_keep[n - 2] + y_got[n].astype(F32)).T
 
     @pl.when(step == 0)
     def _():
@@ -1049,7 +1055,7 @@
         + [whole(D, SHARE)] * 3
         + [whole(SHARE, D)],
         out_specs=[anywhere, anywhere, final_late]
-        + [whole(chunk, UNITS)] * 2
+        + [whole(chunk, UNITS), whole(UNITS, chunk)]
         + [whole(chunk, TILE)] * 2
         + [whole(16, SHARE)],
         scratch_shapes=[
@@ -1086,6 +1092,7 @@
             vmem(6, D // 2, TILE),
             vmem(half, chunk, TILE),
             vmem(half, chunk, TILE),
+            vmem(2, chunk, TILE, dtype=F32),
             vmem(8, D, dtype=F32),
             vmem(8, SHARE, dtype=F32),
             vmem(8, SHARE, dtype=F32),
@@ -1110,7 +1117,7 @@
         + [dma(12)] * (2 * (levels - 1)),
         out_shape=[like((SEQ, SHARE), BF), like((OWN, SHARE), BF)]
         + [like((SEQ, SHARE), F32)]
-        + [like((chunk, UNITS), F32)] * 2
+        + [like((chunk, UNITS), F32), like((UNITS, chunk), F32)]
         + [like((chunk, TILE), F32)] * 2
         + [like((16, SHARE), F32)],
         compiler_params=remote_params(2),
@@ -1214,7 +1221,6 @@
         xs, h1, gn, mk, ms, dy, gu, gd, ru, su, sd, up_sums, hm, p, q, linv, ctx, k, v, vec,
         w_query, w_key, w_value, w_dense, (order_a, order_b), part,
     )
-    w_down_grad = w_down_grad.T
     head_max = sums[12, :LH]
     column_scale = jnp.repeat(jnp.sqrt(TAU / jnp.maximum(head_max, TAU)), HD)
     return (

time: 281 us -> 281 us (level)
  no operation moved by 1% of the time
where the time goes in v7:
time: 281 us; the launch traced here: 280 us
  Pallas kernels  228 us (81%)
  between operations  14.4 us (5%)
  local copies, waits for them, and re-layouts  12.6 us (4%)
  waiting for transfers between devices  12.3 us (4%)
  other arithmetic  9.52 us (3%)
  starting transfers between devices  3.07 us (1%)
    pallas_call x1, Pallas kernels, attention_backward(): pl.pallas_call(functools.partial(bwd_kernel, orders=orders, chunk=chunk),...  112 us
    pallas_call x1, Pallas kernels, attention_forward(): pl.pallas_call(fwd_kernel, grid=(NB + TAIL,), in_specs=[pl.BlockSpec(memo...  67.7 us
    pallas_call x1, Pallas kernels, feed_forward(): pl.pallas_call(functools.partial(mlp_kernel, bits=bits, chunk=chunk), gri...  48.4 us
    all_gather x1, waiting for transfers between devices, shards(): w_other = lax.all_gather(w_part, 'dp', axis=0, tiled=True)  7.3 us
    unnamed x45, local copies, waits for them, and re-layouts  6.84 us
  transfers between devices with their start and end apart: 2, of which 2 were waited for; matrix products, arithmetic and copies ran while one was open for 2% of the time, Pallas kernels for 24%

profile of v7, /device:TPU:0, one launch (start us, length us, event | category | flops | bytes accessed | tf_op | source)
XLA Modules:
  0.0 280.3 jit_solution(359799844618667839)
XLA Ops:
  7.4 1.1 constant_dynamic-slice_fusion
  8.5 3.0 %collective-permute-start = (bf16[128,2048]{1,0:T(8,128)(2,1)S(1)}, bf16[128,2048]{1,0:T(8,128)(2,1)S(1)}, u32[]{:S(2)}, u32[]{:S(2)}) collective-permute-start(bf16[128,2048]{1,0:T(8,128)(2,1)S(1)} %pad_maximum_fusion), channel_id=1, source_target_pairs={{0,2},{1,3},{2,0},{3,1},{4,6},{5,7},{6,4},{7,5},{8,10},{9,11},{10,... | collective-permute-start | bytes 1572872 | tf_op jit(solution)/shard_map/ppermute | solution.py:1135
  11.6 0.7 fusion.1
  12.3 0.1 broadcast_multiply_fusion
  12.4 2.0 fusion
  14.3 0.6 fusion.7.bqv
  15.1 0.6 convert_element_type.45.own_vec
  15.7 0.6 pad.18.alibi
  16.3 0.6 pad.17
  17.0 0.4 copy.41
  17.4 1.1 add_maximum_fusion.lo
  18.5 5.0 %collective-permute-done = bf16[128,2048]{1,0:T(8,128)(2,1)S(1)} collective-permute-done((bf16[128,2048]{1,0:T(8,128)(2,1)S(1)}, bf16[128,2048]{1,0:T(8,128)(2,1)S(1)}, u32[]{:S(2)}, u32[]{:S(2)}) %collective-permute-start) | collective-permute-done | bytes 524320 | tf_op jit(solution)/shard_map/ppermute | solution.py:1135
  23.4 0.8 copy-done.2
  24.3 67.7 %attention_forward.1 = (bf16[4,2048,1280]{2,1,0:T(8,128)(2,1)}, bf16[2048,256]{1,0:T(8,128)(2,1)}, bf16[2048,256]{1,0:T(8,128)(2,1)}, bf16[2048,256]{1,0:T(8,128...) custom-call(bf16[2048,256]{1,0:T(8,128)(2,1)} %x_late.1, ...), custom_call_target="tpu_custom_call" | custom-call | flops 16000000000 | bytes 41943040 | tf_op jit(solution)/shard_map/attention_forward/pallas_call | solution.py:372
  92.0 7.3 %all-gather.2.cloned.1.call-done.wu1.wd1 = bf16[1024,2048]{1,0:T(8,128)(2,1)} async-done(((bf16[128,2048]{1,0:T(8,128)(2,1)}), bf16[1024,2048]{1,0:T(8,128)(2,1)}) %all-gather.2.cloned.1.call-update) | async-done | bytes 4194320 | tf_op jit(solution)/shard_map/all_gather | solution.py:1206
  99.3 48.4 %feed_forward.1 = (bf16[1024,512]{1,0:T(8,128)(2,1)}, bf16[1024,512]{1,0:T(8,128)(2,1)}, bf16[1024,1024]{1,0:T(8,128)(2,1)}, f32[1024,1024]{1,0:T(8,128)}, bf16[...) custom-call(bf16[1024,512]{1,0:T(8,128)(2,1)} %get-tuple-element.68., ...), custom_call_target="tpu_custom_call" | custom-call | flops 25999998976 | bytes 41943040 | tf_op jit(solution)/shard_map/feed_forward/pallas_call | solution.py:512
  147.6 112.4 %backward.1 = (bf16[2048,256]{1,0:T(8,128)(2,1)}, bf16[1024,256]{1,0:T(8,128)(2,1)}, f32[2048,256]{1,0:T(8,128)}, f32[128,1024]{1,0:T(8,128)}, f32[1024,128]{1,0...) custom-call(bf16[2048,256]{1,0:T(8,128)(2,1)} %x_late.1, ...), custom_call_target="tpu_custom_call" | custom-call | flops 30000001024 | bytes 52428800 | tf_op jit(solution)/shard_map/backward/pallas_call | solution.py:1042
  260.1 1.2 divide_sqrt_fusion
  261.3 0.7 slice_bitcast_fusion.1
  262.0 1.4 fusion.9
  263.5 0.1 broadcast_in_dim.32
  263.5 0.1 mul.46
  263.6 0.6 convert_multiply_fusion.2
  264.2 2.6 convert_multiply_fusion
  266.8 0.6 copy.43
  267.4 0.7 fusion.8
  268.1 0.7 slice_bitcast_fusion
  268.8 0.8 copy.42
  269.6 1.0 copy.48
  270.5 1.3 copy.49
  271.9 0.8 copy.50
  272.7 0.8 copy.51
  (53 shorter events, 0.3 us)
Async XLA Ops:
  7.2 4.3 %copy-start.12 = (bf16[256]{0:T(256)(128)(2,1)S(1)}, bf16[256]{0:T(256)(128)(2,1)}, u32[]{:S(2)}) copy-start(bf16[256]{0:T(256)(128)(2,1)} %param.29) | copy-start | bytes 1540
  7.2 4.3 %copy-start.11 = (bf16[256]{0:T(256)(128)(2,1)S(1)}, bf16[256]{0:T(256)(128)(2,1)}, u32[]{:S(2)}) copy-start(bf16[256]{0:T(256)(128)(2,1)} %param.26) | copy-start | bytes 1540
  7.2 4.4 %copy-start.8 = (s32[1,2048]{1,0:T(1,128)S(1)}, s32[1,2048]{1,0:T(1,128)}, u32[]{:S(2)}) copy-start(s32[1,2048]{1,0:T(1,128)} %param.21) | copy-start | bytes 24580
  7.2 5.0 %copy-start.9 = (s32[1,2048]{1,0:T(1,128)S(1)}, s32[1,2048]{1,0:T(1,128)}, u32[]{:S(2)}) copy-start(s32[1,2048]{1,0:T(1,128)} %param.22) | copy-start | bytes 24580
  7.2 7.7 %copy-start.13 = (bf16[256]{0:T(256)(128)(2,1)S(1)}, bf16[256]{0:T(256)(128)(2,1)}, u32[]{:S(2)}) copy-start(bf16[256]{0:T(256)(128)(2,1)} %param.23) | copy-start | bytes 1540
  7.2 7.7 %copy-start.14 = (bf16[256]{0:T(256)(128)(2,1)S(1)}, bf16[256]{0:T(256)(128)(2,1)}, u32[]{:S(2)}) copy-start(bf16[256]{0:T(256)(128)(2,1)} %param.24) | copy-start | bytes 1540
  7.3 7.7 %copy-start.15 = (bf16[256]{0:T(256)(128)(2,1)S(1)}, bf16[256]{0:T(256)(128)(2,1)}, u32[]{:S(2)}) copy-start(bf16[256]{0:T(256)(128)(2,1)} %param.31) | copy-start | bytes 1540
  7.3 7.7 %copy-start.16 = (bf16[256]{0:T(256)(128)(2,1)S(1)}, bf16[256]{0:T(256)(128)(2,1)}, u32[]{:S(2)}) copy-start(bf16[256]{0:T(256)(128)(2,1)} %param.32) | copy-start | bytes 1540
  7.3 7.7 %copy-start.17 = (bf16[256]{0:T(256)(128)(2,1)S(1)}, bf16[256]{0:T(256)(128)(2,1)}, u32[]{:S(2)}) copy-start(bf16[256]{0:T(256)(128)(2,1)} %param.33) | copy-start | bytes 1540
  7.3 7.7 %copy-start.18 = (bf16[256]{0:T(256)(128)(2,1)S(1)}, bf16[256]{0:T(256)(128)(2,1)}, u32[]{:S(2)}) copy-start(bf16[256]{0:T(256)(128)(2,1)} %param.37) | copy-start | bytes 1540
  7.3 7.7 %copy-start.10 = (bf16[1024]{0:T(1024)(128)(2,1)S(1)}, bf16[1024]{0:T(1024)(128)(2,1)}, u32[]{:S(2)}) copy-start(bf16[1024]{0:T(1024)(128)(2,1)} %param.35) | copy-start | bytes 6148
  7.3 92.0 %all-gather.2.cloned.1.call-start = ((), (), s32[]{:S(2)}) async-start(), calls=%async_computation | async-start | bytes 4718592 | tf_op jit(solution)/shard_map/all_gather | solution.py:1206
  8.5 15.0 %collective-permute-start = (bf16[128,2048]{1,0:T(8,128)(2,1)S(1)}, bf16[128,2048]{1,0:T(8,128)(2,1)S(1)}, u32[]{:S(2)}, u32[]{:S(2)}) collective-permute-start(bf16[128,2048]{1,0:T(8,128)(2,1)S(1)} %pad_maximum_fusion), channel_id=1, source_target_pairs={{0,2},{1,3},{2,0},{3,1},{4,6},{5,7},{6,4},{7,5},{8,10},{9,11},{10,... | collective-permute-start | bytes 1572872 | tf_op jit(solution)/shard_map/ppermute | solution.py:1135
  23.4 0.8 copy-start.2
  147.6 116.6 %copy-start.5 = (bf16[1024,256]{1,0:T(8,128)(2,1)S(1)}, bf16[1024,256]{1,0:T(8,128)(2,1)}, u32[]{:S(2)}) copy-start(bf16[1024,256]{1,0:T(8,128)(2,1)} %wq.3) | copy-start | bytes 1572868
  260.1 8.1 %copy-start.6 = (f32[128,512]{1,0:T(8,128)S(1)}, f32[128,512]{1,0:T(8,128)}, u32[]{:S(2)}) copy-start(f32[128,512]{1,0:T(8,128)} %get-tuple-element.96) | copy-start | bytes 786436
  263.6 3.8 %copy-start.7 = (f32[128,512]{1,0:T(8,128)S(1)}, f32[128,512]{1,0:T(8,128)}, u32[]{:S(2)}) copy-start(f32[128,512]{1,0:T(8,128)} %get-tuple-element.95) | copy-start | bytes 786436
  264.2 5.4 %copy-start.1 = (bf16[2048,256]{1,0:T(8,128)(2,1)S(1)}, bf16[2048,256]{1,0:T(8,128)(2,1)}, u32[]{:S(2)}) copy-start(bf16[2048,256]{1,0:T(8,128)(2,1)} %get-tuple-element.183) | copy-start | bytes 3145732
  266.8 3.7 %copy-start = (f32[2048,256]{1,0:T(8,128)S(1)}, f32[2048,256]{1,0:T(8,128)}, u32[]{:S(2)}) copy-start(f32[2048,256]{1,0:T(8,128)} %get-tuple-element.184) | copy-start | bytes 6291460
  270.5 1.4 copy-start.4
  270.5 2.2 copy-start.3
Sparse Core Ops, SparseCore 0:
  24.4 74.8 all-gather.1
